TPU v7x, 128 devices: a whole 4x4x4 slice. The times are simulated.
128 devices in a mesh: row: 8 (over x_lo, z), col: 16 (over x_hi, y, core).
Axes of the slice: x: 4 (x_hi: 2, x_lo: 2; x = x_hi * 2 + x_lo), y: 4, z: 4, core: 2. Of those that a mesh axis runs over, the one named last changes fastest.
Arguments:
- coarse_in: bfloat16 [256, 128, 512], P(('row', 'col')), may hold values from -6 to 6
- fine_in: bfloat16 [1024, 512, 256], P('row', 'col'), may hold values from -6 to 6
- band_weight: bfloat16 [4, 512, 512], replicated, may hold values from -0.25 to 0.25
- point_weight: bfloat16 [512, 512], replicated, may hold values from -0.25 to 0.25
- proj_weight: bfloat16 [512, 256], replicated, may hold values from -0.25 to 0.25
- conv_weight: bfloat16 [9, 256, 256], replicated, may hold values from -0.125 to 0.125
- out_cot: bfloat16 [1024, 512, 256], P('row', 'col'), may hold values from -6 to 6
Outputs:
- fine_out: bfloat16 [1024, 512, 256], P('row', 'col')
- grad_conv: float32 [9, 256, 256], replicated
- grad_band: float32 [4, 512, 512], replicated
- grad_point: float32 [512, 512], replicated
- grad_proj: float32 [512, 256], replicated
All inputs are finite; a program needn't handle non-finite values.
Results may differ from a plain program's by a relative error of at most 0.017.
Values may be sent and summed in bfloat16 or wider, within the bound.
No kernel may reach another device: no remote copies, remote signals or barrier semaphores. Data moves between devices by JAX's collectives and lax.ppermute only.
A program may use at most 128 MiB of HBM per device.

v0:
```python
import jax
import jax.numpy as jnp
from jax import lax
from jax.sharding import PartitionSpec as P


def extended(block, sides, width):
    for axis, dim in sides:
        count = lax.axis_size(axis)
        forward = [(i, i + 1) for i in range(count - 1)]
        backward = [(target, source) for source, target in forward]
        low = lax.ppermute(
            lax.slice_in_dim(block, block.shape[dim] - width, None, axis=dim), axis, forward
        )
        high = lax.ppermute(lax.slice_in_dim(block, 0, width, axis=dim), axis, backward)
        block = jnp.concatenate([low, block, high], axis=dim)
    return block


def project_rows(field, weight):
    flat = field.reshape(-1, field.shape[-1])
    result = jnp.dot(flat, weight, preferred_element_type=jnp.float32)
    return result.reshape(field.shape[:-1] + (weight.shape[-1],))


def contract_rows(left, right):
    left_flat = left.reshape(-1, left.shape[-1])
    right_flat = right.reshape(-1, right.shape[-1])
    return lax.dot_general(
        left_flat, right_flat, (((0,), (0,)), ((), ())), preferred_element_type=jnp.float32
    )


def haar_split(field):
    even_even = field[0::2, 0::2]
    even_odd = field[0::2, 1::2]
    odd_even = field[1::2, 0::2]
    odd_odd = field[1::2, 1::2]
    return (
        jnp.stack(
            [
                even_even + even_odd + odd_even + odd_odd,
                even_even - even_odd + odd_even - odd_odd,
                even_even + even_odd - odd_even - odd_odd,
                even_even - even_odd - odd_even + odd_odd,
            ]
        )
        * 0.5
    )


def haar_merge(bands):
    first, second, third, fourth = (bands[0], bands[1], bands[2], bands[3])
    even_even = (first + second + third + fourth) * 0.5
    even_odd = (first - second + third - fourth) * 0.5
    odd_even = (first + second - third - fourth) * 0.5
    odd_odd = (first - second - third + fourth) * 0.5
    height, width, depth = first.shape
    top_row = jnp.stack([even_even, even_odd], axis=2).reshape(height, 2 * width, depth)
    low_row = jnp.stack([odd_even, odd_odd], axis=2).reshape(height, 2 * width, depth)
    return jnp.stack([top_row, low_row], axis=1).reshape(2 * height, 2 * width, depth)


def upsample(field):
    height, width, depth = field.shape
    grown = jnp.broadcast_to(field[:, None, :, None, :], (height, 4, width, 4, depth))
    return grown.reshape(4 * height, 4 * width, depth)


def pad_tile(field):
    with_rows = extended(field, (("row", 0),), 1)
    return extended(with_rows, (("col", 1),), 1)


def local(coarse_in, fine_in, band_weight, point_weight, proj_weight, conv_weight, out_cot):
    coarse = coarse_in.astype(jnp.float32)
    subbands = haar_split(coarse).astype(jnp.bfloat16)
    band_mixed = jnp.einsum(
        "shwc,scd->shwd", subbands, band_weight, preferred_element_type=jnp.float32
    )
    pre_act = haar_merge(band_mixed) + project_rows(coarse_in, point_weight)
    coarse_hidden = jax.nn.gelu(pre_act).astype(jnp.bfloat16)
    hidden_tiles = lax.all_to_all(coarse_hidden, "col", split_axis=1, concat_axis=0, tiled=True)
    coarse_out = project_rows(hidden_tiles, proj_weight).astype(jnp.bfloat16)
    conv_in = (fine_in.astype(jnp.float32) + upsample(coarse_out).astype(jnp.float32)).astype(
        jnp.bfloat16
    )
    tile_rows, tile_cols, depth = conv_in.shape
    padded = pad_tile(conv_in)
    total = jnp.zeros((tile_rows, tile_cols, depth), jnp.float32)
    for lat_off in range(3):
        for lon_off in range(3):
            window = padded[lat_off : lat_off + tile_rows, lon_off : lon_off + tile_cols]
            total = total + project_rows(window, conv_weight[3 * lat_off + lon_off])
    fine_out = total.astype(jnp.bfloat16)
    grad_pad = pad_tile(out_cot)
    grad_in = jnp.zeros((tile_rows, tile_cols, depth), jnp.float32)
    kernel_parts = []
    for lat_off in range(3):
        for lon_off in range(3):
            weight = conv_weight[3 * lat_off + lon_off]
            window = padded[lat_off : lat_off + tile_rows, lon_off : lon_off + tile_cols]
            kernel_parts.append(contract_rows(window, out_cot))
            back_window = grad_pad[
                2 - lat_off : 2 - lat_off + tile_rows, 2 - lon_off : 2 - lon_off + tile_cols
            ]
            grad_in = grad_in + project_rows(back_window, weight.T)
    kernel_local = jnp.stack(kernel_parts)
    cells_all = tile_rows * lax.axis_size("row") * tile_cols * lax.axis_size("col")
    loss_scale = float(cells_all) ** (-0.5)
    d_tiles = (
        grad_in.reshape(tile_rows // 4, 4, tile_cols // 4, 4, depth)
        .sum(axis=(1, 3))
        .astype(jnp.bfloat16)
    )
    proj_local = contract_rows(hidden_tiles, d_tiles)
    d_hidden_tiles = project_rows(d_tiles, proj_weight.T)
    d_hidden = lax.all_to_all(
        d_hidden_tiles.astype(jnp.bfloat16), "col", split_axis=0, concat_axis=1, tiled=True
    ).astype(d_hidden_tiles.dtype)
    unused, gelu_pull = jax.vjp(jax.nn.gelu, pre_act)
    d_pre = gelu_pull(d_hidden)[0].astype(jnp.bfloat16)
    point_local = contract_rows(coarse_in, d_pre)
    d_mixed = haar_split(d_pre.astype(jnp.float32)).astype(jnp.bfloat16)
    band_local = jnp.einsum("shwc,shwd->scd", subbands, d_mixed, preferred_element_type=jnp.float32)
    kernel_sum, band_sum, point_sum, proj_sum = lax.psum(
        (kernel_local, band_local, point_local, proj_local), ("row", "col")
    )
    return (
        fine_out,
        kernel_sum * loss_scale,
        band_sum * loss_scale,
        point_sum * loss_scale,
        proj_sum * loss_scale,
    )


def solution(mesh):
    in_specs = (
        P(("row", "col"), None, None),
        P("row", "col", None),
        P(),
        P(),
        P(),
        P(),
        P("row", "col", None),
    )
    out_specs = (P("row", "col", None), P(), P(), P(), P())
    return jax.shard_map(local, mesh=mesh, in_specs=in_specs, out_specs=out_specs, check_vma=False)
```

profile of v0, /device:TPU:1, one launch (start us, length us, event | category | flops | bytes accessed | tf_op | source)
XLA Modules:
  0.0 358.9 jit_solution(813588103560851152)
XLA Ops:
  7.2 2.9 copy.120
  12.1 5.0 %collective-permute-start.4 = (bf16[1,32,256]{2,0,1:T(2,128)(2,1)}, bf16[1,32,256]{2,0,1:T(2,128)(2,1)}, u32[]{:S(2)}, u32[]{:S(2)}) collective-permute-start(bf16[1,32,256]{2,0,1:T(2,128)(2,1)} %get-tuple-element.38), channel_id=1, source_target_pairs={{0,16},{16,32},{32,48},{48,64},{64,80},{80,96},{96,112},{1,17},{17... | collective-permute-start | bytes 49160 | tf_op jit(solution)/shard_map/ppermute | solution.py:12
  21.2 4.1 %fusion.118 = f32[128,32,256]{2,0,1:T(8,128)S(1)} fusion(bf16[9,256,256]{2,1,0:T(8,128)(2,1)S(1)} %copy-done.10, bf16[128,32,256]{2,1,0:T(8,128)(2,1)} %param.13), kind=kOutput, calls=%fused_computation.120 | convolution fusion | flops 536870912 | bytes 6422528 | tf_op jit(solution)/shard_map/dot_general | solution.py:22
  28.1 4.0 %collective-permute-start.7 = (bf16[130,1,256]{2,0,1:T(8,128)(2,1)S(1)}, bf16[130,1,256]{2,0,1:T(8,128)(2,1)S(1)}, u32[]{:S(2)}, u32[]{:S(2)}) collective-permute-start(bf16[130,1,256]{2,0,1:T(8,128)(2,1)S(1)} %get-tuple-element.31), channel_id=1, source_target_pairs={{0,1},{1,2},{2,3},{3,4},{4,5},{5,6},{6,7},{7,8},{8,9},{9,10},{10,1... | collective-permute-start | bytes 199688 | tf_op jit(solution)/shard_map/ppermute | solution.py:12
  32.1 2.1 collective-permute-start.6
  35.8 3.5 fusion.14
  39.3 3.0 maximum_maximum_fusion.1
  42.3 2.7 fusion.6
  45.0 2.8 fusion.10
  47.9 2.8 fusion.8
  50.6 2.7 fusion.12
  53.3 2.7 fusion.16
  56.1 11.3 %add_add_fusion = f32[128,32,256]{2,0,1:T(8,128)} fusion(f32[128,32,256]{2,0,1:T(8,128)S(1)} %fusion.4, f32[128,32,256]{2,0,1:T(8,128)} %fusion.6, f32[128,32,256]{2,0,1:T(8,128)} %fusion.8, f32[128,32,256]{2,0,1:T(8,128)S(1)} %fusion.118, f32[128,32,256]{2,0,1:T(8,128)} %fusion.10, f32[128,32,256]{2,0,1:T(8,128)} %fusion.12, f32[128,32,256]{2,0,1:T(8,128)} %fusion.16, ...), kind=kOutput, calls=%fused_computation | convolution fusion | flops 545259520 | bytes 39976960 | tf_op jit(solution)/shard_map/dot_general | solution.py:22
  67.4 5.2 %reshape.212 = f32[32,4,8,4,256]{4,1,0,3,2:T(4,128)} reshape(f32[128,32,256]{2,0,1:T(8,128)} %add_add_fusion) | data formatting | bytes 8388608 | tf_op jit(solution)/shard_map/reshape | solution.py:112
  72.5 3.5 reduce_sum.9
  77.1 8.5 %all-to-all-start.1 = ((bf16[32,8,512]{2,1,0:T(8,128)(2,1)}), bf16[32,8,512]{2,1,0:T(8,128)(2,1)S(1)}, u32[]{:S(2)}, u32[]{:S(2)}) async-start(bf16[32,8,512]{2,1,0:T(8,128)(2,1)} %convolution_convert_fusion), calls=%async_computation.1 | async-start | bytes 524288 | tf_op jit(solution)/shard_map/all_to_all | solution.py:118
  86.5 7.7 %all-to-all-done.1 = bf16[32,8,512]{2,1,0:T(8,128)(2,1)S(1)} async-done(((bf16[32,8,512]{2,1,0:T(8,128)(2,1)}), bf16[32,8,512]{2,1,0:T(8,128)(2,1)S(1)}, u32[]{:S(2)}, u32[]{:S(2)}) %all-to-all-start.1) | async-done | bytes 262176 | tf_op jit(solution)/shard_map/all_to_all | solution.py:118
  98.7 4.3 %all-to-all-start = ((bf16[2,128,512]{2,0,1:T(2,128)(2,1)}), bf16[2,128,512]{2,0,1:T(2,128)(2,1)S(1)}, u32[]{:S(2)}, u32[]{:S(2)}) async-start(bf16[2,128,512]{2,0,1:T(2,128)(2,1)} %copy.115), calls=%async_computation | async-start | bytes 524288 | tf_op jit(solution)/shard_map/all_to_all | solution.py:83
  105.8 2.7 fusion.103
  108.5 3.2 all-to-all-done
  112.1 3.0 broadcast_in_dim.2
  115.1 5.4 %convert_element_type.79 = f32[128,32,256]{2,0,1:T(8,128)} reshape(f32[32,4,8,4,256]{4,1,0,3,2:T(4,128)} %broadcast_in_dim.2) | data formatting | bytes 8388608 | tf_op jit(solution)/shard_map/convert_element_type | solution.py:85
  120.4 4.2 %add_convert_fusion.1 = bf16[128,32,256]{2,0,1:T(8,128)(2,1)S(1)} fusion(f32[128,32,256]{2,0,1:T(8,128)} %convert_element_type.79, bf16[128,32,256]{2,1,0:T(8,128)(2,1)} %param.8), kind=kLoop, calls=%fused_computation.2 | loop fusion | flops 3145728 | bytes 8388608 | tf_op jit(solution)/shard_map/convert_element_type | solution.py:85
  126.0 4.9 %collective-permute-start = (bf16[1,32,256]{2,0,1:T(2,128)(2,1)S(1)}, bf16[1,32,256]{2,0,1:T(2,128)(2,1)S(1)}, u32[]{:S(2)}, u32[]{:S(2)}) collective-permute-start(bf16[1,32,256]{2,0,1:T(2,128)(2,1)S(1)} %get-tuple-element.39), channel_id=1, source_target_pairs={{0,16},{16,32},{32,48},{48,64},{64,80},{80,96},{96,112},{1,17},{17... | collective-permute-start | bytes 49160 | tf_op jit(solution)/shard_map/ppermute | solution.py:12
  130.9 2.8 fusion.120
  133.8 3.3 collective-permute-start.3
  137.1 2.4 collective-permute-start.2
  140.8 2.2 pad_maximum_fusion
  143.1 3.3 fusion.55
  146.4 3.4 fusion.51
  149.8 3.3 fusion.61
  153.1 3.4 fusion.67
  156.6 3.4 fusion.88
  160.0 3.5 fusion.73
  163.5 3.4 fusion.79
  166.9 3.4 fusion.49
  170.3 3.5 fusion.85
  175.5 2.7 fusion.44
  178.2 2.7 fusion.26
  180.9 2.7 fusion.30
  183.6 2.7 fusion.34
  186.3 2.8 fusion.38
  189.1 3.7 %fusion.42 = f32[128,32,256]{2,0,1:T(8,128)} fusion(bf16[130,33,256]{2,0,1:T(8,128)(2,1)S(1)} %copy-done.7, bf16[9,256,256]{2,1,0:T(8,128)(2,1)} %param.12), kind=kOutput, calls=%fused_computation.50 | convolution fusion | flops 536870912 | bytes 6422528 | tf_op jit(solution)/shard_map/dot_general | solution.py:22
  192.9 10.1 %add_convert_fusion = bf16[128,32,256]{2,0,1:T(8,128)(2,1)S(1)} fusion(f32[128,32,256]{2,0,1:T(8,128)S(1)} %fusion.46, f32[128,32,256]{2,0,1:T(8,128)} %fusion.26, f32[128,32,256]{2,0,1:T(8,128)} %fusion.30, f32[128,32,256]{2,0,1:T(8,128)S(1)} %copy-done.8, f32[128,32,256]{2,0,1:T(8,128)} %fusion.34, f32[128,32,256]{2,0,1:T(8,128)} %fusion.38, ...), kind=kOutput, calls=%fused_computation.1 | convolution fusion | flops 546308096 | bytes 37879808 | tf_op jit(solution)/shard_map/dot_general | solution.py:22
  203.0 2.5 copy.148
  205.5 136.8 %all-reduce.3.cloned.1.call-done = (f32[9,256,256]{2,1,0:T(8,128)}, f32[4,512,512]{2,1,0:T(8,128)}, f32[512,512]{0,1:T(8,128)}, f32[512,256]{1,0:T(8,128)}) async-done(((f32[9,256,256]{2,1,0:T(8,128)}, f32[4,512,512]{2,1,0:T(8,128)}, f32[512,512]{0,1:T(8,128)}, f32[512,256]{1,0:T(8,128)}), (f32[9,256,256]{2,1,0:T(8,128)}, f32[4,512,512]{2,1,0:T(8,128)}, f32[512,512]{0,1:T(8,128)}, ...) | async-done | bytes 8126480 | tf_op jit(solution)/shard_map/psum | solution.py:126
  342.3 3.4 broadcast_multiply_fusion.1
  345.8 2.8 broadcast_multiply_fusion
  (115 shorter events, 27.4 us)
Async XLA Ops:
  7.2 18.3 %copy-start = (bf16[4,512,512]{2,1,0:T(8,128)(2,1)S(1)}, bf16[4,512,512]{2,1,0:T(8,128)(2,1)}, u32[]{:S(2)}) copy-start(bf16[4,512,512]{2,1,0:T(8,128)(2,1)} %param.9) | copy-start | bytes 6291460
  7.2 11.2 %copy-start.12 = (bf16[2,128,512]{2,1,0:T(8,128)(2,1)S(1)}, bf16[2,128,512]{2,1,0:T(8,128)(2,1)}, u32[]{:S(2)}) copy-start(bf16[2,128,512]{2,1,0:T(8,128)(2,1)} %param.7) | copy-start | bytes 786436
  7.2 14.0 %copy-start.10 = (bf16[9,256,256]{2,1,0:T(8,128)(2,1)S(1)}, bf16[9,256,256]{2,1,0:T(8,128)(2,1)}, u32[]{:S(2)}) copy-start(bf16[9,256,256]{2,1,0:T(8,128)(2,1)} %param.12) | copy-start | bytes 3538948
  10.1 1.3 copy-start.2
  12.1 14.7 %collective-permute-start.4 = (bf16[1,32,256]{2,0,1:T(2,128)(2,1)}, bf16[1,32,256]{2,0,1:T(2,128)(2,1)}, u32[]{:S(2)}, u32[]{:S(2)}) collective-permute-start(bf16[1,32,256]{2,0,1:T(2,128)(2,1)} %get-tuple-element.38), channel_id=1, source_target_pairs={{0,16},{16,32},{32,48},{48,64},{64,80},{80,96},{96,112},{1,17},{17... | collective-permute-start | bytes 49160 | tf_op jit(solution)/shard_map/ppermute | solution.py:12
  17.1 9.7 %collective-permute-start.5 = (bf16[1,32,256]{2,0,1:T(2,128)(2,1)}, bf16[1,32,256]{2,0,1:T(2,128)(2,1)}, u32[]{:S(2)}, u32[]{:S(2)}) collective-permute-start(bf16[1,32,256]{2,0,1:T(2,128)(2,1)} %get-tuple-element.37), channel_id=1, source_target_pairs={{16,0},{32,16},{48,32},{64,48},{80,64},{96,80},{112,96},{17,1},{33... | collective-permute-start | bytes 49160 | tf_op jit(solution)/shard_map/ppermute | solution.py:15
  21.2 4.1 %copy-start.26 = (f32[1,64,512]{2,1,0:T(8,128)S(1)}, f32[1,64,512]{2,1,0:T(8,128)}, u32[]{:S(2)}) copy-start(f32[1,64,512]{2,1,0:T(8,128)} %slice.183) | copy-start | bytes 393220
  21.2 4.1 %copy-start.27 = (f32[1,64,512]{2,1,0:T(8,128)S(1)}, f32[1,64,512]{2,1,0:T(8,128)}, u32[]{:S(2)}) copy-start(f32[1,64,512]{2,1,0:T(8,128)} %slice.182) | copy-start | bytes 393220
  21.2 4.1 %copy-start.28 = (f32[1,64,512]{2,1,0:T(8,128)S(1)}, f32[1,64,512]{2,1,0:T(8,128)}, u32[]{:S(2)}) copy-start(f32[1,64,512]{2,1,0:T(8,128)} %slice.180) | copy-start | bytes 393220
  21.2 4.1 %copy-start.29 = (f32[1,64,512]{2,1,0:T(8,128)S(1)}, f32[1,64,512]{2,1,0:T(8,128)}, u32[]{:S(2)}) copy-start(f32[1,64,512]{2,1,0:T(8,128)} %slice.181) | copy-start | bytes 393220
  25.4 2.0 copy-start.3
  25.5 2.6 copy-start.16
  25.5 2.6 copy-start.18
  25.5 2.6 copy-start.20
  25.5 2.6 copy-start.22
  28.1 11.2 %collective-permute-start.7 = (bf16[130,1,256]{2,0,1:T(8,128)(2,1)S(1)}, bf16[130,1,256]{2,0,1:T(8,128)(2,1)S(1)}, u32[]{:S(2)}, u32[]{:S(2)}) collective-permute-start(bf16[130,1,256]{2,0,1:T(8,128)(2,1)S(1)} %get-tuple-element.31), channel_id=1, source_target_pairs={{0,1},{1,2},{2,3},{3,4},{4,5},{5,6},{6,7},{7,8},{8,9},{9,10},{10,1... | collective-permute-start | bytes 199688 | tf_op jit(solution)/shard_map/ppermute | solution.py:12
  32.1 7.1 %collective-permute-start.6 = (bf16[130,1,256]{2,0,1:T(8,128)(2,1)S(1)}, bf16[130,1,256]{2,0,1:T(8,128)(2,1)S(1)}, u32[]{:S(2)}, u32[]{:S(2)}) collective-permute-start(bf16[130,1,256]{2,0,1:T(8,128)(2,1)S(1)} %get-tuple-element.32), channel_id=1, source_target_pairs={{1,0},{2,1},{3,2},{4,3},{5,4},{6,5},{7,6},{8,7},{9,8},{10,9},{11,1... | collective-permute-start | bytes 199688 | tf_op jit(solution)/shard_map/ppermute | solution.py:15
  72.5 3.6 copy-start.24
  72.5 13.0 %copy-start.13 = (f32[4,64,512]{2,1,0:T(8,128)S(1)}, f32[4,64,512]{2,1,0:T(8,128)}, u32[]{:S(2)}) copy-start(f32[4,64,512]{2,1,0:T(8,128)} %fusion.159) | copy-start | bytes 1572868
  76.1 10.2 %copy-start.14 = (bf16[32,8,256]{2,0,1:T(8,128)(2,1)}, bf16[32,8,256]{2,0,1:T(8,128)(2,1)S(1)}, u32[]{:S(2)}) copy-start(bf16[32,8,256]{2,0,1:T(8,128)(2,1)S(1)} %reduce_sum.9) | copy-start | bytes 393220
  77.1 17.2 %all-to-all-start.1 = ((bf16[32,8,512]{2,1,0:T(8,128)(2,1)}), bf16[32,8,512]{2,1,0:T(8,128)(2,1)S(1)}, u32[]{:S(2)}, u32[]{:S(2)}) async-start(bf16[32,8,512]{2,1,0:T(8,128)(2,1)} %convolution_convert_fusion), calls=%async_computation.1 | async-start | bytes 524288 | tf_op jit(solution)/shard_map/all_to_all | solution.py:118
  96.1 9.7 %copy-start.17 = (f32[1,64,512]{2,1,0:T(8,128)S(1)}, f32[1,64,512]{2,1,0:T(8,128)}, u32[]{:S(2)}) copy-start(f32[1,64,512]{2,1,0:T(8,128)} %copy-done.16) | copy-start | bytes 393220
  96.1 9.6 %copy-start.19 = (f32[1,64,512]{2,1,0:T(8,128)S(1)}, f32[1,64,512]{2,1,0:T(8,128)}, u32[]{:S(2)}) copy-start(f32[1,64,512]{2,1,0:T(8,128)} %copy-done.18) | copy-start | bytes 393220
  96.1 9.6 %copy-start.21 = (f32[1,64,512]{2,1,0:T(8,128)S(1)}, f32[1,64,512]{2,1,0:T(8,128)}, u32[]{:S(2)}) copy-start(f32[1,64,512]{2,1,0:T(8,128)} %copy-done.20) | copy-start | bytes 393220
  96.1 9.6 %copy-start.23 = (f32[1,64,512]{2,1,0:T(8,128)S(1)}, f32[1,64,512]{2,1,0:T(8,128)}, u32[]{:S(2)}) copy-start(f32[1,64,512]{2,1,0:T(8,128)} %copy-done.22) | copy-start | bytes 393220
  98.7 13.0 %all-to-all-start = ((bf16[2,128,512]{2,0,1:T(2,128)(2,1)}), bf16[2,128,512]{2,0,1:T(2,128)(2,1)S(1)}, u32[]{:S(2)}, u32[]{:S(2)}) async-start(bf16[2,128,512]{2,0,1:T(2,128)(2,1)} %copy.115), calls=%async_computation | async-start | bytes 524288 | tf_op jit(solution)/shard_map/all_to_all | solution.py:83
  103.0 239.4 %all-reduce.3.cloned.1.call-start = ((), (), s32[]{:S(2)}) async-start(), calls=%async_computation.2 | async-start | bytes 16252928 | tf_op jit(solution)/shard_map/psum | solution.py:126
  124.7 9.0 %collective-permute-start.1 = (bf16[1,32,256]{2,0,1:T(2,128)(2,1)S(1)}, bf16[1,32,256]{2,0,1:T(2,128)(2,1)S(1)}, u32[]{:S(2)}, u32[]{:S(2)}) collective-permute-start(bf16[1,32,256]{2,0,1:T(2,128)(2,1)S(1)} %get-tuple-element.40), channel_id=1, source_target_pairs={{16,0},{32,16},{48,32},{64,48},{80,64},{96,80},{112,96},{17,1},{33... | collective-permute-start | bytes 49160 | tf_op jit(solution)/shard_map/ppermute | solution.py:15
  126.0 7.7 %collective-permute-start = (bf16[1,32,256]{2,0,1:T(2,128)(2,1)S(1)}, bf16[1,32,256]{2,0,1:T(2,128)(2,1)S(1)}, u32[]{:S(2)}, u32[]{:S(2)}) collective-permute-start(bf16[1,32,256]{2,0,1:T(2,128)(2,1)S(1)} %get-tuple-element.39), channel_id=1, source_target_pairs={{0,16},{16,32},{32,48},{48,64},{64,80},{80,96},{96,112},{1,17},{17... | collective-permute-start | bytes 49160 | tf_op jit(solution)/shard_map/ppermute | solution.py:12
  133.7 5.8 %copy-start.15 = (bf16[32,8,256]{2,0,1:T(8,128)(2,1)S(1)}, bf16[32,8,256]{2,0,1:T(8,128)(2,1)}, u32[]{:S(2)}) copy-start(bf16[32,8,256]{2,0,1:T(8,128)(2,1)} %copy-done.14) | copy-start | bytes 393220
  133.7 33.2 %copy-start.30 = (bf16[1,32,256]{2,0,1:T(2,128)(2,1)}, bf16[1,32,256]{2,0,1:T(2,128)(2,1)S(1)}, u32[]{:S(2)}) copy-start(bf16[1,32,256]{2,0,1:T(2,128)(2,1)S(1)} %collective-permute-done.1) | copy-start | bytes 49156
  133.7 12.7 %copy-start.32 = (bf16[1,32,256]{2,0,1:T(2,128)(2,1)}, bf16[1,32,256]{2,0,1:T(2,128)(2,1)S(1)}, u32[]{:S(2)}) copy-start(bf16[1,32,256]{2,0,1:T(2,128)(2,1)S(1)} %collective-permute-done) | copy-start | bytes 49156
  133.8 6.8 %collective-permute-start.3 = (bf16[130,1,256]{2,0,1:T(8,128)(2,1)S(1)}, bf16[130,1,256]{2,0,1:T(8,128)(2,1)S(1)}, u32[]{:S(2)}, u32[]{:S(2)}) collective-permute-start(bf16[130,1,256]{2,0,1:T(8,128)(2,1)S(1)} %get-tuple-element.35), channel_id=1, source_target_pairs={{1,0},{2,1},{3,2},{4,3},{5,4},{6,5},{7,6},{8,7},{9,8},{10,9},{11,1... | collective-permute-start | bytes 199688 | tf_op jit(solution)/shard_map/ppermute | solution.py:15
  137.1 3.7 %collective-permute-start.2 = (bf16[130,1,256]{2,0,1:T(8,128)(2,1)S(1)}, bf16[130,1,256]{2,0,1:T(8,128)(2,1)S(1)}, u32[]{:S(2)}, u32[]{:S(2)}) collective-permute-start(bf16[130,1,256]{2,0,1:T(8,128)(2,1)S(1)} %get-tuple-element.36), channel_id=1, source_target_pairs={{0,1},{1,2},{2,3},{3,4},{4,5},{5,6},{6,7},{7,8},{8,9},{9,10},{10,1... | collective-permute-start | bytes 199688 | tf_op jit(solution)/shard_map/ppermute | solution.py:12
  140.6 2.5 copy-start.9
  143.1 20.4 %copy-start.6 = (bf16[130,33,256]{2,0,1:T(8,128)(2,1)}, bf16[130,33,256]{2,0,1:T(8,128)(2,1)S(1)}, u32[]{:S(2)}) copy-start(bf16[130,33,256]{2,0,1:T(8,128)(2,1)S(1)} %get-tuple-element.34) | copy-start | bytes 6589444
  143.1 27.2 %copy-start.4 = (bf16[130,33,256]{2,0,1:T(8,128)(2,1)}, bf16[130,33,256]{2,0,1:T(8,128)(2,1)S(1)}, u32[]{:S(2)}) copy-start(bf16[130,33,256]{2,0,1:T(8,128)(2,1)S(1)} %get-tuple-element.33) | copy-start | bytes 6589444
  173.7 0.8 copy-start.31
  174.5 1.0 copy-start.33
  175.5 2.7 copy-start.7
  178.2 2.7 copy-start.5
  189.1 3.7 %copy-start.8 = (f32[128,32,256]{2,0,1:T(8,128)S(1)}, f32[128,32,256]{2,0,1:T(8,128)}, u32[]{:S(2)}) copy-start(f32[128,32,256]{2,0,1:T(8,128)} %fusion.120) | copy-start | bytes 12582916
  342.3 3.4 copy-start.11
  345.8 2.8 copy-start.25
  348.5 3.3 copy-start.1
Sparse Core Ops, SparseCore 0:
  173.9 168.4 all-reduce.2
where the time goes:
time: 364 us; the launch traced here: 359 us
  waiting for transfers between devices  148 us (41%)
  matrix products  105 us (29%)
  starting transfers between devices  37.5 us (10%)
  local copies, waits for them, and re-layouts  30 us (8%)
  other arithmetic  23.2 us (6%)
  between operations  14.8 us (4%)
    psum x1, waiting for transfers between devices, local(): lax.psum((kernel_local, band_local, point_local, proj_local), ('row', 'co...  137 us
    dot_general x21, matrix products, project_rows(): result = jnp.dot(flat, weight, preferred_element_type=jnp.float32)  68.3 us
    dot_general x11, matrix products, contract_rows(): lax.dot_general(left_flat, right_flat, (((0,), (0,)), ((), ())), preferre...  33 us
    ppermute x4, starting transfers between devices, extended(): lax.ppermute(lax.slice_in_dim(block, block.shape[dim] - width, None, axis...  16.3 us
    unnamed x71, local copies, waits for them, and re-layouts  9.45 us
    all_to_all x1, starting transfers between devices, local(): lax.all_to_all(d_hidden_tiles.astype(jnp.bfloat16), 'col', split_axis=0,...  8.48 us
    ppermute x4, starting transfers between devices, extended(): lax.ppermute(lax.slice_in_dim(block, 0, width, axis=dim), axis, backward)  7.98 us
    all_to_all x1, waiting for transfers between devices, local(): lax.all_to_all(d_hidden_tiles.astype(jnp.bfloat16), 'col', split_axis=0,...  7.72 us
  transfers between devices with their start and end apart: 11, of which 4 were waited for; matrix products, arithmetic and copies ran while one was open for 15% of the time, Pallas kernels for 0%

commit v1 on v0

v1 whole, which is shorter than its diff:
```python
import functools

import jax
import jax.numpy as jnp
import numpy as np
from jax import lax
from jax.experimental import pallas as pl
from jax.experimental.pallas import tpu as pltpu
from jax.sharding import Mesh
from jax.sharding import PartitionSpec as P

BF = jnp.bfloat16
F32 = jnp.float32
ROW = ("xl", "z")
COL = ("xh", "y", "c")
CHIPS = ("xl", "z", "xh", "y")
GRID = (("xl", 2), ("z", 4), ("xh", 2), ("y", 4), ("c", 2))

C, CF, BANDS, TAPS = 512, 256, 4, 9
TR, TC = 128, 32
IR, IC = 32, 8
CELLS = IR * IC
HB = 16
NB = TR // HB
EARLY = 5 * 2 * 256 + 256
LATE = TAPS * 128
PACK = 4096
PEERS = 64
SCALE = float(1024 * 512) ** (-0.5)
VMEM = 56 * 1024 * 1024


def params(n=1):
    return pltpu.CompilerParams(vmem_limit_bytes=VMEM, dimension_semantics=("arbitrary",) * n)


def dot(a, b, dims=((1,), (0,))):
    return lax.dot_general(a, b, (dims, ((), ())), preferred_element_type=F32)


def haar_matrix():
    out = np.zeros((BANDS, IR // 2, IC // 2, IR, IC), np.float32)
    signs = ((1, 1, 1, 1), (1, -1, 1, -1), (1, 1, -1, -1), (1, -1, -1, 1))
    for k in range(BANDS):
        for i in range(IR // 2):
            for j in range(IC // 2):
                for t in range(4):
                    out[k, i, j, 2 * i + t // 2, 2 * j + t % 2] = 0.5 * signs[k][t]
    return out.reshape(CELLS, CELLS)


def cot_kernel(oc, top, bot, left, right, wconv, shifted, dcoarse, win, sums, pooled):
    i = pl.program_id(0)
    r0 = i * HB
    win[1 : HB + 1, 8 : 8 + TC, :] = oc[pl.ds(r0, HB)].astype(F32)
    before = oc[pl.ds(jnp.maximum(r0 - 1, 0), 1)].astype(F32)
    after = oc[pl.ds(jnp.minimum(r0 + HB, TR - 1), 1)].astype(F32)
    win[0:1, 8 : 8 + TC, :] = jnp.where(i == 0, top[...], before)
    win[HB + 1 : HB + 2, 8 : 8 + TC, :] = jnp.where(i == NB - 1, bot[...], after)
    win[:, 7:8, :] = left[pl.ds(r0, HB + 2)]
    win[:, 8 + TC : 9 + TC, :] = right[pl.ds(r0, HB + 2)]
    for b in range(3):
        shifted[0, :, :, b * CF : (b + 1) * CF] = win[:, 9 - b : 9 - b + TC, :].astype(BF)
    for q in range(HB // 4):
        w = [win[4 * q + t] for t in range(6)]
        mid = w[2] + w[3]
        low = w[1] + mid
        high = mid + w[4]
        for a, part in enumerate((high + w[5], low + w[4], w[0] + low)):
            sums[a, q, 0] = part[:, :128]
            sums[a, q, 1] = part[:, 128:]
    for a in range(3):
        for q in range(HB // 4):
            cells = pl.ds(pl.multiple_of((i * (HB // 4) + q) * IC, IC), IC)
            for h in range(2):
                cols = [sums[a, q, h, pl.ds(7 + s, IC, stride=4), :] for s in range(6)]
                mid = cols[2] + cols[3]
                low = cols[1] + mid
                high = mid + cols[4]
                for b, part in enumerate((high + cols[5], low + cols[4], cols[0] + low)):
                    at = (3 * a + b) * CF + 128 * h
                    pooled[cells, at : at + 128] = part

    @pl.when(i == NB - 1)
    def _():
        total = jnp.zeros((CELLS, CF), F32)
        for t in range(TAPS):
            total += dot(pooled[:, t * CF : (t + 1) * CF].astype(BF), wconv[t], ((1,), (1,)))
        dcoarse[...] = total.astype(BF)


def cot_pass(oc, top, bot, left, right, wconv):
    whole = lambda *s: pl.BlockSpec(s, lambda i: (0,) * len(s))
    return pl.pallas_call(
        cot_kernel,
        grid=(NB,),
        in_specs=[
            whole(TR, TC, CF),
            whole(1, TC, CF),
            whole(1, TC, CF),
            whole(TR + 2, 1, CF),
            whole(TR + 2, 1, CF),
            whole(TAPS, CF, CF),
        ],
        out_specs=[
            pl.BlockSpec((1, HB + 2, TC, 3 * CF), lambda i: (i, 0, 0, 0)),
            whole(CELLS, CF),
        ],
        out_shape=[
            jax.ShapeDtypeStruct((NB, HB + 2, TC, 3 * CF), BF),
            jax.ShapeDtypeStruct((CELLS, CF), BF),
        ],
        scratch_shapes=[
            pltpu.VMEM((HB + 2, 48, CF), F32),
            pltpu.VMEM((3, HB // 4, 2, 48, 128), F32),
            pltpu.VMEM((CELLS, TAPS * CF), F32),
        ],
        compiler_params=params(),
        cost_estimate=pl.CostEstimate(flops=400_000_000, bytes_accessed=10_000_000, transcendentals=0),
        name="cotangent_windows",
    )(oc, top, bot, left, right, wconv)


GELU_A = 0.7978845608028654
GELU_B = 0.044715


def coarse_kernel(x, haar, wband, wpoint, wproj, sub, pre, hidden, cout, mixed):
    k = pl.program_id(0)
    part = dot(haar[pl.ds(pl.multiple_of(k * 64, 64), 64), :], x[...]).astype(BF)
    sub[pl.ds(pl.multiple_of(k * 64, 64), 64), :] = part
    mixed[pl.ds(pl.multiple_of(k * 64, 64), 64), :] = dot(part, wband[0])

    @pl.when(k == BANDS - 1)
    def _():
        m = mixed[...]
        hi = m.astype(BF)
        lo = (m - hi.astype(F32)).astype(BF)
        h = haar[...]
        value = dot(h, hi, ((0,), (0,))) + dot(h, lo, ((0,), (0,))) + dot(x[...], wpoint[...])
        pre[...] = value
        act = 0.5 * value * (1.0 + jnp.tanh(GELU_A * (value + GELU_B * (value * value * value))))
        act = act.astype(BF)
        hidden[...] = act
        cout[...] = dot(act, wproj[...]).astype(BF)


def coarse_pass(x, haar, wband, wpoint, wproj):
    whole = lambda *s: pl.BlockSpec(s, lambda i: (0,) * len(s))
    return pl.pallas_call(
        coarse_kernel,
        grid=(BANDS,),
        in_specs=[
            whole(CELLS, C),
            whole(CELLS, CELLS),
            pl.BlockSpec((1, C, C), lambda i: (i, 0, 0)),
            whole(C, C),
            whole(C, CF),
        ],
        out_specs=[whole(CELLS, C), whole(CELLS, C), whole(CELLS, C), whole(CELLS, CF)],
        out_shape=[
            jax.ShapeDtypeStruct((CELLS, C), BF),
            jax.ShapeDtypeStruct((CELLS, C), F32),
            jax.ShapeDtypeStruct((CELLS, C), BF),
            jax.ShapeDtypeStruct((CELLS, CF), BF),
        ],
        scratch_shapes=[pltpu.VMEM((CELLS, C), F32)],
        compiler_params=params(),
        cost_estimate=pl.CostEstimate(flops=500_000_000, bytes_accessed=5_000_000, transcendentals=131072),
        name="coarse_forward",
    )(x, haar, wband, wpoint, wproj)


def grads_kernel(core, x, haar, wproj, sub, pre, hidden, dco, keep, send):
    value = pre[...]
    square = value * value
    th = jnp.tanh(GELU_A * (value + GELU_B * (value * square)))
    slope = 0.5 * (1.0 + th) + 0.5 * value * (1.0 - th * th) * (GELU_A * (1.0 + 3.0 * GELU_B * square))
    d = dco[...]
    dhid = dot(d, wproj[...], ((1,), (1,)))
    dpre = (dhid * slope).astype(BF)
    dmix = dot(haar[...], dpre).astype(BF)
    for out, c in ((keep, core[0]), (send, 1 - core[0])):
        half = pl.ds(pl.multiple_of(c * 256, 256), 256)
        for k in range(5):
            if k < BANDS:
                g = dot(sub[k * 64 : (k + 1) * 64, half], dmix[k * 64 : (k + 1) * 64], ((0,), (0,)))
            else:
                g = dot(x[:, half], dpre, ((0,), (0,)))
            out[k * 512 : k * 512 + 256, :] = g[:, :256].astype(BF)
            out[k * 512 + 256 : k * 512 + 512, :] = g[:, 256:].astype(BF)
        out[2560:2816, :] = dot(hidden[:, half], d, ((0,), (0,))).astype(BF)


def grads_pass(core, x, haar, wproj, sub, pre, hidden, dco):
    vm = pl.BlockSpec(memory_space=pltpu.VMEM)
    return pl.pallas_call(
        grads_kernel,
        in_specs=[pl.BlockSpec(memory_space=pltpu.SMEM)] + [vm] * 7,
        out_specs=[vm, vm],
        out_shape=[jax.ShapeDtypeStruct((EARLY, 256), BF)] * 2,
        compiler_params=pltpu.CompilerParams(vmem_limit_bytes=VMEM),
        cost_estimate=pl.CostEstimate(flops=600_000_000, bytes_accessed=5_000_000, transcendentals=131072),
        name="coarse_gradients",
    )(core, x, haar, wproj, sub, pre, hidden, dco)


def wgrad_kernel(core, fine, cout, shifted, conv_in, keep, send, up, acc):
    i = pl.program_id(0)
    for q in range(HB // 4):
        cell = cout[q * IC : (q + 1) * IC, :].astype(F32)
        for s in range(4):
            up[q, 0, pl.ds(s, IC, stride=4), :] = cell[:, :128]
            up[q, 1, pl.ds(s, IC, stride=4), :] = cell[:, 128:]
        grown = jnp.concatenate([up[q, 0], up[q, 1]], axis=-1)
        for t in range(4):
            conv_in[4 * q + t] = (fine[4 * q + t].astype(F32) + grown).astype(BF)
    left = conv_in[...].reshape(HB * TC, CF).T
    for a in range(3):
        y = shifted[0, 2 - a : 2 - a + HB].reshape(HB * TC, 3 * CF)
        part = dot(left, y)

        @pl.when(i == 0)
        def _():
            acc[a] = part

        @pl.when(i > 0)
        def _():
            acc[a] += part

    @pl.when(i == NB - 1)
    def _():
        for out, c in ((keep, core[0]), (send, 1 - core[0])):
            half = pl.ds(pl.multiple_of(c * 128, 128), 128)
            for t in range(TAPS):
                b = t % 3
                out[t * 128 : (t + 1) * 128, :] = acc[t // 3, half, b * CF : (b + 1) * CF].astype(BF)


def wgrad_pass(core, fine, cout, shifted):
    whole = lambda *s: pl.BlockSpec(s, lambda i: (0,) * len(s))
    return pl.pallas_call(
        wgrad_kernel,
        grid=(NB,),
        in_specs=[
            pl.BlockSpec(memory_space=pltpu.SMEM),
            pl.BlockSpec((HB, TC, CF), lambda i: (i, 0, 0)),
            pl.BlockSpec((HB // 4 * IC, CF), lambda i: (i, 0)),
            pl.BlockSpec((1, HB + 2, TC, 3 * CF), lambda i: (i, 0, 0, 0)),
        ],
        out_specs=[
            pl.BlockSpec((HB, TC, CF), lambda i: (i, 0, 0)),
            whole(LATE, 256),
            whole(LATE, 256),
        ],
        out_shape=[
            jax.ShapeDtypeStruct((TR, TC, CF), BF),
            jax.ShapeDtypeStruct((LATE, 256), BF),
            jax.ShapeDtypeStruct((LATE, 256), BF),
        ],
        scratch_shapes=[pltpu.VMEM((HB // 4, 2, TC, 128), F32), pltpu.VMEM((3, CF, 3 * CF), F32)],
        compiler_params=params(),
        cost_estimate=pl.CostEstimate(flops=5_000_000_000, bytes_accessed=13_000_000, transcendentals=0),
        name="conv_weight_gradient",
    )(core, fine, cout, shifted)


def conv_kernel(ci, top, bot, left, right, wconv, out, win, wide):
    i = pl.program_id(0)
    r0 = i * HB
    win[1 : HB + 1, 8 : 8 + TC, :] = ci[pl.ds(r0, HB)].astype(F32)
    before = ci[pl.ds(jnp.maximum(r0 - 1, 0), 1)].astype(F32)
    after = ci[pl.ds(jnp.minimum(r0 + HB, TR - 1), 1)].astype(F32)
    win[0:1, 8 : 8 + TC, :] = jnp.where(i == 0, top[...], before)
    win[HB + 1 : HB + 2, 8 : 8 + TC, :] = jnp.where(i == NB - 1, bot[...], after)
    win[:, 7:8, :] = left[pl.ds(r0, HB + 2)]
    win[:, 8 + TC : 9 + TC, :] = right[pl.ds(r0, HB + 2)]
    for b in range(3):
        wide[:, :, b * CF : (b + 1) * CF] = win[:, 7 + b : 7 + b + TC, :].astype(BF)
    total = jnp.zeros((HB * TC, CF), F32)
    for a in range(3):
        total += dot(wide[a : a + HB].reshape(HB * TC, 3 * CF), wconv[a])
    out[...] = total.astype(BF).reshape(HB, TC, CF)


def conv_pass(ci, top, bot, left, right, wconv):
    whole = lambda *s: pl.BlockSpec(s, lambda i: (0,) * len(s))
    return pl.pallas_call(
        conv_kernel,
        grid=(NB,),
        in_specs=[
            whole(TR, TC, CF),
            whole(1, TC, CF),
            whole(1, TC, CF),
            whole(TR + 2, 1, CF),
            whole(TR + 2, 1, CF),
            whole(3, 3 * CF, CF),
        ],
        out_specs=pl.BlockSpec((HB, TC, CF), lambda i: (i, 0, 0)),
        out_shape=jax.ShapeDtypeStruct((TR, TC, CF), BF),
        scratch_shapes=[pltpu.VMEM((HB + 2, 48, CF), F32), pltpu.VMEM((HB + 2, TC, 3 * CF), BF)],
        compiler_params=params(),
        cost_estimate=pl.CostEstimate(flops=5_000_000_000, bytes_accessed=6_000_000, transcendentals=0),
        name="conv_forward",
    )(ci, top, bot, left, right, wconv.reshape(3, 3 * CF, CF))


def finish_kernel(core, mine, other, conv, band, point, proj):
    own = core[0] == 0

    def place(out, rows, n, start, cols):
        a = mine[start : start + n, :]
        b = other[start : start + n, :]
        out[rows : rows + n, cols : cols + 256] = jnp.where(own, a, b).astype(F32)
        out[rows + n : rows + 2 * n, cols : cols + 256] = jnp.where(own, b, a).astype(F32)

    for k in range(BANDS):
        place(band.at[k], 0, 256, k * 512, 0)
        place(band.at[k], 0, 256, k * 512 + 256, 256)
    place(point, 0, 256, 2048, 0)
    place(point, 0, 256, 2304, 256)
    place(proj, 0, 256, 2560, 0)
    for t in range(TAPS):
        place(conv.at[t], 0, 128, EARLY + t * 128, 0)


def finish_pass(core, mine, other):
    vm = pl.BlockSpec(memory_space=pltpu.VMEM)
    return pl.pallas_call(
        finish_kernel,
        in_specs=[pl.BlockSpec(memory_space=pltpu.SMEM), vm, vm],
        out_specs=[vm] * 4,
        out_shape=[
            jax.ShapeDtypeStruct((TAPS, CF, CF), F32),
            jax.ShapeDtypeStruct((BANDS, C, C), F32),
            jax.ShapeDtypeStruct((C, C), F32),
            jax.ShapeDtypeStruct((C, CF), F32),
        ],
        compiler_params=pltpu.CompilerParams(vmem_limit_bytes=VMEM),
        name="place_gradients",
    )(core, mine, other)


def neighbours(axes, count):
    forward = [(i, i + 1) for i in range(count - 1)]
    return forward, [(b, a) for a, b in forward]


def halo(tile):
    forward, backward = neighbours(COL, 16)
    west = lax.ppermute(tile[:, TC - 1 :], COL, forward)
    east = lax.ppermute(tile[:, :1], COL, backward)
    forward, backward = neighbours(ROW, 8)
    low = jnp.concatenate([tile[TR - 1 :], west[TR - 1 :], east[TR - 1 :]], axis=1)
    high = jnp.concatenate([tile[:1], west[:1], east[:1]], axis=1)
    above = lax.ppermute(low, ROW, forward)
    below = lax.ppermute(high, ROW, backward)
    left = jnp.concatenate([above[:, TC : TC + 1], west, below[:, TC : TC + 1]], axis=0)
    right = jnp.concatenate([above[:, TC + 1 :], east, below[:, TC + 1 :]], axis=0)
    return above[:, :TC].astype(F32), below[:, :TC].astype(F32), left.astype(F32), right.astype(F32)


def local(coarse_in, fine_in, band_weight, point_weight, proj_weight, conv_weight, out_cot):
    core = lax.axis_index("c").astype(jnp.int32).reshape(1)
    haar = jnp.asarray(haar_matrix(), BF)
    x = lax.all_to_all(coarse_in, COL, 1, 0, tiled=True).reshape(CELLS, C)
    top, bot, left, right = halo(out_cot)
    shifted, dco = cot_pass(out_cot, top, bot, left, right, conv_weight)
    sub, pre, hidden, cout = coarse_pass(x, haar, band_weight, point_weight, proj_weight)
    conv_in, keep_late, send_late = wgrad_pass(core, fine_in, cout, shifted)
    keep_early, send_early = grads_pass(core, x, haar, proj_weight, sub, pre, hidden, dco)
    swap = [(0, 1), (1, 0)]
    got_late = lax.ppermute(send_late, "c", swap)
    got_early = lax.ppermute(send_early, "c", swap)
    chip = jnp.concatenate(
        [
            keep_early.astype(F32) + got_early.astype(F32),
            keep_late.astype(F32) + got_late.astype(F32),
            jnp.zeros((PACK - EARLY - LATE, 256), F32),
        ]
    ).astype(BF)
    parts = lax.all_to_all(chip, CHIPS, 0, 0, tiled=True).reshape(PEERS, PACK // PEERS, 256)
    done = (jnp.sum(parts.astype(F32), axis=0) * SCALE).astype(BF)
    spread = jnp.broadcast_to(done[None], (PEERS, PACK // PEERS, 256)).reshape(PACK, 256)
    mine = lax.all_to_all(spread, CHIPS, 0, 0, tiled=True)
    other = lax.ppermute(mine, "c", swap)
    grad_conv, grad_band, grad_point, grad_proj = finish_pass(core, mine, other)
    fine_out = conv_pass(conv_in, *halo(conv_in), conv_weight)
    return fine_out, grad_conv, grad_band, grad_point, grad_proj


def solution(mesh):
    fine_mesh = Mesh(
        np.asarray(mesh.devices).reshape([n for _, n in GRID]), tuple(name for name, _ in GRID)
    )
    fine = P(ROW, COL, None)
    in_specs = (P(ROW + COL, None, None), fine, P(), P(), P(), P(), fine)
    out_specs = (fine, P(), P(), P(), P())
    return jax.shard_map(local, mesh=fine_mesh, in_specs=in_specs, out_specs=out_specs, check_vma=False)
```

time: 364 us -> 181 us (0.50); the launches traced: 359 us -> 180 us
  waiting for transfers between devices: 148 us -> 30.8 us
  matrix products: 105 us -> 0 us
  Pallas kernels: 0 us -> 47.5 us
  blocking collectives: 0 us -> 41 us
  local copies, waits for them, and re-layouts: 30 us -> 9.92 us
  between operations: 14.8 us -> 0.84 us
  other arithmetic: 23.2 us -> 10.4 us
    psum x1 -> x0, waiting for transfers between devices: 137 us -> none  [local(): lax.psum((kernel_local, band_local, point_local, proj_local), ('row', 'co...]
    dot_general x34 -> x0, matrix products: 105 us -> none  [the longest x21 68.3 us: project_rows(): result = jnp.dot(flat, weight, preferred_element_type=jnp.float32)]
    pallas_call x0 -> x6, Pallas kernels: none -> 47.5 us  [the longest x1 14.9 us: wgrad_pass(): pl.pallas_call(wgrad_kernel, grid=(NB,), in_specs=[pl.BlockSpec(memory_sp...]
    all_to_all x0 -> x1, blocking collectives: none -> 41 us  [local(): lax.all_to_all(chip, CHIPS, 0, 0, tiled=True)]
    ppermute x8 -> x11, waiting for transfers between devices: 0.26 us -> 11.4 us  [the longest x2 5.98 us: halo(): below = lax.ppermute(high, ROW, backward)]
    all_to_all x2, waiting for transfers between devices: 10.9 us -> 19.4 us  [the longest x1 19.4 us: local(): mine = lax.all_to_all(spread, CHIPS, 0, 0, tiled=True)]
    mul x4 -> x0, other arithmetic: 8.19 us -> none  [the longest x1 3.42 us: local(): kernel_sum * loss_scale]
    convert_element_type x3 -> x0, local copies, waits for them, and re-layouts: 6.42 us -> none  [the longest x2 5.44 us: local(): upsample(coarse_out).astype(jnp.float32)]
  transfers between devices with their start and end apart: 11 -> 13, of which waited for: 4 -> 5; matrix products, arithmetic and copies ran while one was open for 15% -> 6% of each run, Pallas kernels for 0% -> 18%
where the time goes in v1:
time: 181 us; the launch traced here: 180 us
  Pallas kernels  47.5 us (26%)
  blocking collectives  41 us (23%)
  starting transfers between devices  39.8 us (22%)
  waiting for transfers between devices  30.8 us (17%)
  other arithmetic  10.4 us (6%)
  local copies, waits for them, and re-layouts  9.92 us (5%)
    all_to_all x1, blocking collectives, local(): lax.all_to_all(chip, CHIPS, 0, 0, tiled=True)  41 us
    all_to_all x1, waiting for transfers between devices, local(): mine = lax.all_to_all(spread, CHIPS, 0, 0, tiled=True)  19.4 us
    pallas_call x1, Pallas kernels, wgrad_pass(): pl.pallas_call(wgrad_kernel, grid=(NB,), in_specs=[pl.BlockSpec(memory_sp...  14.9 us
    pallas_call x1, Pallas kernels, conv_pass(): pl.pallas_call(conv_kernel, grid=(NB,), in_specs=[whole(TR, TC, CF), whol...  9.4 us
    all_to_all x1, starting transfers between devices, local(): x = lax.all_to_all(coarse_in, COL, 1, 0, tiled=True).reshape(CELLS, C)  8.45 us
    all_to_all x1, starting transfers between devices, local(): mine = lax.all_to_all(spread, CHIPS, 0, 0, tiled=True)  8.22 us
    pallas_call x1, Pallas kernels, cot_pass(): pl.pallas_call(cot_kernel, grid=(NB,), in_specs=[whole(TR, TC, CF), whole...  8.09 us
    ppermute x2, starting transfers between devices, halo(): west = lax.ppermute(tile[:, TC - 1:], COL, forward)  7.68 us
  transfers between devices with their start and end apart: 13, of which 5 were waited for; matrix products, arithmetic and copies ran while one was open for 6% of the time, Pallas kernels for 18%

profile of v1, /device:TPU:1, one launch (start us, length us, event | category | flops | bytes accessed | tf_op | source)
XLA Modules:
  0.0 180.2 jit_solution(422844504839547207)
XLA Ops:
  0.6 1.9 %copy.14 = bf16[2,128,512]{2,0,1:T(2,128)(2,1)} copy(bf16[2,128,512]{2,1,0:T(8,128)(2,1)} %param.8) | data formatting | bytes 524288 | tf_op args[0]
  2.6 8.4 %all-to-all-start = ((bf16[2,128,512]{2,0,1:T(2,128)(2,1)}), bf16[2,128,512]{2,0,1:T(2,128)(2,1)S(1)}, u32[]{:S(2)}, u32[]{:S(2)}) async-start(bf16[2,128,512]{2,0,1:T(2,128)(2,1)} %copy.14), calls=%async_computation | async-start | bytes 524288 | tf_op jit(solution)/shard_map/all_to_all | solution.py:366
  11.0 1.4 fusion.3
  12.4 3.5 %collective-permute-start = (bf16[128,1,256]{2,1,0:T(2,128)(2,1)S(1)}, bf16[128,1,256]{2,1,0:T(2,128)(2,1)S(1)}, u32[]{:S(2)}, u32[]{:S(2)}) collective-permute-start(bf16[128,1,256]{2,1,0:T(2,128)(2,1)S(1)} %get-tuple-element.41), channel_id=1, source_target_pairs={{0,1},{1,2},{2,3},{3,4},{4,5},{5,6},{6,7},{7,8},{8,9},{9,10},{10,1... | collective-permute-start | bytes 196616 | tf_op jit(solution)/shard_map/ppermute | solution.py:351
  16.0 1.9 %collective-permute-start.1 = (bf16[128,1,256]{2,1,0:T(2,128)(2,1)S(1)}, bf16[128,1,256]{2,1,0:T(2,128)(2,1)S(1)}, u32[]{:S(2)}, u32[]{:S(2)}) collective-permute-start(bf16[128,1,256]{2,1,0:T(2,128)(2,1)S(1)} %get-tuple-element.42), channel_id=1, source_target_pairs={{1,0},{2,1},{3,2},{4,3},{5,4},{6,5},{7,6},{8,7},{9,8},{10,9},{11,1... | collective-permute-start | bytes 196616 | tf_op jit(solution)/shard_map/ppermute | solution.py:352
  17.9 0.7 fusion.2
  18.6 3.6 %collective-permute-done.1 = bf16[128,1,256]{2,1,0:T(2,128)(2,1)S(1)} collective-permute-done((bf16[128,1,256]{2,1,0:T(2,128)(2,1)S(1)}, bf16[128,1,256]{2,1,0:T(2,128)(2,1)S(1)}, u32[]{:S(2)}, u32[]{:S(2)}) %collective-permute-start.1) | collective-permute-done | bytes 65568 | tf_op jit(solution)/shard_map/ppermute | solution.py:352
  22.3 3.5 %collective-permute-start.2 = (bf16[1,34,256]{2,1,0:T(8,128)(2,1)S(1)}, bf16[1,34,256]{2,1,0:T(8,128)(2,1)S(1)}, u32[]{:S(2)}, u32[]{:S(2)}) collective-permute-start(bf16[1,34,256]{2,1,0:T(8,128)(2,1)S(1)} %pad_maximum_fusion), channel_id=1, source_target_pairs={{0,16},{16,32},{32,48},{48,64},{64,80},{80,96},{96,112},{1,17},{17... | collective-permute-start | bytes 52232 | tf_op jit(solution)/shard_map/ppermute | solution.py:356
  25.8 1.3 collective-permute-start.3
  27.1 0.6 slice_convert_fusion.3.top
  27.8 2.8 %collective-permute-done.3 = bf16[1,34,256]{2,1,0:T(8,128)(2,1)S(1)} collective-permute-done((bf16[1,34,256]{2,1,0:T(8,128)(2,1)S(1)}, bf16[1,34,256]{2,1,0:T(8,128)(2,1)S(1)}, u32[]{:S(2)}, u32[]{:S(2)}) %collective-permute-start.3) | collective-permute-done | bytes 17440 | tf_op jit(solution)/shard_map/ppermute | solution.py:357
  30.6 1.1 maximum_convert_fusion
  31.7 0.6 slice_convert_fusion.2.bot
  32.3 8.1 %cotangent_windows.1 = (bf16[8,18,32,768]{3,2,1,0:T(8,128)(2,1)}, bf16[256,256]{1,0:T(8,128)(2,1)}) custom-call(bf16[128,32,256]{2,1,0:T(8,128)(2,1)} %oc.1, f32[1,32,256]{2,1,0:T(8,128)} %slice_convert_fusion.3.top, f32[1,32,256]{2,1,0:T(8,128)} %slice_convert_fusion.2.bot, f32[130,1,256]{2,1,0:T(1,128)} %get-tuple-element.59.left, ...), custom_call_target="tpu_custom_call" | custom-call | flops 400000000 | bytes 10000000 | tf_op jit(solution)/shard_map/cotangent_windows/pallas_call | solution.py:94
  40.4 0.0 all-to-all-done
  40.4 0.7 copy.15
  41.1 5.2 %coarse_forward.1 = (bf16[256,512]{1,0:T(8,128)(2,1)}, f32[256,512]{1,0:T(8,128)}, bf16[256,512]{1,0:T(8,128)(2,1)}, bf16[256,256]{1,0:T(8,128)(2,1)}) custom-call(bf16[256,512]{1,0:T(8,128)(2,1)} %bitcast.12, bf16[256,256]{1,0:T(8,128)(2,1)} %constant.13.clone.haar, bf16[4,512,512]{2,1,0:T(8,128)(2,1)} %wband.1, bf16[512,512]{1,0:T(8,128)(2,1)} %wpoint.1, ...), custom_call_target="tpu_custom_call" | custom-call | flops 500000000 | bytes 5000000 | tf_op jit(solution)/shard_map/coarse_forward/pallas_call | solution.py:150
  46.3 4.1 %coarse_gradients.1 = (bf16[2816,256]{1,0:T(8,128)(2,1)}, bf16[2816,256]{1,0:T(8,128)(2,1)}) custom-call(s32[1]{0:T(128)} %bitcast.core, bf16[256,512]{1,0:T(8,128)(2,1)} %bitcast.13, bf16[256,256]{1,0:T(8,128)(2,1)} %constant.13.clone.haar, bf16[512,256]{1,0:T(8,128)(2,1)} %wproj.3, bf16[256,512]{1,0:T(8,128)(2,1)} %get-tuple-element.23.sub, ...), custom_call_target="tpu_custom_call" | custom-call | flops 600000000 | bytes 5000000 | tf_op jit(solution)/shard_map/coarse_gradients/pallas_call | solution.py:197
  50.4 0.0 collective-permute-start.8
  50.4 14.9 %conv_weight_gradient.1 = (bf16[128,32,256]{2,1,0:T(8,128)(2,1)}, bf16[1152,256]{1,0:T(8,128)(2,1)}, bf16[1152,256]{1,0:T(8,128)(2,1)}) custom-call(s32[1]{0:T(128)} %bitcast.core, bf16[128,32,256]{2,1,0:T(8,128)(2,1)} %fine.1, bf16[256,256]{1,0:T(8,128)(2,1)} %get-tuple-element.20.cout, bf16[8,18,32,768]{3,2,1,0:T(8,128)(2,1)} %get-tuple-element.21.shifted), custom_call_target="tpu_custom_call" | custom-call | flops 5000000000 | bytes 13000000 | tf_op jit(solution)/shard_map/conv_weight_gradient/pallas_call | solution.py:242
  65.3 0.6 collective-permute-start.9
  65.9 1.8 %collective-permute-done.9 = bf16[1152,256]{1,0:T(8,128)(2,1)S(1)} collective-permute-done((bf16[1152,256]{1,0:T(8,128)(2,1)}, bf16[1152,256]{1,0:T(8,128)(2,1)S(1)}, u32[]{:S(2)}, u32[]{:S(2)}) %collective-permute-start.9) | collective-permute-done | bytes 589856 | tf_op jit(solution)/shard_map/ppermute | solution.py:373
  67.7 1.2 add_convert_fusion.1
  69.0 0.4 add_convert_fusion
  69.3 3.2 %maximum_maximum_fusion = bf16[4096,256]{1,0:T(8,128)(2,1)S(1)} fusion(bf16[1152,256]{1,0:T(8,128)(2,1)S(1)} %add_convert_fusion.1, bf16[2816,256]{1,0:T(8,128)(2,1)S(1)} %add_convert_fusion, bf16[4096]{0:T(1024)(128)(2,1)S(1)} %pad.2.clone), kind=kLoop, calls=%fused_computation.2 | loop fusion | flops 6291456 | bytes 4136960 | tf_op jit(solution)/shard_map/concatenate | solution.py:375
  72.6 41.0 %all_to_all.29 = bf16[64,64,256]{2,1,0:T(8,128)(2,1)S(1)} all-to-all(bf16[64,64,256]{2,1,0:T(8,128)(2,1)S(1)} %bitcast.10), channel_id=1, replica_groups=mesh['xl'=2,'z'=4,'xh'=2,'y'=4,'c'=2] {'xl','z','xh','y'}, dimensions={0} | all-to-all | bytes 4194304 | tf_op jit(solution)/shard_map/all_to_all | solution.py:382
  113.5 0.3 convert_reduce_fusion
  113.8 1.6 broadcast_in_dim.10
  115.4 8.2 %all-to-all-start.2 = ((bf16[64,64,256]{2,1,0:T(8,128)(2,1)}), bf16[64,64,256]{2,1,0:T(8,128)(2,1)S(1)}, u32[]{:S(2)}, u32[]{:S(2)}) async-start(bf16[64,64,256]{2,1,0:T(8,128)(2,1)} %broadcast_in_dim.10), calls=%async_computation.2 | async-start | bytes 4194304 | tf_op jit(solution)/shard_map/all_to_all | solution.py:385
  123.6 1.4 fusion.1
  125.1 4.1 %collective-permute-start.4 = (bf16[128,1,256]{2,1,0:T(2,128)(2,1)S(1)}, bf16[128,1,256]{2,1,0:T(2,128)(2,1)S(1)}, u32[]{:S(2)}, u32[]{:S(2)}) collective-permute-start(bf16[128,1,256]{2,1,0:T(2,128)(2,1)S(1)} %get-tuple-element.37), channel_id=1, source_target_pairs={{0,1},{1,2},{2,3},{3,4},{4,5},{5,6},{6,7},{7,8},{8,9},{9,10},{10,1... | collective-permute-start | bytes 196616 | tf_op jit(solution)/shard_map/ppermute | solution.py:351
  129.2 0.7 fusion
  130.0 1.9 %collective-permute-start.5 = (bf16[128,1,256]{2,1,0:T(2,128)(2,1)S(1)}, bf16[128,1,256]{2,1,0:T(2,128)(2,1)S(1)}, u32[]{:S(2)}, u32[]{:S(2)}) collective-permute-start(bf16[128,1,256]{2,1,0:T(2,128)(2,1)S(1)} %get-tuple-element.38), channel_id=1, source_target_pairs={{1,0},{2,1},{3,2},{4,3},{5,4},{6,5},{7,6},{8,7},{9,8},{10,9},{11,1... | collective-permute-start | bytes 196616 | tf_op jit(solution)/shard_map/ppermute | solution.py:352
  131.9 19.4 %all-to-all-done.2 = bf16[64,64,256]{2,1,0:T(8,128)(2,1)S(1)} async-done(((bf16[64,64,256]{2,1,0:T(8,128)(2,1)}), bf16[64,64,256]{2,1,0:T(8,128)(2,1)S(1)}, u32[]{:S(2)}, u32[]{:S(2)}) %all-to-all-start.2) | async-done | bytes 2097184 | tf_op jit(solution)/shard_map/all_to_all | solution.py:385
  151.3 2.1 %collective-permute-start.10 = (bf16[4096,256]{1,0:T(8,128)(2,1)S(1)}, bf16[4096,256]{1,0:T(8,128)(2,1)S(1)}, u32[]{:S(2)}, u32[]{:S(2)}) collective-permute-start(bf16[4096,256]{1,0:T(8,128)(2,1)S(1)} %bitcast.8), channel_id=1, source_target_pairs={{0,1},{1,0},{2,3},{3,2},{4,5},{5,4},{6,7},{7,6},{8,9},{9,8},{10,11... | collective-permute-start | bytes 6291464 | tf_op jit(solution)/shard_map/ppermute | solution.py:386
  153.4 0.0 collective-permute-done.5
  153.4 2.8 %collective-permute-start.6 = (bf16[1,34,256]{2,1,0:T(8,128)(2,1)S(1)}, bf16[1,34,256]{2,1,0:T(8,128)(2,1)S(1)}, u32[]{:S(2)}, u32[]{:S(2)}) collective-permute-start(bf16[1,34,256]{2,1,0:T(8,128)(2,1)S(1)} %pad_maximum_fusion.2), channel_id=1, source_target_pairs={{0,16},{16,32},{32,48},{48,64},{64,80},{80,96},{96,112},{1,17},{17... | collective-permute-start | bytes 52232 | tf_op jit(solution)/shard_map/ppermute | solution.py:356
  156.2 1.3 collective-permute-start.7
  157.5 0.0 collective-permute-done.6
  157.5 3.2 %collective-permute-done.7 = bf16[1,34,256]{2,1,0:T(8,128)(2,1)S(1)} collective-permute-done((bf16[1,34,256]{2,1,0:T(8,128)(2,1)S(1)}, bf16[1,34,256]{2,1,0:T(8,128)(2,1)S(1)}, u32[]{:S(2)}, u32[]{:S(2)}) %collective-permute-start.7) | collective-permute-done | bytes 17440 | tf_op jit(solution)/shard_map/ppermute | solution.py:357
  160.7 0.9 maximum_convert_fusion.3.right
  161.6 0.9 maximum_convert_fusion.2.left
  162.5 0.6 slice_convert_fusion.1.top
  163.1 0.6 slice_convert_fusion.bot
  163.7 9.4 %conv_forward.1 = bf16[128,32,256]{2,1,0:T(8,128)(2,1)} custom-call(bf16[128,32,256]{2,1,0:T(8,128)(2,1)} %get-tuple-element.22.ci, f32[1,32,256]{2,1,0:T(8,128)} %slice_convert_fusion.1.top, f32[1,32,256]{2,1,0:T(8,128)} %slice_convert_fusion.bot, f32[130,1,256]{2,1,0:T(1,128)} %maximum_convert_fusion.2.left, f32[130,1,256]{2,1,0:T(1,128)} %maximum_convert_fusion.3.right, ...), custom_call_target="tpu_custom_call" | custom-call | flops 5000000000 | bytes 6000000 | tf_op jit(solution)/shard_map/conv_forward/pallas_call | solution.py:288
  173.1 0.0 collective-permute-done.10.other
  173.1 1.3 copy-done.1
  174.4 5.8 %place_gradients.1 = (f32[9,256,256]{2,1,0:T(8,128)}, f32[4,512,512]{2,1,0:T(8,128)}, f32[512,512]{1,0:T(8,128)}, f32[512,256]{1,0:T(8,128)}) custom-call(s32[1]{0:T(128)} %bitcast.core, bf16[4096,256]{1,0:T(8,128)(2,1)} %bitcast.9, bf16[4096,256]{1,0:T(8,128)(2,1)} %copy-done.1), custom_call_target="tpu_custom_call" | custom-call | tf_op jit(solution)/shard_map/place_gradients/pallas_call | solution.py:329
  (24 shorter events, 0.1 us)
Async XLA Ops:
  2.6 37.8 %all-to-all-start = ((bf16[2,128,512]{2,0,1:T(2,128)(2,1)}), bf16[2,128,512]{2,0,1:T(2,128)(2,1)S(1)}, u32[]{:S(2)}, u32[]{:S(2)}) async-start(bf16[2,128,512]{2,0,1:T(2,128)(2,1)} %copy.14), calls=%async_computation | async-start | bytes 524288 | tf_op jit(solution)/shard_map/all_to_all | solution.py:366
  12.4 6.2 %collective-permute-start = (bf16[128,1,256]{2,1,0:T(2,128)(2,1)S(1)}, bf16[128,1,256]{2,1,0:T(2,128)(2,1)S(1)}, u32[]{:S(2)}, u32[]{:S(2)}) collective-permute-start(bf16[128,1,256]{2,1,0:T(2,128)(2,1)S(1)} %get-tuple-element.41), channel_id=1, source_target_pairs={{0,1},{1,2},{2,3},{3,4},{4,5},{5,6},{6,7},{7,8},{8,9},{9,10},{10,1... | collective-permute-start | bytes 196616 | tf_op jit(solution)/shard_map/ppermute | solution.py:351
  16.0 6.3 %collective-permute-start.1 = (bf16[128,1,256]{2,1,0:T(2,128)(2,1)S(1)}, bf16[128,1,256]{2,1,0:T(2,128)(2,1)S(1)}, u32[]{:S(2)}, u32[]{:S(2)}) collective-permute-start(bf16[128,1,256]{2,1,0:T(2,128)(2,1)S(1)} %get-tuple-element.42), channel_id=1, source_target_pairs={{1,0},{2,1},{3,2},{4,3},{5,4},{6,5},{7,6},{8,7},{9,8},{10,9},{11,1... | collective-permute-start | bytes 196616 | tf_op jit(solution)/shard_map/ppermute | solution.py:352
  22.3 4.9 %collective-permute-start.2 = (bf16[1,34,256]{2,1,0:T(8,128)(2,1)S(1)}, bf16[1,34,256]{2,1,0:T(8,128)(2,1)S(1)}, u32[]{:S(2)}, u32[]{:S(2)}) collective-permute-start(bf16[1,34,256]{2,1,0:T(8,128)(2,1)S(1)} %pad_maximum_fusion), channel_id=1, source_target_pairs={{0,16},{16,32},{32,48},{48,64},{64,80},{80,96},{96,112},{1,17},{17... | collective-permute-start | bytes 52232 | tf_op jit(solution)/shard_map/ppermute | solution.py:356
  25.8 4.7 %collective-permute-start.3 = (bf16[1,34,256]{2,1,0:T(8,128)(2,1)S(1)}, bf16[1,34,256]{2,1,0:T(8,128)(2,1)S(1)}, u32[]{:S(2)}, u32[]{:S(2)}) collective-permute-start(bf16[1,34,256]{2,1,0:T(8,128)(2,1)S(1)} %pad_maximum_fusion.1), channel_id=1, source_target_pairs={{16,0},{32,16},{48,32},{64,48},{80,64},{96,80},{112,96},{17,1},{33... | collective-permute-start | bytes 52232 | tf_op jit(solution)/shard_map/ppermute | solution.py:357
  50.4 18.5 %collective-permute-start.8 = (bf16[2816,256]{1,0:T(8,128)(2,1)}, bf16[2816,256]{1,0:T(8,128)(2,1)S(1)}, u32[]{:S(2)}, u32[]{:S(2)}) collective-permute-start(bf16[2816,256]{1,0:T(8,128)(2,1)} %get-tuple-element.28), channel_id=1, source_target_pairs={{0,1},{1,0},{2,3},{3,2},{4,5},{5,4},{6,7},{7,6},{8,9},{9,8},{10,11... | collective-permute-start | bytes 4325384 | tf_op jit(solution)/shard_map/ppermute | solution.py:374
  65.3 3.6 %copy-start.2 = (bf16[2816,256]{1,0:T(8,128)(2,1)S(1)}, bf16[2816,256]{1,0:T(8,128)(2,1)}, u32[]{:S(2)}) copy-start(bf16[2816,256]{1,0:T(8,128)(2,1)} %get-tuple-element.27) | copy-start | bytes 4325380
  65.3 2.4 %collective-permute-start.9 = (bf16[1152,256]{1,0:T(8,128)(2,1)}, bf16[1152,256]{1,0:T(8,128)(2,1)S(1)}, u32[]{:S(2)}, u32[]{:S(2)}) collective-permute-start(bf16[1152,256]{1,0:T(8,128)(2,1)} %get-tuple-element.30), channel_id=1, source_target_pairs={{0,1},{1,0},{2,3},{3,2},{4,5},{5,4},{6,7},{7,6},{8,9},{9,8},{10,11... | collective-permute-start | bytes 1769480 | tf_op jit(solution)/shard_map/ppermute | solution.py:373
  115.4 35.8 %all-to-all-start.2 = ((bf16[64,64,256]{2,1,0:T(8,128)(2,1)}), bf16[64,64,256]{2,1,0:T(8,128)(2,1)S(1)}, u32[]{:S(2)}, u32[]{:S(2)}) async-start(bf16[64,64,256]{2,1,0:T(8,128)(2,1)} %broadcast_in_dim.10), calls=%async_computation.2 | async-start | bytes 4194304 | tf_op jit(solution)/shard_map/all_to_all | solution.py:385
  125.1 28.3 %collective-permute-start.4 = (bf16[128,1,256]{2,1,0:T(2,128)(2,1)S(1)}, bf16[128,1,256]{2,1,0:T(2,128)(2,1)S(1)}, u32[]{:S(2)}, u32[]{:S(2)}) collective-permute-start(bf16[128,1,256]{2,1,0:T(2,128)(2,1)S(1)} %get-tuple-element.37), channel_id=1, source_target_pairs={{0,1},{1,2},{2,3},{3,4},{4,5},{5,6},{6,7},{7,8},{8,9},{9,10},{10,1... | collective-permute-start | bytes 196616 | tf_op jit(solution)/shard_map/ppermute | solution.py:351
  130.0 23.4 %collective-permute-start.5 = (bf16[128,1,256]{2,1,0:T(2,128)(2,1)S(1)}, bf16[128,1,256]{2,1,0:T(2,128)(2,1)S(1)}, u32[]{:S(2)}, u32[]{:S(2)}) collective-permute-start(bf16[128,1,256]{2,1,0:T(2,128)(2,1)S(1)} %get-tuple-element.38), channel_id=1, source_target_pairs={{1,0},{2,1},{3,2},{4,3},{5,4},{6,5},{7,6},{8,7},{9,8},{10,9},{11,1... | collective-permute-start | bytes 196616 | tf_op jit(solution)/shard_map/ppermute | solution.py:352
  151.2 21.8 %copy-start = (bf16[64,64,256]{2,1,0:T(8,128)(2,1)}, bf16[64,64,256]{2,1,0:T(8,128)(2,1)S(1)}, u32[]{:S(2)}) copy-start(bf16[64,64,256]{2,1,0:T(8,128)(2,1)S(1)} %all-to-all-done.2) | copy-start | bytes 6291460
  151.3 21.8 %collective-permute-start.10 = (bf16[4096,256]{1,0:T(8,128)(2,1)S(1)}, bf16[4096,256]{1,0:T(8,128)(2,1)S(1)}, u32[]{:S(2)}, u32[]{:S(2)}) collective-permute-start(bf16[4096,256]{1,0:T(8,128)(2,1)S(1)} %bitcast.8), channel_id=1, source_target_pairs={{0,1},{1,0},{2,3},{3,2},{4,5},{5,4},{6,7},{7,6},{8,9},{9,8},{10,11... | collective-permute-start | bytes 6291464 | tf_op jit(solution)/shard_map/ppermute | solution.py:386
  153.4 4.1 %collective-permute-start.6 = (bf16[1,34,256]{2,1,0:T(8,128)(2,1)S(1)}, bf16[1,34,256]{2,1,0:T(8,128)(2,1)S(1)}, u32[]{:S(2)}, u32[]{:S(2)}) collective-permute-start(bf16[1,34,256]{2,1,0:T(8,128)(2,1)S(1)} %pad_maximum_fusion.2), channel_id=1, source_target_pairs={{0,16},{16,32},{32,48},{48,64},{64,80},{80,96},{96,112},{1,17},{17... | collective-permute-start | bytes 52232 | tf_op jit(solution)/shard_map/ppermute | solution.py:356
  156.2 4.5 %collective-permute-start.7 = (bf16[1,34,256]{2,1,0:T(8,128)(2,1)S(1)}, bf16[1,34,256]{2,1,0:T(8,128)(2,1)S(1)}, u32[]{:S(2)}, u32[]{:S(2)}) collective-permute-start(bf16[1,34,256]{2,1,0:T(8,128)(2,1)S(1)} %pad_maximum_fusion.3), channel_id=1, source_target_pairs={{16,0},{32,16},{48,32},{64,48},{80,64},{96,80},{112,96},{17,1},{33... | collective-permute-start | bytes 52232 | tf_op jit(solution)/shard_map/ppermute | solution.py:357
  173.1 1.3 copy-start.1

commit v2 on v1

v2 whole, which is shorter than its diff:
```python
import functools

import jax
import jax.numpy as jnp
import numpy as np
from jax import lax
from jax.experimental import pallas as pl
from jax.experimental.pallas import tpu as pltpu
from jax.sharding import Mesh
from jax.sharding import PartitionSpec as P

BF = jnp.bfloat16
F32 = jnp.float32
ROW = ("xl", "z")
COL = ("xh", "y", "c")
CHIPS = ("xl", "z", "xh", "y")
GRID = (("xl", 2), ("z", 4), ("xh", 2), ("y", 4), ("c", 2))

C, CF, BANDS, TAPS = 512, 256, 4, 9
TR, TC = 128, 32
IR, IC = 32, 8
CELLS = IR * IC
PAIR = 2 * CELLS
HB = 32
NB = TR // HB
SIDE = 136
EARLY = 5 * 4 * 256 + 2 * 256
LATE = TAPS * 2 * 128
PEERS = 64
SCALE = float(1024 * 512) ** (-0.5)
MIB = 1024 * 1024
GELU_A = 0.7978845608028654
GELU_B = 0.044715


def params(mib, grid=1):
    return pltpu.CompilerParams(
        vmem_limit_bytes=mib * MIB, dimension_semantics=("arbitrary",) * grid if grid else None
    )


def cost(flops, moved):
    return pl.CostEstimate(flops=flops, bytes_accessed=moved, transcendentals=0)


def whole(*shape):
    return pl.BlockSpec(shape, lambda i: (0,) * len(shape))


def dot(a, b, dims=((1,), (0,))):
    return lax.dot_general(a, b, (dims, ((), ())), preferred_element_type=F32)


def haar_matrix():
    out = np.zeros((BANDS, 8, 8, 16, 16), np.float32)
    signs = ((1, 1, 1, 1), (1, -1, 1, -1), (1, 1, -1, -1), (1, -1, -1, 1))
    for k in range(BANDS):
        for i in range(8):
            for j in range(8):
                for t in range(4):
                    out[k, i, j, 2 * i + t // 2, 2 * j + t % 2] = 0.5 * signs[k][t]
    return out.reshape(256, 256)


def pool_matrices():
    inner = np.zeros((3, 3, IC, 6, TC), np.float32)
    side = np.zeros((3, IR, SIDE), np.float32)
    for a in range(3):
        for b in range(3):
            for j in range(IC):
                low, high = max(4 * j - b + 1, 0), min(4 * j - b + 4, TC - 1)
                inner[a, b, j, 2 - a : 6 - a, low : high + 1] = 1
        for i in range(IR):
            side[a, i, 4 * i + 2 - a : 4 * i + 6 - a] = 1
    return inner.reshape(TAPS * IC, 6 * TC), side.reshape(3 * IR, SIDE)


def dcoarse_kernel(oc, rows, left, right, inner, side, wconv, out, pooled):
    pool = inner[...]
    for i in range(IR):
        if i == 0:
            block = jnp.concatenate([rows[0], oc[: 5 * TC, :]], axis=0)
        elif i == IR - 1:
            block = jnp.concatenate([oc[(4 * i - 1) * TC :, :], rows[1]], axis=0)
        else:
            block = oc[(4 * i - 1) * TC : (4 * i + 5) * TC, :]
        part = dot(pool, block)
        for t in range(TAPS):
            for h in range(2):
                pooled[t, h, i * IC : (i + 1) * IC, :] = part[t * IC : (t + 1) * IC, h * 128 : (h + 1) * 128]
    for edge, b, start in ((left, 2, 0), (right, 0, IC - 1)):
        part = dot(side[...], edge[...].astype(BF))
        for a in range(3):
            for h in range(2):
                cells = pl.ds(start, IR, stride=IC)
                pooled[3 * a + b, h, cells, :] += part[a * IR : (a + 1) * IR, h * 128 : (h + 1) * 128]
    total = jnp.zeros((CELLS, CF), F32)
    for t in range(TAPS):
        s = jnp.concatenate([pooled[t, 0], pooled[t, 1]], axis=-1).astype(BF)
        total += dot(s, wconv[t], ((1,), (1,)))
    out[...] = total.astype(BF)


def dcoarse_pass(oc, rows, left, right, wconv):
    inner, side = pool_matrices()
    vm = pl.BlockSpec(memory_space=pltpu.VMEM)
    return pl.pallas_call(
        dcoarse_kernel,
        in_specs=[vm] * 7,
        out_specs=vm,
        out_shape=jax.ShapeDtypeStruct((CELLS, CF), BF),
        scratch_shapes=[pltpu.VMEM((TAPS, 2, CELLS, 128), F32)],
        compiler_params=params(20, 0),
        cost_estimate=cost(600_000_000, 4_000_000),
        name="coarse_cotangent",
    )(oc.reshape(TR * TC, CF), rows, left, right, jnp.asarray(inner, BF), jnp.asarray(side, BF), wconv)


def coarse_kernel(core, x, haar, wband, wpoint, wproj, sub, pre, hidden, cout, split, outs):
    k = pl.program_id(0)
    h = haar[pl.ds(pl.multiple_of(k * 64, 64), 64), :]
    part = jnp.concatenate([dot(h, x[:256, :]), dot(h, x[256:, :])], axis=0).astype(BF)
    sub[pl.ds(pl.multiple_of(k * 128, 128), 128), :] = part
    m = dot(part, wband[0])
    hi = m.astype(BF)
    lo = (m - hi.astype(F32)).astype(BF)
    rows = pl.ds(pl.multiple_of(k * 64, 64), 64)
    for g in range(2):
        split[g, 0, rows, :] = hi[g * 64 : (g + 1) * 64]
        split[g, 1, rows, :] = lo[g * 64 : (g + 1) * 64]

    @pl.when(k == BANDS - 1)
    def _():
        h = haar[...]
        for g in range(2):
            cells = slice(g * 256, (g + 1) * 256)
            value = dot(h, split[g, 0], ((0,), (0,))) + dot(h, split[g, 1], ((0,), (0,)))
            value = value + dot(x[cells, :], wpoint[...])
            pre[cells, :] = value
            act = 0.5 * value * (1.0 + jnp.tanh(GELU_A * (value + GELU_B * (value * value * value))))
            act = act.astype(BF)
            hidden[cells, :] = act
            outs[g * 16 : (g + 1) * 16] = dot(act, wproj[...]).reshape(16, 16, CF)
        own = outs[:, pl.ds(pl.multiple_of(core[0] * IC, IC), IC), :]
        cout[...] = own.reshape(CELLS, CF).astype(BF)


def coarse_pass(core, x, haar, wband, wpoint, wproj):
    return pl.pallas_call(
        coarse_kernel,
        grid=(BANDS,),
        in_specs=[
            pl.BlockSpec(memory_space=pltpu.SMEM),
            whole(PAIR, C),
            whole(256, 256),
            pl.BlockSpec((1, C, C), lambda i: (i, 0, 0)),
            whole(C, C),
            whole(C, CF),
        ],
        out_specs=[whole(PAIR, C), whole(PAIR, C), whole(PAIR, C), whole(CELLS, CF)],
        out_shape=[
            jax.ShapeDtypeStruct((PAIR, C), BF),
            jax.ShapeDtypeStruct((PAIR, C), F32),
            jax.ShapeDtypeStruct((PAIR, C), BF),
            jax.ShapeDtypeStruct((CELLS, CF), BF),
        ],
        scratch_shapes=[pltpu.VMEM((2, 2, 256, C), BF), pltpu.VMEM((IR, 2 * IC, CF), F32)],
        compiler_params=params(24),
        cost_estimate=cost(1_000_000_000, 6_000_000),
        name="coarse_forward",
    )(core, x, haar, wband, wpoint, wproj)


def grads_kernel(core, x, haar, wproj, sub, pre, hidden, dco, dtwin, out, both):
    own = pl.multiple_of(core[0] * IC, IC)
    both[:, pl.ds(own, IC), :] = dco[...].astype(F32).reshape(IR, IC, CF)
    both[:, pl.ds(IC - own, IC), :] = dtwin[...].astype(F32).reshape(IR, IC, CF)
    d = both[...].reshape(PAIR, CF).astype(BF)
    value = pre[...]
    square = value * value
    th = jnp.tanh(GELU_A * (value + GELU_B * (value * square)))
    slope = 0.5 * (1.0 + th) + 0.5 * value * (1.0 - th * th) * (GELU_A * (1.0 + 3.0 * GELU_B * square))
    dpre = (dot(d, wproj[...], ((1,), (1,))) * slope).astype(BF)
    h = haar[...]
    dmix = [dot(h, dpre[g * 256 : (g + 1) * 256]).astype(BF) for g in range(2)]
    half = pl.ds(pl.multiple_of(core[0] * 256, 256), 256)
    for k in range(5):
        if k < BANDS:
            dk = jnp.concatenate([dmix[g][k * 64 : (k + 1) * 64] for g in range(2)], axis=0)
            grad = dot(sub[k * 128 : (k + 1) * 128, half], dk, ((0,), (0,)))
        else:
            grad = dot(x[:, half], dpre, ((0,), (0,)))
        for n in range(4):
            at = (4 * k + n) * 256
            out[at : at + 256, :] = grad[:, n * 128 : (n + 1) * 128].astype(BF)
    grad = dot(hidden[:, half], d, ((0,), (0,)))
    for n in range(2):
        at = (20 + n) * 256
        out[at : at + 256, :] = grad[:, n * 128 : (n + 1) * 128].astype(BF)


def grads_pass(core, x, haar, wproj, sub, pre, hidden, dco, dtwin):
    vm = pl.BlockSpec(memory_space=pltpu.VMEM)
    return pl.pallas_call(
        grads_kernel,
        in_specs=[pl.BlockSpec(memory_space=pltpu.SMEM)] + [vm] * 8,
        out_specs=vm,
        out_shape=jax.ShapeDtypeStruct((EARLY, 128), BF),
        scratch_shapes=[pltpu.VMEM((IR, 2 * IC, CF), F32)],
        compiler_params=params(24, 0),
        cost_estimate=cost(1_000_000_000, 6_000_000),
        name="coarse_gradients",
    )(core, x, haar, wproj, sub, pre, hidden, dco, dtwin)


def fill_windows(i, tile, rows, left, right, win):
    r0 = i * HB
    win[1 : HB + 1, 8 : 8 + TC, :] = tile[pl.ds(r0, HB)].astype(F32)
    before = tile[pl.ds(jnp.maximum(r0 - 1, 0), 1)].astype(F32)
    after = tile[pl.ds(jnp.minimum(r0 + HB, TR - 1), 1)].astype(F32)
    win[0:1, 8 : 8 + TC, :] = jnp.where(i == 0, rows[0:1].astype(F32), before)
    win[HB + 1 : HB + 2, 8 : 8 + TC, :] = jnp.where(i == NB - 1, rows[1:2].astype(F32), after)
    for r in range(HB + 2):
        win[r, 7:8, :] = left[pl.ds(r0 + r, 1), :]
        win[r, 8 + TC : 9 + TC, :] = right[pl.ds(r0 + r, 1), :]


def wgrad_kernel(core, fine, cout, oc, rows, left, right, conv_in, keep, send, up, win, shifted, acc):
    i = pl.program_id(0)
    for q in range(HB // 4):
        cell = cout[q * IC : (q + 1) * IC, :].astype(F32)
        for s in range(4):
            up[q, 0, pl.ds(s, IC, stride=4), :] = cell[:, :128]
            up[q, 1, pl.ds(s, IC, stride=4), :] = cell[:, 128:]
        grown = jnp.concatenate([up[q, 0], up[q, 1]], axis=-1)
        for t in range(4):
            conv_in[4 * q + t] = (fine[4 * q + t].astype(F32) + grown).astype(BF)
    fill_windows(i, oc, rows, left, right, win)
    for b in range(3):
        shifted[:, :, b * CF : (b + 1) * CF] = win[:, 9 - b : 9 - b + TC, :].astype(BF)

    @pl.when(i == 0)
    def _():
        acc[...] = jnp.zeros_like(acc)

    cells = conv_in[...].reshape(HB * TC, CF).T
    for a in range(3):
        acc[a] += dot(cells, shifted[2 - a : 2 - a + HB].reshape(HB * TC, 3 * CF))

    @pl.when(i == NB - 1)
    def _():
        for out, c in ((keep, core[0]), (send, 1 - core[0])):
            half = pl.ds(pl.multiple_of(c * 128, 128), 128)
            for t in range(TAPS):
                for n in range(2):
                    at = (t % 3) * CF + n * 128
                    out[(2 * t + n) * 128 : (2 * t + n + 1) * 128, :] = acc[t // 3, half, at : at + 128].astype(BF)


def wgrad_pass(core, fine, cout, oc, rows, left, right):
    return pl.pallas_call(
        wgrad_kernel,
        grid=(NB,),
        in_specs=[
            pl.BlockSpec(memory_space=pltpu.SMEM),
            pl.BlockSpec((HB, TC, CF), lambda i: (i, 0, 0)),
            pl.BlockSpec((HB // 4 * IC, CF), lambda i: (i, 0)),
            whole(TR, TC, CF),
            whole(2, TC, CF),
            whole(SIDE, CF),
            whole(SIDE, CF),
        ],
        out_specs=[
            pl.BlockSpec((HB, TC, CF), lambda i: (i, 0, 0)),
            whole(LATE, 128),
            whole(LATE, 128),
        ],
        out_shape=[
            jax.ShapeDtypeStruct((TR, TC, CF), BF),
            jax.ShapeDtypeStruct((LATE, 128), BF),
            jax.ShapeDtypeStruct((LATE, 128), BF),
        ],
        scratch_shapes=[
            pltpu.VMEM((HB // 4, 2, TC, 128), F32),
            pltpu.VMEM((HB + 2, 48, CF), F32),
            pltpu.VMEM((HB + 2, TC, 3 * CF), BF),
            pltpu.VMEM((3, CF, 3 * CF), F32),
        ],
        compiler_params=params(32),
        cost_estimate=cost(8_000_000_000, 9_000_000),
        name="conv_weight_gradient",
    )(core, fine, cout, oc, rows, left, right)


def conv_kernel(ci, rows, left, right, wconv, out, win, wide):
    i = pl.program_id(0)
    fill_windows(i, ci, rows, left, right, win)
    for b in range(3):
        wide[:, :, b * CF : (b + 1) * CF] = win[:, 7 + b : 7 + b + TC, :].astype(BF)
    total = jnp.zeros((HB * TC, CF), F32)
    for a in range(3):
        total += dot(wide[a : a + HB].reshape(HB * TC, 3 * CF), wconv[a])
    out[...] = total.astype(BF).reshape(HB, TC, CF)


def conv_pass(ci, rows, left, right, wconv):
    return pl.pallas_call(
        conv_kernel,
        grid=(NB,),
        in_specs=[
            whole(TR, TC, CF),
            whole(2, TC, CF),
            whole(SIDE, CF),
            whole(SIDE, CF),
            whole(3, 3 * CF, CF),
        ],
        out_specs=pl.BlockSpec((HB, TC, CF), lambda i: (i, 0, 0)),
        out_shape=jax.ShapeDtypeStruct((TR, TC, CF), BF),
        scratch_shapes=[pltpu.VMEM((HB + 2, 48, CF), F32), pltpu.VMEM((HB + 2, TC, 3 * CF), BF)],
        compiler_params=params(32),
        cost_estimate=cost(8_000_000_000, 6_000_000),
        name="conv_forward",
    )(ci, rows, left, right, wconv.reshape(3, 3 * CF, CF))


def small_call(kernel, name, outs, *args):
    vm = pl.BlockSpec(memory_space=pltpu.VMEM)
    return pl.pallas_call(
        kernel,
        in_specs=[pl.BlockSpec(memory_space=pltpu.SMEM)] + [vm] * (len(args) - 1),
        out_specs=[vm] * len(outs),
        out_shape=[jax.ShapeDtypeStruct(s, BF) for s in outs],
        compiler_params=params(16, 0),
        name=name,
    )(*args)


def deal_kernel(at, *refs):
    ins, outs = refs[:-4], refs[-4:]
    n = outs[0].shape[0]
    for d in range(4):
        rows = pl.ds(pl.multiple_of(lax.rem(at[0] + d, 4) * n, n), n)
        total = ins[0][rows, :].astype(F32)
        for r in ins[1:]:
            total = total + r[rows, :].astype(F32)
        outs[d][...] = total.astype(BF)


def deal(at, *ins):
    n = ins[0].shape[0] // 4
    return small_call(deal_kernel, "sum_and_deal", [(n, 128)] * 4, at, *ins)


def add_kernel(at, *refs):
    total = refs[0][...].astype(F32)
    for r in refs[1:-1]:
        total = total + r[...].astype(F32)
    refs[-1][...] = total.astype(BF)


def add(at, *ins):
    return small_call(add_kernel, "sum_parts", [ins[0].shape], at, *ins)[0]


def ordered_sum_kernel(at, own, r1, r2, r3, out, slots):
    for d, r in enumerate((own, r1, r2, r3)):
        slots[lax.rem(at[0] + 4 - d, 4)] = r[...].astype(F32)
    out[...] = (((slots[0] + slots[1]) + (slots[2] + slots[3])) * SCALE).astype(BF)


def ordered_sum(at, *ins):
    vm = pl.BlockSpec(memory_space=pltpu.VMEM)
    shape = ins[0].shape
    return pl.pallas_call(
        ordered_sum_kernel,
        in_specs=[pl.BlockSpec(memory_space=pltpu.SMEM)] + [vm] * 4,
        out_specs=vm,
        out_shape=jax.ShapeDtypeStruct(shape, BF),
        scratch_shapes=[pltpu.VMEM((4,) + shape, F32)],
        compiler_params=params(16, 0),
        name="ordered_sum",
    )(at, *ins)


def gather_kernel(at, own, r1, r2, r3, out):
    n = own.shape[0]
    for d, r in enumerate((own, r1, r2, r3)):
        rows = pl.ds(pl.multiple_of(lax.rem(at[0] + 4 - d, 4) * n, n), n)
        out[rows, :] = r[...]


def gather(at, *ins):
    n = ins[0].shape[0]
    return small_call(gather_kernel, "place_parts", [(4 * n, 128)], at, *ins)[0]


def ring(parts, axes):
    return [lax.ppermute(p, axes, [(i, (i + d + 1) % 4) for i in range(4)]) for d, p in enumerate(parts)]


def finish_kernel(core, mine, other, mine_late, other_late, conv, band, point, proj):
    own = core[0] == 0

    def place(out, n, a, b, start, cols):
        a, b = a[start : start + n, :], b[start : start + n, :]
        out[0:n, cols : cols + 128] = jnp.where(own, a, b).astype(F32)
        out[n : 2 * n, cols : cols + 128] = jnp.where(own, b, a).astype(F32)

    for k in range(5):
        for n in range(4):
            place(band.at[k] if k < BANDS else point, 256, mine, other, (4 * k + n) * 256, 128 * n)
    for n in range(2):
        place(proj, 256, mine, other, (20 + n) * 256, 128 * n)
    for t in range(TAPS):
        for n in range(2):
            place(conv.at[t], 128, mine_late, other_late, (2 * t + n) * 128, 128 * n)


def finish_pass(core, *ins):
    vm = pl.BlockSpec(memory_space=pltpu.VMEM)
    return pl.pallas_call(
        finish_kernel,
        in_specs=[pl.BlockSpec(memory_space=pltpu.SMEM)] + [vm] * 4,
        out_specs=[vm] * 4,
        out_shape=[
            jax.ShapeDtypeStruct((TAPS, CF, CF), F32),
            jax.ShapeDtypeStruct((BANDS, C, C), F32),
            jax.ShapeDtypeStruct((C, C), F32),
            jax.ShapeDtypeStruct((C, CF), F32),
        ],
        compiler_params=params(24, 0),
        name="place_gradients",
    )(core, *ins)


def neighbours(axes, count):
    forward = [(i, i + 1) for i in range(count - 1)]
    return forward, [(b, a) for a, b in forward]


def halo(tile, east_edge, west_edge):
    forward, backward = neighbours(COL, 16)
    west = lax.ppermute(east_edge, COL, forward)
    east = lax.ppermute(west_edge, COL, backward)
    forward, backward = neighbours(ROW, 8)
    low = jnp.concatenate([tile[TR - 1], west[TR - 1 :], east[TR - 1 :]], axis=0)
    high = jnp.concatenate([tile[0], west[:1], east[:1]], axis=0)
    above = lax.ppermute(low, ROW, forward)
    below = lax.ppermute(high, ROW, backward)
    pad = jnp.zeros((SIDE - TR - 2, CF), BF)
    left = jnp.concatenate([above[TC : TC + 1], west, below[TC : TC + 1], pad], axis=0)
    right = jnp.concatenate([above[TC + 1 :], east, below[TC + 1 :], pad], axis=0)
    return jnp.stack([above[:TC], below[:TC]]), left.astype(F32), right.astype(F32)


def local(coarse_in, fine_in, band_weight, point_weight, proj_weight, conv_weight, out_cot):
    index = lambda axes: lax.axis_index(axes).astype(jnp.int32).reshape(1)
    core, at_y, at_z, at_x = index("c"), index("y"), index("z"), index(("xl", "xh"))
    swap = [(0, 1), (1, 0)]
    haar = jnp.asarray(haar_matrix(), BF)

    chunks = coarse_in.reshape(2, 8, 16, C).transpose(1, 0, 2, 3)
    chunks = jnp.broadcast_to(chunks[:, None], (8, 2, 2, 16, C)).reshape(16, 2, 16, C)
    x = lax.all_to_all(chunks, COL, 0, 0, tiled=True).reshape(PAIR, C)
    cot_halo = halo(out_cot, out_cot[:, TC - 1], out_cot[:, 0])
    sub, pre, hidden, cout = coarse_pass(core, x, haar, band_weight, point_weight, proj_weight)
    dco = dcoarse_pass(out_cot, *cot_halo, conv_weight)
    dtwin = lax.ppermute(dco, "c", swap)
    early = grads_pass(core, x, haar, proj_weight, sub, pre, hidden, dco, dtwin)

    parts = lax.all_to_all(early, CHIPS, 0, 0, tiled=True)
    conv_in, keep, send = wgrad_pass(core, fine_in, cout, out_cot, *cot_halo)
    got = lax.ppermute(send, "c", swap)
    own, *away = deal(at_y, keep, got)
    own, *away = deal(at_z, own, *ring(away, "y"))
    own = add(at_z, own, *ring(away, "z"))
    own = ordered_sum(at_x, own, *ring([own] * 3, ("xl", "xh")))

    parts = parts.reshape(PEERS, EARLY // PEERS, 128)
    done = (jnp.sum(parts.astype(F32), axis=0) * SCALE).astype(BF)
    spread = jnp.broadcast_to(done[None], (PEERS, EARLY // PEERS, 128)).reshape(EARLY, 128)
    mine = lax.all_to_all(spread, CHIPS, 0, 0, tiled=True)

    own = gather(at_z, own, *ring([own] * 3, "z"))
    mine_late = gather(at_y, own, *ring([own] * 3, "y"))
    other_late = lax.ppermute(mine_late, "c", swap)
    other = lax.ppermute(mine, "c", swap)
    fine_out = conv_pass(conv_in, *halo(conv_in, conv_in[:, TC - 1], conv_in[:, 0]), conv_weight)
    grad_conv, grad_band, grad_point, grad_proj = finish_pass(core, mine, other, mine_late, other_late)
    return fine_out, grad_conv, grad_band, grad_point, grad_proj


def solution(mesh):
    fine_mesh = Mesh(
        np.asarray(mesh.devices).reshape([n for _, n in GRID]), tuple(name for name, _ in GRID)
    )
    fine = P(ROW, COL, None)
    in_specs = (P(ROW + COL, None, None), fine, P(), P(), P(), P(), fine)
    out_specs = (fine, P(), P(), P(), P())
    return jax.shard_map(local, mesh=fine_mesh, in_specs=in_specs, out_specs=out_specs, check_vma=False)
```

time: 181 us -> 172 us (0.950)
  starting transfers between devices: 39.8 us -> 92 us
  blocking collectives: 41 us -> 0 us
  Pallas kernels: 47.5 us -> 28.4 us
  other arithmetic: 10.4 us -> 2.71 us
  local copies, waits for them, and re-layouts: 9.92 us -> 16.8 us
    all_to_all x1 -> x0, blocking collectives: 41 us -> none  [local(): lax.all_to_all(chip, CHIPS, 0, 0, tiled=True)]
    ppermute x6 -> x22, starting transfers between devices: 12.1 us -> 43.8 us  [the longest x15 26.2 us: ring(): lax.ppermute(p, axes, [(i, (i + d + 1) % 4) for i in range(4)])]
    all_to_all x1 -> x2, starting transfers between devices: 8.45 us -> 28 us  [the longest x1 19.6 us: local(): parts = lax.all_to_all(early, CHIPS, 0, 0, tiled=True)]
    all_to_all x1, waiting for transfers between devices: 19.4 us -> 0.01 us  [local(): mine = lax.all_to_all(spread, CHIPS, 0, 0, tiled=True)]
    ppermute x6 -> x22, waiting for transfers between devices: 5.44 us -> 23.6 us  [the longest x15 15.6 us: ring(): lax.ppermute(p, axes, [(i, (i + d + 1) % 4) for i in range(4)])]
    pallas_call x2 -> x8, Pallas kernels: 13.3 us -> 5.43 us  [the longest x1 2.55 us: coarse_pass(): pl.pallas_call(coarse_kernel, grid=(BANDS,), in_specs=[pl.BlockSpec(memor...]
    pallas_call x1, Pallas kernels: 14.9 us -> 8.81 us  [wgrad_pass(): pl.pallas_call(wgrad_kernel, grid=(NB,), in_specs=[pl.BlockSpec(memory_sp...]
    ppermute x2, waiting for transfers between devices: 5.98 us -> 0.01 us  [halo(): below = lax.ppermute(high, ROW, backward)]
  transfers between devices with their start and end apart: 13 -> 30, of which waited for: 5 -> 15; matrix products, arithmetic and copies ran while one was open for 6% -> 4% of each run, Pallas kernels for 18% -> 12%
where the time goes in v2:
time: 172 us; the launch traced here: 171 us
  starting transfers between devices  92 us (53%)
  waiting for transfers between devices  29.6 us (17%)
  Pallas kernels  28.4 us (17%)
  local copies, waits for them, and re-layouts  16.8 us (10%)
  other arithmetic  2.71 us (2%)
    ppermute x15, starting transfers between devices, ring(): lax.ppermute(p, axes, [(i, (i + d + 1) % 4) for i in range(4)])  26.2 us
    all_to_all x1, starting transfers between devices, local(): parts = lax.all_to_all(early, CHIPS, 0, 0, tiled=True)  19.6 us
    ppermute x15, waiting for transfers between devices, ring(): lax.ppermute(p, axes, [(i, (i + d + 1) % 4) for i in range(4)])  15.6 us
    pallas_call x1, Pallas kernels, wgrad_pass(): pl.pallas_call(wgrad_kernel, grid=(NB,), in_specs=[pl.BlockSpec(memory_sp...  8.81 us
    all_to_all x1, starting transfers between devices, local(): x = lax.all_to_all(chunks, COL, 0, 0, tiled=True).reshape(PAIR, C)  8.45 us
    unnamed x46, local copies, waits for them, and re-layouts  8.33 us
    ppermute x2, starting transfers between devices, halo(): above = lax.ppermute(low, ROW, forward)  8.16 us
    ppermute x2, starting transfers between devices, halo(): west = lax.ppermute(east_edge, COL, forward)  7.92 us
  transfers between devices with their start and end apart: 30, of which 15 were waited for; matrix products, arithmetic and copies ran while one was open for 4% of the time, Pallas kernels for 12%

profile of v2, /device:TPU:1, one launch (start us, length us, event | category | flops | bytes accessed | tf_op | source)
XLA Modules:
  0.0 170.6 jit_solution(10725369103461417410)
XLA Ops:
  0.7 1.1 copy.15
  2.6 8.4 %all-to-all-start = ((bf16[16,2,16,512]{3,2,1,0:T(8,128)(2,1)}), bf16[16,2,16,512]{3,2,1,0:T(8,128)(2,1)S(1)}, u32[]{:S(2)}, u32[]{:S(2)}) async-start(bf16[16,2,16,512]{3,2,1,0:T(8,128)(2,1)} %bitcast.3), calls=%async_computation | async-start | bytes 1048576 | tf_op jit(solution)/shard_map/all_to_all | solution.py:464
  11.3 2.1 %collective-permute-start.1 = (bf16[128,256]{1,0:T(8,128)(2,1)S(1)}, bf16[128,256]{1,0:T(8,128)(2,1)S(1)}, u32[]{:S(2)}, u32[]{:S(2)}) collective-permute-start(bf16[128,256]{1,0:T(8,128)(2,1)S(1)} %bitcast.46), channel_id=1, source_target_pairs={{1,0},{2,1},{3,2},{4,3},{5,4},{6,5},{7,6},{8,7},{9,8},{10,9},{11,1... | collective-permute-start | bytes 196616 | tf_op jit(solution)/shard_map/ppermute | solution.py:444
  13.5 3.5 %collective-permute-start = (bf16[128,256]{1,0:T(8,128)(2,1)S(1)}, bf16[128,256]{1,0:T(8,128)(2,1)S(1)}, u32[]{:S(2)}, u32[]{:S(2)}) collective-permute-start(bf16[128,256]{1,0:T(8,128)(2,1)S(1)} %bitcast.47), channel_id=1, source_target_pairs={{0,1},{1,2},{2,3},{3,4},{4,5},{5,6},{6,7},{7,8},{8,9},{9,10},{10,1... | collective-permute-start | bytes 196616 | tf_op jit(solution)/shard_map/ppermute | solution.py:443
  17.2 1.1 collective-permute-done.1
  18.7 1.3 collective-permute-start.3
  20.0 4.2 %collective-permute-start.2 = (bf16[34,256]{1,0:T(8,128)(2,1)S(1)}, bf16[34,256]{1,0:T(8,128)(2,1)S(1)}, u32[]{:S(2)}, u32[]{:S(2)}) collective-permute-start(bf16[34,256]{1,0:T(8,128)(2,1)S(1)} %pad_maximum_fusion.2), channel_id=1, source_target_pairs={{0,16},{16,32},{32,48},{48,64},{64,80},{80,96},{96,112},{1,17},{17... | collective-permute-start | bytes 52232 | tf_op jit(solution)/shard_map/ppermute | solution.py:448
  25.3 1.1 coarse_cotangent.1.dco
  26.5 1.6 copy-done.11
  28.1 1.0 copy-done.14
  29.1 2.6 %coarse_forward.1 = (bf16[512,512]{1,0:T(8,128)(2,1)S(1)}, f32[512,512]{1,0:T(8,128)S(1)}, bf16[512,512]{1,0:T(8,128)(2,1)S(1)}, bf16[256,256]{1,0:T(8,128)(2,1)S(1)}) custom-call(s32[1]{0:T(128)} %bitcast.core, bf16[512,512]{1,0:T(8,128)(2,1)S(1)} %bitcast.42, bf16[256,256]{1,0:T(8,128)(2,1)S(1)} %copy-done.8, bf16[4,512,512]{2,1,0:T(8,128)(2,1)S(1)} %copy-done.11, ...), custom_call_target="tpu_custom_call" | custom-call | flops 1000000000 | bytes 6000000 | tf_op jit(solution)/shard_map/coarse_forward/pallas_call | solution.py:149
  31.7 3.5 %coarse_gradients.1 = bf16[5632,128]{1,0:T(8,128)(2,1)} custom-call(s32[1]{0:T(128)} %bitcast.core, bf16[512,512]{1,0:T(8,128)(2,1)S(1)} %bitcast.43, bf16[256,256]{1,0:T(8,128)(2,1)S(1)} %copy-done.8, bf16[512,256]{1,0:T(8,128)(2,1)S(1)} %copy-done.7, bf16[512,512]{1,0:T(8,128)(2,1)S(1)} %get-tuple-element.26.sub, f32[512,512]{1,0:T(8,128)S(1)} %get-tuple-element.27.pre, ...), custom_call_target="tpu_custom_call" | custom-call | flops 1000000000 | bytes 6000000 | tf_op jit(solution)/shard_map/coarse_gradients/pallas_call | solution.py:204
  35.2 19.6 %all-to-all-start.1 = ((bf16[64,88,128]{2,1,0:T(8,128)(2,1)}), bf16[64,88,128]{2,1,0:T(8,128)(2,1)}, u32[]{:S(2)}, u32[]{:S(2)}) async-start(bf16[64,88,128]{2,1,0:T(8,128)(2,1)} %bitcast.19), calls=%async_computation.1 | async-start | bytes 2883584 | tf_op jit(solution)/shard_map/all_to_all | solution.py:471
  54.9 1.6 copy-done.12
  56.4 8.8 %conv_weight_gradient.1 = (bf16[128,32,256]{2,1,0:T(8,128)(2,1)S(1)}, bf16[2304,128]{1,0:T(8,128)(2,1)S(1)}, bf16[2304,128]{1,0:T(8,128)(2,1)S(1)}) custom-call(s32[1]{0:T(128)} %bitcast.core, bf16[128,32,256]{2,1,0:T(8,128)(2,1)S(1)} %copy-done.12, bf16[256,256]{1,0:T(8,128)(2,1)S(1)} %copy-done.16, bf16[128,32,256]{2,1,0:T(8,128)(2,1)S(1)} %copy-done, ...), custom_call_target="tpu_custom_call" | custom-call | flops 8000000000 | bytes 9000000 | tf_op jit(solution)/shard_map/conv_weight_gradient/pallas_call | solution.py:261
  66.9 1.3 copy-done.1
  68.2 2.5 %copy.18 = bf16[128,32,256]{2,0,1:T(8,128)(2,1)} copy(bf16[128,32,256]{2,1,0:T(8,128)(2,1)S(1)} %get-tuple-element.25.ci) | data formatting | bytes 4194304 | tf_op jit(solution)/shard_map/conv_weight_gradient/pallas_call | solution.py:261
  70.7 5.1 %all-to-all-done.1 = bf16[64,88,128]{2,1,0:T(8,128)(2,1)} async-done(((bf16[64,88,128]{2,1,0:T(8,128)(2,1)}), bf16[64,88,128]{2,1,0:T(8,128)(2,1)}, u32[]{:S(2)}, u32[]{:S(2)}) %all-to-all-start.1) | async-done | bytes 1441824 | tf_op jit(solution)/shard_map/all_to_all | solution.py:471
  75.9 1.6 convert_reduce_fusion
  77.5 1.3 broadcast_in_dim.5
  78.8 6.5 %all-to-all-start.2 = ((bf16[64,88,128]{2,1,0:T(8,128)(2,1)}), bf16[64,88,128]{2,1,0:T(8,128)(2,1)S(1)}, u32[]{:S(2)}, u32[]{:S(2)}) async-start(bf16[64,88,128]{2,1,0:T(8,128)(2,1)} %broadcast_in_dim.5), calls=%async_computation.2 | async-start | bytes 2883584 | tf_op jit(solution)/shard_map/all_to_all | solution.py:482
  86.1 4.4 %collective-permute-start.4 = (bf16[128,256]{1,0:T(8,128)(2,1)S(1)}, bf16[128,256]{1,0:T(8,128)(2,1)S(1)}, u32[]{:S(2)}, u32[]{:S(2)}) collective-permute-start(bf16[128,256]{1,0:T(8,128)(2,1)S(1)} %get-tuple-element.45), channel_id=1, source_target_pairs={{0,1},{1,2},{2,3},{3,4},{4,5},{5,6},{6,7},{7,8},{8,9},{9,10},{10,1... | collective-permute-start | bytes 196616 | tf_op jit(solution)/shard_map/ppermute | solution.py:443
  90.6 2.4 %collective-permute-start.5 = (bf16[128,256]{1,0:T(8,128)(2,1)S(1)}, bf16[128,256]{1,0:T(8,128)(2,1)S(1)}, u32[]{:S(2)}, u32[]{:S(2)}) collective-permute-start(bf16[128,256]{1,0:T(8,128)(2,1)S(1)} %get-tuple-element.46), channel_id=1, source_target_pairs={{1,0},{2,1},{3,2},{4,3},{5,4},{6,5},{7,6},{8,7},{9,8},{10,9},{11,1... | collective-permute-start | bytes 196616 | tf_op jit(solution)/shard_map/ppermute | solution.py:444
  93.0 2.5 %collective-permute-done.4 = bf16[128,256]{1,0:T(8,128)(2,1)S(1)} collective-permute-done((bf16[128,256]{1,0:T(8,128)(2,1)S(1)}, bf16[128,256]{1,0:T(8,128)(2,1)S(1)}, u32[]{:S(2)}, u32[]{:S(2)}) %collective-permute-start.4) | collective-permute-done | bytes 65568 | tf_op jit(solution)/shard_map/ppermute | solution.py:443
  95.6 3.9 %collective-permute-done.5 = bf16[128,256]{1,0:T(8,128)(2,1)S(1)} collective-permute-done((bf16[128,256]{1,0:T(8,128)(2,1)S(1)}, bf16[128,256]{1,0:T(8,128)(2,1)S(1)}, u32[]{:S(2)}, u32[]{:S(2)}) %collective-permute-start.5) | collective-permute-done | bytes 65568 | tf_op jit(solution)/shard_map/ppermute | solution.py:444
  99.5 1.3 collective-permute-start.7
  100.9 4.0 %collective-permute-start.6 = (bf16[34,256]{1,0:T(8,128)(2,1)S(1)}, bf16[34,256]{1,0:T(8,128)(2,1)S(1)}, u32[]{:S(2)}, u32[]{:S(2)}) collective-permute-start(bf16[34,256]{1,0:T(8,128)(2,1)S(1)} %pad_maximum_fusion.4), channel_id=1, source_target_pairs={{0,16},{16,32},{32,48},{48,64},{64,80},{80,96},{96,112},{1,17},{17... | collective-permute-start | bytes 52232 | tf_op jit(solution)/shard_map/ppermute | solution.py:448
  104.9 1.1 copy-done.6
  106.1 1.3 collective-permute-start.11
  107.4 7.8 %collective-permute-start.12 = (bf16[576,128]{1,0:T(8,128)(2,1)S(1)}, bf16[576,128]{1,0:T(8,128)(2,1)S(1)}, u32[]{:S(2)}, u32[]{:S(2)}) collective-permute-start(bf16[576,128]{1,0:T(8,128)(2,1)S(1)} %get-tuple-element.33), channel_id=1, source_target_pairs={{0,4},{2,6},{4,0},{6,2},{1,5},{3,7},{5,1},{7,3},{8,12},{10,14},{12... | collective-permute-start | bytes 442376 | tf_op jit(solution)/shard_map/ppermute | solution.py:398
  115.2 1.3 collective-permute-done.11.refs_1_
  116.6 2.8 %collective-permute-done.12.refs_2_ = bf16[576,128]{1,0:T(8,128)(2,1)S(1)} collective-permute-done((bf16[576,128]{1,0:T(8,128)(2,1)S(1)}, bf16[576,128]{1,0:T(8,128)(2,1)S(1)}, u32[]{:S(2)}, u32[]{:S(2)}) %collective-permute-start.12) | collective-permute-done | bytes 147488 | tf_op jit(solution)/shard_map/ppermute | solution.py:398
  119.4 1.2 collective-permute-start.14
  120.6 4.9 %collective-permute-start.15 = (bf16[144,128]{1,0:T(8,128)(2,1)S(1)}, bf16[144,128]{1,0:T(8,128)(2,1)S(1)}, u32[]{:S(2)}, u32[]{:S(2)}) collective-permute-start(bf16[144,128]{1,0:T(8,128)(2,1)S(1)} %get-tuple-element.37), channel_id=1, source_target_pairs={{0,32},{16,48},{32,0},{48,16},{1,33},{17,49},{33,1},{49,17},{2,34}... | collective-permute-start | bytes 110600 | tf_op jit(solution)/shard_map/ppermute | solution.py:398
  126.0 1.2 collective-permute-done.15.refs_2_
  127.2 1.1 collective-permute-done.16.refs_3_
  128.9 1.8 %collective-permute-start.18 = (bf16[144,128]{1,0:T(8,128)(2,1)}, bf16[144,128]{1,0:T(8,128)(2,1)}, u32[]{:S(2)}, u32[]{:S(2)}) collective-permute-start(bf16[144,128]{1,0:T(8,128)(2,1)} %sum_parts.1.own), channel_id=1, source_target_pairs={{0,64},{8,72},{64,0},{72,8},{1,65},{9,73},{65,1},{73,9},{2,66},{10... | collective-permute-start | bytes 110600 | tf_op jit(solution)/shard_map/ppermute | solution.py:398
  130.7 2.5 %collective-permute-start.17 = (bf16[144,128]{1,0:T(8,128)(2,1)}, bf16[144,128]{1,0:T(8,128)(2,1)}, u32[]{:S(2)}, u32[]{:S(2)}) collective-permute-start(bf16[144,128]{1,0:T(8,128)(2,1)} %sum_parts.1.own), channel_id=1, source_target_pairs={{0,8},{8,64},{64,72},{72,0},{1,9},{9,65},{65,73},{73,1},{2,10},{10... | collective-permute-start | bytes 110600 | tf_op jit(solution)/shard_map/ppermute | solution.py:398
  133.2 2.9 %collective-permute-start.9 = (bf16[5632,128]{1,0:T(8,128)(2,1)S(1)}, bf16[5632,128]{1,0:T(8,128)(2,1)S(1)}, u32[]{:S(2)}, u32[]{:S(2)}) collective-permute-start(bf16[5632,128]{1,0:T(8,128)(2,1)S(1)} %bitcast.39), channel_id=1, source_target_pairs={{0,1},{1,0},{2,3},{3,2},{4,5},{5,4},{6,7},{7,6},{8,9},{9,8},{10,11... | collective-permute-start | bytes 4325384 | tf_op jit(solution)/shard_map/ppermute | solution.py:487
  138.0 3.3 %collective-permute-start.22 = (bf16[144,128]{1,0:T(8,128)(2,1)S(1)}, bf16[144,128]{1,0:T(8,128)(2,1)S(1)}, u32[]{:S(2)}, u32[]{:S(2)}) collective-permute-start(bf16[144,128]{1,0:T(8,128)(2,1)S(1)} %ordered_sum.1.own), channel_id=1, source_target_pairs={{0,48},{16,0},{32,16},{48,32},{1,49},{17,1},{33,17},{49,33},{2,50}... | collective-permute-start | bytes 110600 | tf_op jit(solution)/shard_map/ppermute | solution.py:398
  142.7 3.0 %collective-permute-done.21.r2 = bf16[144,128]{1,0:T(8,128)(2,1)S(1)} collective-permute-done((bf16[144,128]{1,0:T(8,128)(2,1)S(1)}, bf16[144,128]{1,0:T(8,128)(2,1)S(1)}, u32[]{:S(2)}, u32[]{:S(2)}) %collective-permute-start.21) | collective-permute-done | bytes 36896 | tf_op jit(solution)/shard_map/ppermute | solution.py:398
  145.7 2.1 %collective-permute-start.25 = (bf16[576,128]{1,0:T(8,128)(2,1)S(1)}, bf16[576,128]{1,0:T(8,128)(2,1)S(1)}, u32[]{:S(2)}, u32[]{:S(2)}) collective-permute-start(bf16[576,128]{1,0:T(8,128)(2,1)S(1)} %place_parts.2.own), channel_id=1, source_target_pairs={{0,6},{2,0},{4,2},{6,4},{1,7},{3,1},{5,3},{7,5},{8,14},{10,8},{12,... | collective-permute-start | bytes 442376 | tf_op jit(solution)/shard_map/ppermute | solution.py:398
  149.3 2.3 %collective-permute-done.25.r3 = bf16[576,128]{1,0:T(8,128)(2,1)S(1)} collective-permute-done((bf16[576,128]{1,0:T(8,128)(2,1)S(1)}, bf16[576,128]{1,0:T(8,128)(2,1)S(1)}, u32[]{:S(2)}, u32[]{:S(2)}) %collective-permute-start.25) | collective-permute-done | bytes 147488 | tf_op jit(solution)/shard_map/ppermute | solution.py:398
  151.5 1.9 %collective-permute-done.24.r2 = bf16[576,128]{1,0:T(8,128)(2,1)S(1)} collective-permute-done((bf16[576,128]{1,0:T(8,128)(2,1)S(1)}, bf16[576,128]{1,0:T(8,128)(2,1)S(1)}, u32[]{:S(2)}, u32[]{:S(2)}) %collective-permute-start.24) | collective-permute-done | bytes 147488 | tf_op jit(solution)/shard_map/ppermute | solution.py:398
  153.5 1.5 collective-permute-done.23.r1
  155.0 5.0 %collective-permute-start.26 = (bf16[2304,128]{1,0:T(8,128)(2,1)S(1)}, bf16[2304,128]{1,0:T(8,128)(2,1)S(1)}, u32[]{:S(2)}, u32[]{:S(2)}) collective-permute-start(bf16[2304,128]{1,0:T(8,128)(2,1)S(1)} %place_parts.3.mine_late), channel_id=1, source_target_pairs={{0,1},{1,0},{2,3},{3,2},{4,5},{5,4},{6,7},{7,6},{8,9},{9,8},{10,11... | collective-permute-start | bytes 1769480 | tf_op jit(solution)/shard_map/ppermute | solution.py:486
  160.0 6.7 %conv_forward.1 = bf16[128,32,256]{2,1,0:T(8,128)(2,1)} custom-call(bf16[128,32,256]{2,1,0:T(8,128)(2,1)S(1)} %copy-done.2, bf16[2,32,256]{2,1,0:T(8,128)(2,1)S(1)} %pad_maximum_fusion.1.rows, f32[136,256]{1,0:T(8,128)S(1)} %get-tuple-element.68.left, f32[136,256]{1,0:T(8,128)S(1)} %get-tuple-element.67.right, bf16[3,768,256]{2,1,0:T(8,128)(2,1)S(1)} %bitcast.44), custom_call_target="tpu_custom_call" | custom-call | flops 8000000000 | bytes 6000000 | tf_op jit(solution)/shard_map/conv_forward/pallas_call | solution.py:307
  166.7 3.9 %place_gradients.1 = (f32[9,256,256]{2,1,0:T(8,128)}, f32[4,512,512]{2,1,0:T(8,128)}, f32[512,512]{1,0:T(8,128)}, f32[512,256]{1,0:T(8,128)}) custom-call(s32[1]{0:T(128)} %bitcast.core, bf16[5632,128]{1,0:T(8,128)(2,1)S(1)} %bitcast.40, bf16[5632,128]{1,0:T(8,128)(2,1)S(1)} %collective-permute-done.9.other, bf16[2304,128]{1,0:T(8,128)(2,1)S(1)} %place_parts.3.mine_late, ...), custom_call_target="tpu_custom_call" | custom-call | tf_op jit(solution)/shard_map/place_gradients/pallas_call | solution.py:421
  (102 shorter events, 11.5 us)
Async XLA Ops:
  0.6 24.6 %copy-start.9 = (bf16[96,136]{1,0:T(8,128)(2,1)S(1)}, bf16[96,136]{1,0:T(8,128)(2,1)}, u32[]{:S(2)}) copy-start(bf16[96,136]{1,0:T(8,128)(2,1)} %constant.35.clone.side) | copy-start | bytes 78340
  0.6 24.6 %copy-start.10 = (bf16[72,192]{1,0:T(8,128)(2,1)S(1)}, bf16[72,192]{1,0:T(8,128)(2,1)}, u32[]{:S(2)}) copy-start(bf16[72,192]{1,0:T(8,128)(2,1)} %constant.34.clone.inner) | copy-start | bytes 82948
  0.7 10.4 %copy-start = (bf16[128,32,256]{2,1,0:T(8,128)(2,1)S(1)}, bf16[128,32,256]{2,1,0:T(8,128)(2,1)}, u32[]{:S(2)}) copy-start(bf16[128,32,256]{2,1,0:T(8,128)(2,1)} %oc.1) | copy-start | bytes 6291460
  2.6 23.8 %all-to-all-start = ((bf16[16,2,16,512]{3,2,1,0:T(8,128)(2,1)}), bf16[16,2,16,512]{3,2,1,0:T(8,128)(2,1)S(1)}, u32[]{:S(2)}, u32[]{:S(2)}) async-start(bf16[16,2,16,512]{3,2,1,0:T(8,128)(2,1)} %bitcast.3), calls=%async_computation | async-start | bytes 1048576 | tf_op jit(solution)/shard_map/all_to_all | solution.py:464
  11.1 14.2 %copy-start.3 = (bf16[9,256,256]{2,1,0:T(8,128)(2,1)S(1)}, bf16[9,256,256]{2,1,0:T(8,128)(2,1)}, u32[]{:S(2)}) copy-start(bf16[9,256,256]{2,1,0:T(8,128)(2,1)} %wconv.1) | copy-start | bytes 3538948
  11.3 7.0 %collective-permute-start.1 = (bf16[128,256]{1,0:T(8,128)(2,1)S(1)}, bf16[128,256]{1,0:T(8,128)(2,1)S(1)}, u32[]{:S(2)}, u32[]{:S(2)}) collective-permute-start(bf16[128,256]{1,0:T(8,128)(2,1)S(1)} %bitcast.46), channel_id=1, source_target_pairs={{1,0},{2,1},{3,2},{4,3},{5,4},{6,5},{7,6},{8,7},{9,8},{10,9},{11,1... | collective-permute-start | bytes 196616 | tf_op jit(solution)/shard_map/ppermute | solution.py:444
  13.5 5.2 %collective-permute-start = (bf16[128,256]{1,0:T(8,128)(2,1)S(1)}, bf16[128,256]{1,0:T(8,128)(2,1)S(1)}, u32[]{:S(2)}, u32[]{:S(2)}) collective-permute-start(bf16[128,256]{1,0:T(8,128)(2,1)S(1)} %bitcast.47), channel_id=1, source_target_pairs={{0,1},{1,2},{2,3},{3,4},{4,5},{5,6},{6,7},{7,8},{8,9},{9,10},{10,1... | collective-permute-start | bytes 196616 | tf_op jit(solution)/shard_map/ppermute | solution.py:443
  17.2 8.1 %copy-start.21 = (bf16[136]{0:T(256)(128)(2,1)}, bf16[136]{0:T(256)(128)(2,1)S(1)}, u32[]{:S(2)}) copy-start(bf16[136]{0:T(256)(128)(2,1)S(1)} %pad.23.clone) | copy-start | bytes 820
  18.7 5.5 %collective-permute-start.3 = (bf16[34,256]{1,0:T(8,128)(2,1)S(1)}, bf16[34,256]{1,0:T(8,128)(2,1)S(1)}, u32[]{:S(2)}, u32[]{:S(2)}) collective-permute-start(bf16[34,256]{1,0:T(8,128)(2,1)S(1)} %pad_maximum_fusion.3), channel_id=1, source_target_pairs={{16,0},{32,16},{48,32},{64,48},{80,64},{96,80},{112,96},{17,1},{33... | collective-permute-start | bytes 52232 | tf_op jit(solution)/shard_map/ppermute | solution.py:449
  20.0 5.1 %collective-permute-start.2 = (bf16[34,256]{1,0:T(8,128)(2,1)S(1)}, bf16[34,256]{1,0:T(8,128)(2,1)S(1)}, u32[]{:S(2)}, u32[]{:S(2)}) collective-permute-start(bf16[34,256]{1,0:T(8,128)(2,1)S(1)} %pad_maximum_fusion.2), channel_id=1, source_target_pairs={{0,16},{16,32},{32,48},{48,64},{64,80},{80,96},{96,112},{1,17},{17... | collective-permute-start | bytes 52232 | tf_op jit(solution)/shard_map/ppermute | solution.py:448
  25.1 1.4 copy-start.7
  25.1 1.4 copy-start.8
  26.4 5.3 %collective-permute-start.8 = (bf16[256,256]{1,0:T(8,128)(2,1)S(1)}, bf16[256,256]{1,0:T(8,128)(2,1)}, u32[]{:S(2)}, u32[]{:S(2)}) collective-permute-start(bf16[256,256]{1,0:T(8,128)(2,1)S(1)} %coarse_cotangent.1.dco), channel_id=1, source_target_pairs={{0,1},{1,0},{2,3},{3,2},{4,5},{5,4},{6,7},{7,6},{8,9},{9,8},{10,11... | collective-permute-start | bytes 393224 | tf_op jit(solution)/shard_map/ppermute | solution.py:468
  26.5 1.6 copy-start.11
  31.7 3.5 %copy-start.15 = (bf16[256,256]{1,0:T(8,128)(2,1)}, bf16[256,256]{1,0:T(8,128)(2,1)S(1)}, u32[]{:S(2)}) copy-start(bf16[256,256]{1,0:T(8,128)(2,1)S(1)} %get-tuple-element.24.cout) | copy-start | bytes 393220
  35.2 19.6 %copy-start.16 = (bf16[256,256]{1,0:T(8,128)(2,1)S(1)}, bf16[256,256]{1,0:T(8,128)(2,1)}, u32[]{:S(2)}) copy-start(bf16[256,256]{1,0:T(8,128)(2,1)} %copy-done.15) | copy-start | bytes 393220
  35.2 40.6 %all-to-all-start.1 = ((bf16[64,88,128]{2,1,0:T(8,128)(2,1)}), bf16[64,88,128]{2,1,0:T(8,128)(2,1)}, u32[]{:S(2)}, u32[]{:S(2)}) async-start(bf16[64,88,128]{2,1,0:T(8,128)(2,1)} %bitcast.19), calls=%async_computation.1 | async-start | bytes 2883584 | tf_op jit(solution)/shard_map/all_to_all | solution.py:471
  54.9 1.6 copy-start.12
  66.9 1.3 copy-start.1
  77.5 13.0 %copy-start.2 = (bf16[128,32,256]{2,1,0:T(8,128)(2,1)S(1)}, bf16[128,32,256]{2,1,0:T(8,128)(2,1)}, u32[]{:S(2)}) copy-start(bf16[128,32,256]{2,1,0:T(8,128)(2,1)} %copy-done.1) | copy-start | bytes 6291460
  78.8 54.4 %all-to-all-start.2 = ((bf16[64,88,128]{2,1,0:T(8,128)(2,1)}), bf16[64,88,128]{2,1,0:T(8,128)(2,1)S(1)}, u32[]{:S(2)}, u32[]{:S(2)}) async-start(bf16[64,88,128]{2,1,0:T(8,128)(2,1)} %broadcast_in_dim.5), calls=%async_computation.2 | async-start | bytes 2883584 | tf_op jit(solution)/shard_map/all_to_all | solution.py:482
  86.1 9.4 %collective-permute-start.4 = (bf16[128,256]{1,0:T(8,128)(2,1)S(1)}, bf16[128,256]{1,0:T(8,128)(2,1)S(1)}, u32[]{:S(2)}, u32[]{:S(2)}) collective-permute-start(bf16[128,256]{1,0:T(8,128)(2,1)S(1)} %get-tuple-element.45), channel_id=1, source_target_pairs={{0,1},{1,2},{2,3},{3,4},{4,5},{5,6},{6,7},{7,8},{8,9},{9,10},{10,1... | collective-permute-start | bytes 196616 | tf_op jit(solution)/shard_map/ppermute | solution.py:443
  90.5 14.3 %collective-permute-start.10 = (bf16[2304,128]{1,0:T(8,128)(2,1)}, bf16[2304,128]{1,0:T(8,128)(2,1)S(1)}, u32[]{:S(2)}, u32[]{:S(2)}) collective-permute-start(bf16[2304,128]{1,0:T(8,128)(2,1)} %copy-done.13), channel_id=1, source_target_pairs={{0,1},{1,0},{2,3},{3,2},{4,5},{5,4},{6,7},{7,6},{8,9},{9,8},{10,11... | collective-permute-start | bytes 1769480 | tf_op jit(solution)/shard_map/ppermute | solution.py:473
  90.6 8.9 %collective-permute-start.5 = (bf16[128,256]{1,0:T(8,128)(2,1)S(1)}, bf16[128,256]{1,0:T(8,128)(2,1)S(1)}, u32[]{:S(2)}, u32[]{:S(2)}) collective-permute-start(bf16[128,256]{1,0:T(8,128)(2,1)S(1)} %get-tuple-element.46), channel_id=1, source_target_pairs={{1,0},{2,1},{3,2},{4,3},{5,4},{6,5},{7,6},{8,7},{9,8},{10,9},{11,1... | collective-permute-start | bytes 196616 | tf_op jit(solution)/shard_map/ppermute | solution.py:444
  95.6 9.3 %copy-start.17 = (bf16[128,256]{1,0:T(8,128)(2,1)}, bf16[128,256]{1,0:T(8,128)(2,1)S(1)}, u32[]{:S(2)}) copy-start(bf16[128,256]{1,0:T(8,128)(2,1)S(1)} %collective-permute-done.4) | copy-start | bytes 196612
  99.5 5.4 %copy-start.18 = (bf16[128,256]{1,0:T(8,128)(2,1)}, bf16[128,256]{1,0:T(8,128)(2,1)S(1)}, u32[]{:S(2)}) copy-start(bf16[128,256]{1,0:T(8,128)(2,1)S(1)} %collective-permute-done.5) | copy-start | bytes 196612
  99.5 15.7 %collective-permute-start.7 = (bf16[34,256]{1,0:T(8,128)(2,1)S(1)}, bf16[34,256]{1,0:T(8,128)(2,1)S(1)}, u32[]{:S(2)}, u32[]{:S(2)}) collective-permute-start(bf16[34,256]{1,0:T(8,128)(2,1)S(1)} %pad_maximum_fusion.5), channel_id=1, source_target_pairs={{16,0},{32,16},{48,32},{64,48},{80,64},{96,80},{112,96},{17,1},{33... | collective-permute-start | bytes 52232 | tf_op jit(solution)/shard_map/ppermute | solution.py:449
  100.9 24.6 %collective-permute-start.6 = (bf16[34,256]{1,0:T(8,128)(2,1)S(1)}, bf16[34,256]{1,0:T(8,128)(2,1)S(1)}, u32[]{:S(2)}, u32[]{:S(2)}) collective-permute-start(bf16[34,256]{1,0:T(8,128)(2,1)S(1)} %pad_maximum_fusion.4), channel_id=1, source_target_pairs={{0,16},{16,32},{32,48},{48,64},{64,80},{80,96},{96,112},{1,17},{17... | collective-permute-start | bytes 52232 | tf_op jit(solution)/shard_map/ppermute | solution.py:448
  106.1 10.5 %collective-permute-start.11 = (bf16[576,128]{1,0:T(8,128)(2,1)S(1)}, bf16[576,128]{1,0:T(8,128)(2,1)S(1)}, u32[]{:S(2)}, u32[]{:S(2)}) collective-permute-start(bf16[576,128]{1,0:T(8,128)(2,1)S(1)} %get-tuple-element.32), channel_id=1, source_target_pairs={{0,2},{2,4},{4,6},{6,0},{1,3},{3,5},{5,7},{7,1},{8,10},{10,12},{12... | collective-permute-start | bytes 442376 | tf_op jit(solution)/shard_map/ppermute | solution.py:398
  107.4 11.9 %collective-permute-start.12 = (bf16[576,128]{1,0:T(8,128)(2,1)S(1)}, bf16[576,128]{1,0:T(8,128)(2,1)S(1)}, u32[]{:S(2)}, u32[]{:S(2)}) collective-permute-start(bf16[576,128]{1,0:T(8,128)(2,1)S(1)} %get-tuple-element.33), channel_id=1, source_target_pairs={{0,4},{2,6},{4,0},{6,2},{1,5},{3,7},{5,1},{7,3},{8,12},{10,14},{12... | collective-permute-start | bytes 442376 | tf_op jit(solution)/shard_map/ppermute | solution.py:398
  115.2 4.1 %collective-permute-start.13 = (bf16[576,128]{1,0:T(8,128)(2,1)S(1)}, bf16[576,128]{1,0:T(8,128)(2,1)S(1)}, u32[]{:S(2)}, u32[]{:S(2)}) collective-permute-start(bf16[576,128]{1,0:T(8,128)(2,1)S(1)} %get-tuple-element.34), channel_id=1, source_target_pairs={{0,6},{2,0},{4,2},{6,4},{1,7},{3,1},{5,3},{7,5},{8,14},{10,8},{12,... | collective-permute-start | bytes 442376 | tf_op jit(solution)/shard_map/ppermute | solution.py:398
  115.2 15.5 %copy-start.20 = (bf16[34,256]{1,0:T(8,128)(2,1)}, bf16[34,256]{1,0:T(8,128)(2,1)S(1)}, u32[]{:S(2)}) copy-start(bf16[34,256]{1,0:T(8,128)(2,1)S(1)} %collective-permute-done.7) | copy-start | bytes 52228
  119.4 6.6 %collective-permute-start.14 = (bf16[144,128]{1,0:T(8,128)(2,1)S(1)}, bf16[144,128]{1,0:T(8,128)(2,1)S(1)}, u32[]{:S(2)}, u32[]{:S(2)}) collective-permute-start(bf16[144,128]{1,0:T(8,128)(2,1)S(1)} %get-tuple-element.36), channel_id=1, source_target_pairs={{0,16},{16,32},{32,48},{48,0},{1,17},{17,33},{33,49},{49,1},{2,18}... | collective-permute-start | bytes 110600 | tf_op jit(solution)/shard_map/ppermute | solution.py:398
  120.6 6.6 %collective-permute-start.15 = (bf16[144,128]{1,0:T(8,128)(2,1)S(1)}, bf16[144,128]{1,0:T(8,128)(2,1)S(1)}, u32[]{:S(2)}, u32[]{:S(2)}) collective-permute-start(bf16[144,128]{1,0:T(8,128)(2,1)S(1)} %get-tuple-element.37), channel_id=1, source_target_pairs={{0,32},{16,48},{32,0},{48,16},{1,33},{17,49},{33,1},{49,17},{2,34}... | collective-permute-start | bytes 110600 | tf_op jit(solution)/shard_map/ppermute | solution.py:398
  125.5 2.8 %collective-permute-start.16 = (bf16[144,128]{1,0:T(8,128)(2,1)S(1)}, bf16[144,128]{1,0:T(8,128)(2,1)S(1)}, u32[]{:S(2)}, u32[]{:S(2)}) collective-permute-start(bf16[144,128]{1,0:T(8,128)(2,1)S(1)} %get-tuple-element.38), channel_id=1, source_target_pairs={{0,48},{16,0},{32,16},{48,32},{1,49},{17,1},{33,17},{49,33},{2,50}... | collective-permute-start | bytes 110600 | tf_op jit(solution)/shard_map/ppermute | solution.py:398
  125.5 5.2 %copy-start.19 = (bf16[34,256]{1,0:T(8,128)(2,1)}, bf16[34,256]{1,0:T(8,128)(2,1)S(1)}, u32[]{:S(2)}) copy-start(bf16[34,256]{1,0:T(8,128)(2,1)S(1)} %collective-permute-done.6) | copy-start | bytes 52228
  128.9 8.1 %collective-permute-start.19 = (bf16[144,128]{1,0:T(8,128)(2,1)}, bf16[144,128]{1,0:T(8,128)(2,1)}, u32[]{:S(2)}, u32[]{:S(2)}) collective-permute-start(bf16[144,128]{1,0:T(8,128)(2,1)} %sum_parts.1.own), channel_id=1, source_target_pairs={{0,72},{8,0},{64,8},{72,64},{1,73},{9,1},{65,9},{73,65},{2,74},{10... | collective-permute-start | bytes 110600 | tf_op jit(solution)/shard_map/ppermute | solution.py:398
  128.9 8.2 %collective-permute-start.18 = (bf16[144,128]{1,0:T(8,128)(2,1)}, bf16[144,128]{1,0:T(8,128)(2,1)}, u32[]{:S(2)}, u32[]{:S(2)}) collective-permute-start(bf16[144,128]{1,0:T(8,128)(2,1)} %sum_parts.1.own), channel_id=1, source_target_pairs={{0,64},{8,72},{64,0},{72,8},{1,65},{9,73},{65,1},{73,9},{2,66},{10... | collective-permute-start | bytes 110600 | tf_op jit(solution)/shard_map/ppermute | solution.py:398
  130.7 6.4 %collective-permute-start.17 = (bf16[144,128]{1,0:T(8,128)(2,1)}, bf16[144,128]{1,0:T(8,128)(2,1)}, u32[]{:S(2)}, u32[]{:S(2)}) collective-permute-start(bf16[144,128]{1,0:T(8,128)(2,1)} %sum_parts.1.own), channel_id=1, source_target_pairs={{0,8},{8,64},{64,72},{72,0},{1,9},{9,65},{65,73},{73,1},{2,10},{10... | collective-permute-start | bytes 110600 | tf_op jit(solution)/shard_map/ppermute | solution.py:398
  133.2 26.8 %copy-start.4 = (bf16[9,256,256]{2,1,0:T(8,128)(2,1)S(1)}, bf16[9,256,256]{2,1,0:T(8,128)(2,1)}, u32[]{:S(2)}) copy-start(bf16[9,256,256]{2,1,0:T(8,128)(2,1)} %wconv.1) | copy-start | bytes 3538948
  133.2 33.5 %collective-permute-start.9 = (bf16[5632,128]{1,0:T(8,128)(2,1)S(1)}, bf16[5632,128]{1,0:T(8,128)(2,1)S(1)}, u32[]{:S(2)}, u32[]{:S(2)}) collective-permute-start(bf16[5632,128]{1,0:T(8,128)(2,1)S(1)} %bitcast.39), channel_id=1, source_target_pairs={{0,1},{1,0},{2,3},{3,2},{4,5},{5,4},{6,7},{7,6},{8,9},{9,8},{10,11... | collective-permute-start | bytes 4325384 | tf_op jit(solution)/shard_map/ppermute | solution.py:487
  138.0 4.7 %collective-permute-start.22 = (bf16[144,128]{1,0:T(8,128)(2,1)S(1)}, bf16[144,128]{1,0:T(8,128)(2,1)S(1)}, u32[]{:S(2)}, u32[]{:S(2)}) collective-permute-start(bf16[144,128]{1,0:T(8,128)(2,1)S(1)} %ordered_sum.1.own), channel_id=1, source_target_pairs={{0,48},{16,0},{32,16},{48,32},{1,49},{17,1},{33,17},{49,33},{2,50}... | collective-permute-start | bytes 110600 | tf_op jit(solution)/shard_map/ppermute | solution.py:398
  141.3 4.4 %collective-permute-start.21 = (bf16[144,128]{1,0:T(8,128)(2,1)S(1)}, bf16[144,128]{1,0:T(8,128)(2,1)S(1)}, u32[]{:S(2)}, u32[]{:S(2)}) collective-permute-start(bf16[144,128]{1,0:T(8,128)(2,1)S(1)} %ordered_sum.1.own), channel_id=1, source_target_pairs={{0,32},{16,48},{32,0},{48,16},{1,33},{17,49},{33,1},{49,17},{2,34}... | collective-permute-start | bytes 110600 | tf_op jit(solution)/shard_map/ppermute | solution.py:398
  141.3 4.4 %collective-permute-start.20 = (bf16[144,128]{1,0:T(8,128)(2,1)S(1)}, bf16[144,128]{1,0:T(8,128)(2,1)S(1)}, u32[]{:S(2)}, u32[]{:S(2)}) collective-permute-start(bf16[144,128]{1,0:T(8,128)(2,1)S(1)} %ordered_sum.1.own), channel_id=1, source_target_pairs={{0,16},{16,32},{32,48},{48,0},{1,17},{17,33},{33,49},{49,1},{2,18}... | collective-permute-start | bytes 110600 | tf_op jit(solution)/shard_map/ppermute | solution.py:398
  145.7 5.8 %collective-permute-start.25 = (bf16[576,128]{1,0:T(8,128)(2,1)S(1)}, bf16[576,128]{1,0:T(8,128)(2,1)S(1)}, u32[]{:S(2)}, u32[]{:S(2)}) collective-permute-start(bf16[576,128]{1,0:T(8,128)(2,1)S(1)} %place_parts.2.own), channel_id=1, source_target_pairs={{0,6},{2,0},{4,2},{6,4},{1,7},{3,1},{5,3},{7,5},{8,14},{10,8},{12,... | collective-permute-start | bytes 442376 | tf_op jit(solution)/shard_map/ppermute | solution.py:398
  147.9 5.6 %collective-permute-start.24 = (bf16[576,128]{1,0:T(8,128)(2,1)S(1)}, bf16[576,128]{1,0:T(8,128)(2,1)S(1)}, u32[]{:S(2)}, u32[]{:S(2)}) collective-permute-start(bf16[576,128]{1,0:T(8,128)(2,1)S(1)} %place_parts.2.own), channel_id=1, source_target_pairs={{0,4},{2,6},{4,0},{6,2},{1,5},{3,7},{5,1},{7,3},{8,12},{10,14},{12... | collective-permute-start | bytes 442376 | tf_op jit(solution)/shard_map/ppermute | solution.py:398
  148.4 6.5 %collective-permute-start.23 = (bf16[576,128]{1,0:T(8,128)(2,1)S(1)}, bf16[576,128]{1,0:T(8,128)(2,1)S(1)}, u32[]{:S(2)}, u32[]{:S(2)}) collective-permute-start(bf16[576,128]{1,0:T(8,128)(2,1)S(1)} %place_parts.2.own), channel_id=1, source_target_pairs={{0,2},{2,4},{4,6},{6,0},{1,3},{3,5},{5,7},{7,1},{8,10},{10,12},{12... | collective-permute-start | bytes 442376 | tf_op jit(solution)/shard_map/ppermute | solution.py:398
  155.0 11.7 %collective-permute-start.26 = (bf16[2304,128]{1,0:T(8,128)(2,1)S(1)}, bf16[2304,128]{1,0:T(8,128)(2,1)S(1)}, u32[]{:S(2)}, u32[]{:S(2)}) collective-permute-start(bf16[2304,128]{1,0:T(8,128)(2,1)S(1)} %place_parts.3.mine_late), channel_id=1, source_target_pairs={{0,1},{1,0},{2,3},{3,2},{4,5},{5,4},{6,7},{7,6},{8,9},{9,8},{10,11... | collective-permute-start | bytes 1769480 | tf_op jit(solution)/shard_map/ppermute | solution.py:486
  (4 other events, 3.8 us)

commit v3 on v2

--- a/solution.py
+++ b/solution.py
@@ -24,8 +24,9 @@
 HB = 32
 NB = TR // HB
 SIDE = 136
+LATE = TAPS * 2 * 128 + 256
 EARLY = 5 * 4 * 256 + 2 * 256
-LATE = TAPS * 2 * 128
+PACK = LATE + EARLY
 PEERS = 64
 SCALE = float(1024 * 512) ** (-0.5)
 MIB = 1024 * 1024
@@ -191,11 +192,11 @@
         else:
             grad = dot(x[:, half], dpre, ((0,), (0,)))
         for n in range(4):
-            at = (4 * k + n) * 256
+            at = LATE + (4 * k + n) * 256
             out[at : at + 256, :] = grad[:, n * 128 : (n + 1) * 128].astype(BF)
     grad = dot(hidden[:, half], d, ((0,), (0,)))
     for n in range(2):
-        at = (20 + n) * 256
+        at = LATE + (20 + n) * 256
         out[at : at + 256, :] = grad[:, n * 128 : (n + 1) * 128].astype(BF)
 
 
@@ -205,7 +206,7 @@
         grads_kernel,
         in_specs=[pl.BlockSpec(memory_space=pltpu.SMEM)] + [vm] * 8,
         out_specs=vm,
-        out_shape=jax.ShapeDtypeStruct((EARLY, 128), BF),
+        out_shape=jax.ShapeDtypeStruct((PACK, 128), BF),
         scratch_shapes=[pltpu.VMEM((IR, 2 * IC, CF), F32)],
         compiler_params=params(24, 0),
         cost_estimate=cost(1_000_000_000, 6_000_000),
@@ -227,8 +228,9 @@
 
 def wgrad_kernel(core, fine, cout, oc, rows, left, right, conv_in, keep, send, up, win, shifted, acc):
     i = pl.program_id(0)
+    coarse = cout[...].astype(F32)
     for q in range(HB // 4):
-        cell = cout[q * IC : (q + 1) * IC, :].astype(F32)
+        cell = coarse[q * IC : (q + 1) * IC, :]
         for s in range(4):
             up[q, 0, pl.ds(s, IC, stride=4), :] = cell[:, :128]
             up[q, 1, pl.ds(s, IC, stride=4), :] = cell[:, 128:]
@@ -255,6 +257,7 @@
                 for n in range(2):
                     at = (t % 3) * CF + n * 128
                     out[(2 * t + n) * 128 : (2 * t + n + 1) * 128, :] = acc[t // 3, half, at : at + 128].astype(BF)
+            out[TAPS * 256 :, :] = jnp.zeros((LATE - TAPS * 256, 128), BF)
 
 
 def wgrad_pass(core, fine, cout, oc, rows, left, right):
@@ -323,114 +326,65 @@
     )(ci, rows, left, right, wconv.reshape(3, 3 * CF, CF))
 
 
-def small_call(kernel, name, outs, *args):
-    vm = pl.BlockSpec(memory_space=pltpu.VMEM)
-    return pl.pallas_call(
-        kernel,
-        in_specs=[pl.BlockSpec(memory_space=pltpu.SMEM)] + [vm] * (len(args) - 1),
-        out_specs=[vm] * len(outs),
-        out_shape=[jax.ShapeDtypeStruct(s, BF) for s in outs],
-        compiler_params=params(16, 0),
-        name=name,
-    )(*args)
-
-
-def deal_kernel(at, *refs):
-    ins, outs = refs[:-4], refs[-4:]
-    n = outs[0].shape[0]
-    for d in range(4):
-        rows = pl.ds(pl.multiple_of(lax.rem(at[0] + d, 4) * n, n), n)
-        total = ins[0][rows, :].astype(F32)
-        for r in ins[1:]:
-            total = total + r[rows, :].astype(F32)
-        outs[d][...] = total.astype(BF)
-
-
-def deal(at, *ins):
-    n = ins[0].shape[0] // 4
-    return small_call(deal_kernel, "sum_and_deal", [(n, 128)] * 4, at, *ins)
-
-
-def add_kernel(at, *refs):
-    total = refs[0][...].astype(F32)
-    for r in refs[1:-1]:
-        total = total + r[...].astype(F32)
-    refs[-1][...] = total.astype(BF)
-
-
-def add(at, *ins):
-    return small_call(add_kernel, "sum_parts", [ins[0].shape], at, *ins)[0]
-
-
-def ordered_sum_kernel(at, own, r1, r2, r3, out, slots):
-    for d, r in enumerate((own, r1, r2, r3)):
-        slots[lax.rem(at[0] + 4 - d, 4)] = r[...].astype(F32)
-    out[...] = (((slots[0] + slots[1]) + (slots[2] + slots[3])) * SCALE).astype(BF)
-
-
-def ordered_sum(at, *ins):
-    vm = pl.BlockSpec(memory_space=pltpu.VMEM)
-    shape = ins[0].shape
-    return pl.pallas_call(
-        ordered_sum_kernel,
-        in_specs=[pl.BlockSpec(memory_space=pltpu.SMEM)] + [vm] * 4,
-        out_specs=vm,
-        out_shape=jax.ShapeDtypeStruct(shape, BF),
-        scratch_shapes=[pltpu.VMEM((4,) + shape, F32)],
-        compiler_params=params(16, 0),
-        name="ordered_sum",
-    )(at, *ins)
-
-
-def gather_kernel(at, own, r1, r2, r3, out):
-    n = own.shape[0]
-    for d, r in enumerate((own, r1, r2, r3)):
-        rows = pl.ds(pl.multiple_of(lax.rem(at[0] + 4 - d, 4) * n, n), n)
-        out[rows, :] = r[...]
-
-
-def gather(at, *ins):
-    n = ins[0].shape[0]
-    return small_call(gather_kernel, "place_parts", [(4 * n, 128)], at, *ins)[0]
-
-
-def ring(parts, axes):
-    return [lax.ppermute(p, axes, [(i, (i + d + 1) % 4) for i in range(4)]) for d, p in enumerate(parts)]
-
-
-def finish_kernel(core, mine, other, mine_late, other_late, conv, band, point, proj):
-    own = core[0] == 0
-
-    def place(out, n, a, b, start, cols):
-        a, b = a[start : start + n, :], b[start : start + n, :]
-        out[0:n, cols : cols + 128] = jnp.where(own, a, b).astype(F32)
-        out[n : 2 * n, cols : cols + 128] = jnp.where(own, b, a).astype(F32)
-
+def add_late_kernel(keep, got, packed, out):
+    out[...] = (keep[...].astype(F32) + got[...].astype(F32)).astype(BF)
+
+
+def add_late(keep, got, packed):
+    return pl.pallas_call(
+        add_late_kernel,
+        grid=(1,),
+        in_specs=[whole(LATE, 128), whole(LATE, 128), pl.BlockSpec(memory_space=pl.ANY)],
+        out_specs=whole(LATE, 128),
+        out_shape=jax.ShapeDtypeStruct((PACK, 128), BF),
+        input_output_aliases={2: 0},
+        compiler_params=params(16),
+        name="late_core_sum",
+    )(keep, got, packed)
+
+
+def place_kernel(core, half, *refs):
+    conv, band, point, proj = refs[-4:]
+
+    def place(out, n, start, cols):
+        out[:, cols : cols + 128] = half[start : start + n, :].astype(F32)
+
+    for t in range(TAPS):
+        for n in range(2):
+            place(conv.at[t], 128, (2 * t + n) * 128, 128 * n)
     for k in range(5):
         for n in range(4):
-            place(band.at[k] if k < BANDS else point, 256, mine, other, (4 * k + n) * 256, 128 * n)
+            place(band.at[k] if k < BANDS else point, 256, LATE + (4 * k + n) * 256, 128 * n)
     for n in range(2):
-        place(proj, 256, mine, other, (20 + n) * 256, 128 * n)
-    for t in range(TAPS):
-        for n in range(2):
-            place(conv.at[t], 128, mine_late, other_late, (2 * t + n) * 128, 128 * n)
-
-
-def finish_pass(core, *ins):
-    vm = pl.BlockSpec(memory_space=pltpu.VMEM)
-    return pl.pallas_call(
-        finish_kernel,
-        in_specs=[pl.BlockSpec(memory_space=pltpu.SMEM)] + [vm] * 4,
-        out_specs=[vm] * 4,
+        place(proj, 256, LATE + (20 + n) * 256, 128 * n)
+
+
+def place_half(core, half, before=()):
+    any_ref = pl.BlockSpec(memory_space=pl.ANY)
+    return pl.pallas_call(
+        place_kernel,
+        grid_spec=pltpu.PrefetchScalarGridSpec(
+            num_scalar_prefetch=1,
+            grid=(1,),
+            in_specs=[pl.BlockSpec((PACK, 128), lambda i, c: (0, 0))] + [any_ref] * len(before),
+            out_specs=[
+                pl.BlockSpec((TAPS, 128, CF), lambda i, c: (0, c[0], 0)),
+                pl.BlockSpec((BANDS, 256, C), lambda i, c: (0, c[0], 0)),
+                pl.BlockSpec((256, C), lambda i, c: (c[0], 0)),
+                pl.BlockSpec((256, CF), lambda i, c: (c[0], 0)),
+            ],
+        ),
         out_shape=[
             jax.ShapeDtypeStruct((TAPS, CF, CF), F32),
             jax.ShapeDtypeStruct((BANDS, C, C), F32),
             jax.ShapeDtypeStruct((C, C), F32),
             jax.ShapeDtypeStruct((C, CF), F32),
         ],
-        compiler_params=params(24, 0),
+        input_output_aliases={2 + n: n for n in range(len(before))},
+        compiler_params=params(24),
+        cost_estimate=cost(0, 6_000_000),
         name="place_gradients",
-    )(core, *ins)
+    )(core, half, *before)
 
 
 def neighbours(axes, count):
@@ -454,39 +408,34 @@
 
 
 def local(coarse_in, fine_in, band_weight, point_weight, proj_weight, conv_weight, out_cot):
-    index = lambda axes: lax.axis_index(axes).astype(jnp.int32).reshape(1)
-    core, at_y, at_z, at_x = index("c"), index("y"), index("z"), index(("xl", "xh"))
+    core = lax.axis_index("c").astype(jnp.int32).reshape(1)
     swap = [(0, 1), (1, 0)]
     haar = jnp.asarray(haar_matrix(), BF)
 
     chunks = coarse_in.reshape(2, 8, 16, C).transpose(1, 0, 2, 3)
     chunks = jnp.broadcast_to(chunks[:, None], (8, 2, 2, 16, C)).reshape(16, 2, 16, C)
+    chunks, last, first = lax.optimization_barrier((chunks, out_cot[:, TC - 1], out_cot[:, 0]))
     x = lax.all_to_all(chunks, COL, 0, 0, tiled=True).reshape(PAIR, C)
-    cot_halo = halo(out_cot, out_cot[:, TC - 1], out_cot[:, 0])
+    cot_halo = halo(out_cot, last, first)
     sub, pre, hidden, cout = coarse_pass(core, x, haar, band_weight, point_weight, proj_weight)
     dco = dcoarse_pass(out_cot, *cot_halo, conv_weight)
     dtwin = lax.ppermute(dco, "c", swap)
-    early = grads_pass(core, x, haar, proj_weight, sub, pre, hidden, dco, dtwin)
-
-    parts = lax.all_to_all(early, CHIPS, 0, 0, tiled=True)
     conv_in, keep, send = wgrad_pass(core, fine_in, cout, out_cot, *cot_halo)
     got = lax.ppermute(send, "c", swap)
-    own, *away = deal(at_y, keep, got)
-    own, *away = deal(at_z, own, *ring(away, "y"))
-    own = add(at_z, own, *ring(away, "z"))
-    own = ordered_sum(at_x, own, *ring([own] * 3, ("xl", "xh")))
-
-    parts = parts.reshape(PEERS, EARLY // PEERS, 128)
+    packed = grads_pass(core, x, haar, proj_weight, sub, pre, hidden, dco, dtwin)
+    packed = add_late(keep, got, packed)
+
+    packed, conv_in = lax.optimization_barrier((packed, conv_in))
+    parts = lax.all_to_all(packed, CHIPS, 0, 0, tiled=True)
+    fine_out = conv_pass(conv_in, *halo(conv_in, conv_in[:, TC - 1], conv_in[:, 0]), conv_weight)
+    parts, fine_out = lax.optimization_barrier((parts, fine_out))
+    parts = parts.reshape(PEERS, PACK // PEERS, 128)
     done = (jnp.sum(parts.astype(F32), axis=0) * SCALE).astype(BF)
-    spread = jnp.broadcast_to(done[None], (PEERS, EARLY // PEERS, 128)).reshape(EARLY, 128)
+    spread = jnp.broadcast_to(done[None], (PEERS, PACK // PEERS, 128)).reshape(PACK, 128)
     mine = lax.all_to_all(spread, CHIPS, 0, 0, tiled=True)
-
-    own = gather(at_z, own, *ring([own] * 3, "z"))
-    mine_late = gather(at_y, own, *ring([own] * 3, "y"))
-    other_late = lax.ppermute(mine_late, "c", swap)
     other = lax.ppermute(mine, "c", swap)
-    fine_out = conv_pass(conv_in, *halo(conv_in, conv_in[:, TC - 1], conv_in[:, 0]), conv_weight)
-    grad_conv, grad_band, grad_point, grad_proj = finish_pass(core, mine, other, mine_late, other_late)
+    grads = place_half(core, mine)
+    grad_conv, grad_band, grad_point, grad_proj = place_half(1 - core, other, grads)
     return fine_out, grad_conv, grad_band, grad_point, grad_proj
 
 

time: 172 us -> 160 us (0.930)
  starting transfers between devices: 92 us -> 49.3 us
  blocking collectives: 0 us -> 39.1 us
  local copies, waits for them, and re-layouts: 16.8 us -> 7.94 us
  waiting for transfers between devices: 29.6 us -> 32.3 us
    all_to_all x0 -> x1, blocking collectives: none -> 39.1 us  [local(): mine = lax.all_to_all(spread, CHIPS, 0, 0, tiled=True)]
    ppermute x16 -> x0, starting transfers between devices: 31.2 us -> none  [the longest x15 26.2 us: ring(): lax.ppermute(p, axes, [(i, (i + d + 1) % 4) for i in range(4)])]
    ppermute x2, waiting for transfers between devices: 5.08 us -> 28 us  [halo(): east = lax.ppermute(west_edge, COL, backward)]
    ppermute x16 -> x0, waiting for transfers between devices: 15.6 us -> none  [the longest x15 15.6 us: ring(): lax.ppermute(p, axes, [(i, (i + d + 1) % 4) for i in range(4)])]
    all_to_all x2 -> x1, starting transfers between devices: 26.1 us -> 16.3 us  [local(): parts = lax.all_to_all(packed, CHIPS, 0, 0, tiled=True)]
    unnamed x46 -> x24, local copies, waits for them, and re-layouts: 8.33 us -> 2.69 us
    all_to_all x2 -> x1, waiting for transfers between devices: 5.13 us -> 0.01 us  [local(): parts = lax.all_to_all(packed, CHIPS, 0, 0, tiled=True)]
    ppermute x2, waiting for transfers between devices: 2.92 us -> 0.16 us  [halo(): west = lax.ppermute(east_edge, COL, forward)]
  transfers between devices with their start and end apart: 30 -> 13, of which waited for: 15 -> 7; matrix products, arithmetic and copies ran while one was open for 4% -> 0% of each run, Pallas kernels for 12% -> 8%
where the time goes in v3:
time: 160 us
  starting transfers between devices  49.3 us (31%)
  blocking collectives  39.1 us (24%)
  waiting for transfers between devices  32.3 us (20%)
  Pallas kernels  27.7 us (17%)
  local copies, waits for them, and re-layouts  7.94 us (5%)
  other arithmetic  2.16 us (1%)
    all_to_all x1, blocking collectives, local(): mine = lax.all_to_all(spread, CHIPS, 0, 0, tiled=True)  39.1 us
    ppermute x2, waiting for transfers between devices, halo(): east = lax.ppermute(west_edge, COL, backward)  28 us
    all_to_all x1, starting transfers between devices, local(): parts = lax.all_to_all(packed, CHIPS, 0, 0, tiled=True)  16.3 us
    pallas_call x1, Pallas kernels, wgrad_pass(): pl.pallas_call(wgrad_kernel, grid=(NB,), in_specs=[pl.BlockSpec(memory_sp...  8.79 us
    all_to_all x1, starting transfers between devices, local(): x = lax.all_to_all(chunks, COL, 0, 0, tiled=True).reshape(PAIR, C)  8.45 us
    ppermute x2, starting transfers between devices, halo(): above = lax.ppermute(low, ROW, forward)  8.16 us
    ppermute x2, starting transfers between devices, halo(): west = lax.ppermute(east_edge, COL, forward)  7.23 us
    pallas_call x1, Pallas kernels, conv_pass(): pl.pallas_call(conv_kernel, grid=(NB,), in_specs=[whole(TR, TC, CF), whol...  6.77 us
  transfers between devices with their start and end apart: 13, of which 7 were waited for; matrix products, arithmetic and copies ran while one was open for 0% of the time, Pallas kernels for 8%

profile of v3, /device:TPU:1, one launch (start us, length us, event | category | flops | bytes accessed | tf_op | source)
XLA Modules:
  0.0 159.6 jit_solution(17509776467566472279)
XLA Ops:
  0.6 0.0 copy-start.6
  0.6 0.0 copy-start
  0.7 1.1 copy.20
  1.8 1.4 fusion
  3.2 0.9 broadcast_in_dim.4
  4.1 8.4 %all-to-all-start = ((bf16[16,2,16,512]{3,2,1,0:T(8,128)(2,1)}), bf16[16,2,16,512]{3,2,1,0:T(8,128)(2,1)S(1)}, u32[]{:S(2)}, u32[]{:S(2)}) async-start(bf16[16,2,16,512]{3,2,1,0:T(8,128)(2,1)} %bitcast.43), calls=%async_computation | async-start | bytes 1048576 | tf_op jit(solution)/shard_map/all_to_all | solution.py:418
  12.5 3.5 %collective-permute-start = (bf16[128,256]{1,0:T(8,128)(2,1)S(1)}, bf16[128,256]{1,0:T(8,128)(2,1)S(1)}, u32[]{:S(2)}, u32[]{:S(2)}) collective-permute-start(bf16[128,256]{1,0:T(8,128)(2,1)S(1)} %get-tuple-element.29), channel_id=1, source_target_pairs={{0,1},{1,2},{2,3},{3,4},{4,5},{5,6},{6,7},{7,8},{8,9},{9,10},{10,1... | collective-permute-start | bytes 196616 | tf_op jit(solution)/shard_map/ppermute | solution.py:397
  16.1 1.9 %collective-permute-start.1 = (bf16[128,256]{1,0:T(8,128)(2,1)S(1)}, bf16[128,256]{1,0:T(8,128)(2,1)S(1)}, u32[]{:S(2)}, u32[]{:S(2)}) collective-permute-start(bf16[128,256]{1,0:T(8,128)(2,1)S(1)} %get-tuple-element.30), channel_id=1, source_target_pairs={{1,0},{2,1},{3,2},{4,3},{5,4},{6,5},{7,6},{8,7},{9,8},{10,9},{11,1... | collective-permute-start | bytes 196616 | tf_op jit(solution)/shard_map/ppermute | solution.py:398
  18.0 0.1 pad.23.clone
  18.1 0.2 collective-permute-done
  18.3 3.9 %collective-permute-done.1 = bf16[128,256]{1,0:T(8,128)(2,1)S(1)} collective-permute-done((bf16[128,256]{1,0:T(8,128)(2,1)S(1)}, bf16[128,256]{1,0:T(8,128)(2,1)S(1)}, u32[]{:S(2)}, u32[]{:S(2)}) %collective-permute-start.1) | collective-permute-done | bytes 65568 | tf_op jit(solution)/shard_map/ppermute | solution.py:398
  22.2 1.3 collective-permute-start.3
  23.5 4.2 %collective-permute-start.2 = (bf16[34,256]{1,0:T(8,128)(2,1)S(1)}, bf16[34,256]{1,0:T(8,128)(2,1)S(1)}, u32[]{:S(2)}, u32[]{:S(2)}) collective-permute-start(bf16[34,256]{1,0:T(8,128)(2,1)S(1)} %pad_maximum_fusion.2), channel_id=1, source_target_pairs={{0,16},{16,32},{32,48},{48,64},{64,80},{80,96},{96,112},{1,17},{17... | collective-permute-start | bytes 52232 | tf_op jit(solution)/shard_map/ppermute | solution.py:402
  27.8 0.9 collective-permute-done.2
  28.6 0.1 maximum_convert_fusion.1
  28.8 0.0 copy-start.9
  28.8 1.6 copy-done.9
  30.4 1.0 copy-done.11
  31.4 2.6 %coarse_forward.1 = (bf16[512,512]{1,0:T(8,128)(2,1)S(1)}, f32[512,512]{1,0:T(8,128)S(1)}, bf16[512,512]{1,0:T(8,128)(2,1)S(1)}, bf16[256,256]{1,0:T(8,128)(2,1)S(1)}) custom-call(s32[1]{0:T(128)} %bitcast.core, bf16[512,512]{1,0:T(8,128)(2,1)S(1)} %bitcast.40, bf16[256,256]{1,0:T(8,128)(2,1)S(1)} %copy-done.6, bf16[4,512,512]{2,1,0:T(8,128)(2,1)S(1)} %copy-done.9, ...), custom_call_target="tpu_custom_call" | custom-call | flops 1000000000 | bytes 6000000 | tf_op jit(solution)/shard_map/coarse_forward/pallas_call | solution.py:150
  34.0 0.0 copy-start.3
  34.0 0.0 copy-start.7
  34.0 0.0 copy-start.8
  34.0 8.8 %conv_weight_gradient.1 = (bf16[128,32,256]{2,1,0:T(8,128)(2,1)S(1)}, bf16[2560,128]{1,0:T(8,128)(2,1)S(1)}, bf16[2560,128]{1,0:T(8,128)(2,1)S(1)}) custom-call(s32[1]{0:T(128)} %bitcast.core, bf16[128,32,256]{2,1,0:T(8,128)(2,1)S(1)} %copy-done.10, bf16[256,256]{1,0:T(8,128)(2,1)S(1)} %get-tuple-element.28.cout, bf16[128,32,256]{2,1,0:T(8,128)(2,1)S(1)} %copy-done, ...), custom_call_target="tpu_custom_call" | custom-call | flops 8000000000 | bytes 9000000 | tf_op jit(solution)/shard_map/conv_weight_gradient/pallas_call | solution.py:264
  42.8 0.0 copy-start.1
  42.8 0.1 collective-permute-start.4
  42.9 1.1 coarse_cotangent.1.dco
  44.1 0.5 collective-permute-start.5
  44.6 1.0 collective-permute-done.5.dtwin
  45.6 2.8 %coarse_gradients.1.packed = bf16[8192,128]{1,0:T(8,128)(2,1)} custom-call(s32[1]{0:T(128)} %bitcast.core, bf16[512,512]{1,0:T(8,128)(2,1)S(1)} %bitcast.41, bf16[256,256]{1,0:T(8,128)(2,1)S(1)} %copy-done.6, bf16[512,256]{1,0:T(8,128)(2,1)S(1)} %copy-done.5, bf16[512,512]{1,0:T(8,128)(2,1)S(1)} %get-tuple-element.33.sub, ...), custom_call_target="tpu_custom_call" | custom-call | flops 1000000000 | bytes 6000000 | tf_op jit(solution)/shard_map/coarse_gradients/pallas_call | solution.py:205
  48.4 1.0 late_core_sum.1
  49.4 1.2 copy.23
  50.6 3.7 %collective-permute-start.6 = (bf16[128,256]{1,0:T(8,128)(2,1)S(1)}, bf16[128,256]{1,0:T(8,128)(2,1)S(1)}, u32[]{:S(2)}, u32[]{:S(2)}) collective-permute-start(bf16[128,256]{1,0:T(8,128)(2,1)S(1)} %get-tuple-element.51), channel_id=1, source_target_pairs={{0,1},{1,2},{2,3},{3,4},{4,5},{5,6},{6,7},{7,8},{8,9},{9,10},{10,1... | collective-permute-start | bytes 196616 | tf_op jit(solution)/shard_map/ppermute | solution.py:397
  54.3 0.0 copy-start.2
  54.4 16.3 %all-to-all-start.1 = ((bf16[64,128,128]{2,1,0:T(8,128)(2,1)}), bf16[64,128,128]{2,1,0:T(8,128)(2,1)}, u32[]{:S(2)}, u32[]{:S(2)}) async-start(bf16[64,128,128]{2,1,0:T(8,128)(2,1)} %bitcast.12), calls=%async_computation.1 | async-start | bytes 4194304 | tf_op jit(solution)/shard_map/all_to_all | solution.py:429
  70.6 1.9 %collective-permute-start.7 = (bf16[128,256]{1,0:T(8,128)(2,1)S(1)}, bf16[128,256]{1,0:T(8,128)(2,1)S(1)}, u32[]{:S(2)}, u32[]{:S(2)}) collective-permute-start(bf16[128,256]{1,0:T(8,128)(2,1)S(1)} %get-tuple-element.52), channel_id=1, source_target_pairs={{1,0},{2,1},{3,2},{4,3},{5,4},{6,5},{7,6},{8,7},{9,8},{10,9},{11,1... | collective-permute-start | bytes 196616 | tf_op jit(solution)/shard_map/ppermute | solution.py:398
  72.6 24.1 %collective-permute-done.7 = bf16[128,256]{1,0:T(8,128)(2,1)S(1)} collective-permute-done((bf16[128,256]{1,0:T(8,128)(2,1)S(1)}, bf16[128,256]{1,0:T(8,128)(2,1)S(1)}, u32[]{:S(2)}, u32[]{:S(2)}) %collective-permute-start.7) | collective-permute-done | bytes 65568 | tf_op jit(solution)/shard_map/ppermute | solution.py:398
  96.7 1.3 collective-permute-start.9
  98.0 4.0 %collective-permute-start.8 = (bf16[34,256]{1,0:T(8,128)(2,1)S(1)}, bf16[34,256]{1,0:T(8,128)(2,1)S(1)}, u32[]{:S(2)}, u32[]{:S(2)}) collective-permute-start(bf16[34,256]{1,0:T(8,128)(2,1)S(1)} %pad_maximum_fusion.4), channel_id=1, source_target_pairs={{0,16},{16,32},{32,48},{48,64},{64,80},{80,96},{96,112},{1,17},{17... | collective-permute-start | bytes 52232 | tf_op jit(solution)/shard_map/ppermute | solution.py:402
  102.0 0.9 collective-permute-done.8
  102.9 0.1 maximum_convert_fusion.3
  103.0 6.8 %conv_forward.1 = bf16[128,32,256]{2,1,0:T(8,128)(2,1)} custom-call(bf16[128,32,256]{2,1,0:T(8,128)(2,1)S(1)} %copy-done.2, bf16[2,32,256]{2,1,0:T(8,128)(2,1)S(1)} %pad_maximum_fusion.1.rows, f32[136,256]{1,0:T(8,128)S(1)} %get-tuple-element.74.left, f32[136,256]{1,0:T(8,128)S(1)} %get-tuple-element.73.right, bf16[3,768,256]{2,1,0:T(8,128)(2,1)S(1)} %bitcast.42), custom_call_target="tpu_custom_call" | custom-call | flops 8000000000 | bytes 6000000 | tf_op jit(solution)/shard_map/conv_forward/pallas_call | solution.py:310
  109.8 1.9 %convert_reduce_fusion = f32[128,128]{1,0:T(8,128)S(1)} fusion(bf16[64,128,128]{2,1,0:T(8,128)(2,1)} %bitcast.24), kind=kLoop, calls=%fused_computation | loop fusion | flops 2080768 | bytes 2162688 | tf_op jit(solution)/shard_map/reduce_sum | solution.py:433
  111.7 0.5 broadcast_in_dim.5
  112.2 39.1 %all_to_all.25 = bf16[64,128,128]{2,1,0:T(8,128)(2,1)S(1)} all-to-all(bf16[64,128,128]{2,1,0:T(8,128)(2,1)S(1)} %broadcast_in_dim.5), channel_id=1, replica_groups=mesh['xl'=2,'z'=4,'xh'=2,'y'=4,'c'=2] {'xl','z','xh','y'}, dimensions={0} | all-to-all | bytes 4194304 | tf_op jit(solution)/shard_map/all_to_all | solution.py:435
  151.3 2.2 %collective-permute-start.10 = (bf16[8192,128]{1,0:T(8,128)(2,1)S(1)}, bf16[8192,128]{1,0:T(8,128)(2,1)S(1)}, u32[]{:S(2)}, u32[]{:S(2)}) collective-permute-start(bf16[8192,128]{1,0:T(8,128)(2,1)S(1)} %bitcast.37), channel_id=1, source_target_pairs={{0,1},{1,0},{2,3},{3,2},{4,5},{5,4},{6,7},{7,6},{8,9},{9,8},{10,11... | collective-permute-start | bytes 6291464 | tf_op jit(solution)/shard_map/ppermute | solution.py:436
  153.5 2.4 %place_gradients.2 = (f32[9,256,256]{2,1,0:T(8,128)}, f32[4,512,512]{2,1,0:T(8,128)}, f32[512,512]{1,0:T(8,128)}, f32[512,256]{1,0:T(8,128)}) custom-call(s32[1]{0:T(128)} %bitcast.core, bf16[8192,128]{1,0:T(8,128)(2,1)S(1)} %bitcast.38), custom_call_target="tpu_custom_call" | custom-call | bytes 6000000 | tf_op jit(solution)/shard_map/place_gradients/pallas_call | solution.py:364
  155.8 1.4 collective-permute-done.10.half
  157.2 2.4 %place_gradients.3 = (f32[9,256,256]{2,1,0:T(8,128)}, f32[4,512,512]{2,1,0:T(8,128)}, f32[512,512]{1,0:T(8,128)}, f32[512,256]{1,0:T(8,128)}) custom-call(s32[1]{0:T(128)S(6)} %sub.3.core, bf16[8192,128]{1,0:T(8,128)(2,1)S(1)} %collective-permute-done.10.half, ...), custom_call_target="tpu_custom_call", output_to_operand_aliasing={{0}: (2, {}), {1}: (3, {}), {2}: (4, {}), {3}: (5, {})} | custom-call | bytes 6000000 | tf_op jit(solution)/shard_map/place_gradients/pallas_call | solution.py:364
  (44 shorter events, 0.2 us)
Async XLA Ops:
  0.6 28.1 %copy-start.6 = (bf16[256,256]{1,0:T(8,128)(2,1)S(1)}, bf16[256,256]{1,0:T(8,128)(2,1)}, u32[]{:S(2)}) copy-start(bf16[256,256]{1,0:T(8,128)(2,1)} %constant.18.clone.haar) | copy-start | bytes 393220
  0.6 17.4 %copy-start = (bf16[128,32,256]{2,1,0:T(8,128)(2,1)S(1)}, bf16[128,32,256]{2,1,0:T(8,128)(2,1)}, u32[]{:S(2)}) copy-start(bf16[128,32,256]{2,1,0:T(8,128)(2,1)} %oc.1) | copy-start | bytes 6291460
  0.7 28.1 %copy-start.5 = (bf16[512,256]{1,0:T(8,128)(2,1)S(1)}, bf16[512,256]{1,0:T(8,128)(2,1)}, u32[]{:S(2)}) copy-start(bf16[512,256]{1,0:T(8,128)(2,1)} %wproj.3) | copy-start | bytes 786436
  4.1 24.6 %all-to-all-start = ((bf16[16,2,16,512]{3,2,1,0:T(8,128)(2,1)}), bf16[16,2,16,512]{3,2,1,0:T(8,128)(2,1)S(1)}, u32[]{:S(2)}, u32[]{:S(2)}) async-start(bf16[16,2,16,512]{3,2,1,0:T(8,128)(2,1)} %bitcast.43), calls=%async_computation | async-start | bytes 1048576 | tf_op jit(solution)/shard_map/all_to_all | solution.py:418
  12.5 5.7 %collective-permute-start = (bf16[128,256]{1,0:T(8,128)(2,1)S(1)}, bf16[128,256]{1,0:T(8,128)(2,1)S(1)}, u32[]{:S(2)}, u32[]{:S(2)}) collective-permute-start(bf16[128,256]{1,0:T(8,128)(2,1)S(1)} %get-tuple-element.29), channel_id=1, source_target_pairs={{0,1},{1,2},{2,3},{3,4},{4,5},{5,6},{6,7},{7,8},{8,9},{9,10},{10,1... | collective-permute-start | bytes 196616 | tf_op jit(solution)/shard_map/ppermute | solution.py:397
  16.1 6.1 %collective-permute-start.1 = (bf16[128,256]{1,0:T(8,128)(2,1)S(1)}, bf16[128,256]{1,0:T(8,128)(2,1)S(1)}, u32[]{:S(2)}, u32[]{:S(2)}) collective-permute-start(bf16[128,256]{1,0:T(8,128)(2,1)S(1)} %get-tuple-element.30), channel_id=1, source_target_pairs={{1,0},{2,1},{3,2},{4,3},{5,4},{6,5},{7,6},{8,7},{9,8},{10,9},{11,1... | collective-permute-start | bytes 196616 | tf_op jit(solution)/shard_map/ppermute | solution.py:398
  22.2 5.5 %collective-permute-start.3 = (bf16[34,256]{1,0:T(8,128)(2,1)S(1)}, bf16[34,256]{1,0:T(8,128)(2,1)S(1)}, u32[]{:S(2)}, u32[]{:S(2)}) collective-permute-start(bf16[34,256]{1,0:T(8,128)(2,1)S(1)} %pad_maximum_fusion.3), channel_id=1, source_target_pairs={{16,0},{32,16},{48,32},{64,48},{80,64},{96,80},{112,96},{17,1},{33... | collective-permute-start | bytes 52232 | tf_op jit(solution)/shard_map/ppermute | solution.py:403
  23.5 5.1 %collective-permute-start.2 = (bf16[34,256]{1,0:T(8,128)(2,1)S(1)}, bf16[34,256]{1,0:T(8,128)(2,1)S(1)}, u32[]{:S(2)}, u32[]{:S(2)}) collective-permute-start(bf16[34,256]{1,0:T(8,128)(2,1)S(1)} %pad_maximum_fusion.2), channel_id=1, source_target_pairs={{0,16},{16,32},{32,48},{48,64},{64,80},{80,96},{96,112},{1,17},{17... | collective-permute-start | bytes 52232 | tf_op jit(solution)/shard_map/ppermute | solution.py:402
  28.8 1.6 copy-start.9
  30.4 1.0 copy-start.11
  31.4 2.6 %copy-start.10 = (bf16[128,32,256]{2,1,0:T(8,128)(2,1)S(1)}, bf16[128,32,256]{2,1,0:T(8,128)(2,1)}, u32[]{:S(2)}) copy-start(bf16[128,32,256]{2,1,0:T(8,128)(2,1)} %fine.1) | copy-start | bytes 6291460
  34.0 8.9 %copy-start.3 = (bf16[9,256,256]{2,1,0:T(8,128)(2,1)S(1)}, bf16[9,256,256]{2,1,0:T(8,128)(2,1)}, u32[]{:S(2)}) copy-start(bf16[9,256,256]{2,1,0:T(8,128)(2,1)} %wconv.1) | copy-start | bytes 3538948
  34.0 8.9 %copy-start.7 = (bf16[96,136]{1,0:T(8,128)(2,1)S(1)}, bf16[96,136]{1,0:T(8,128)(2,1)}, u32[]{:S(2)}) copy-start(bf16[96,136]{1,0:T(8,128)(2,1)} %constant.20.clone.side) | copy-start | bytes 78340
  34.0 8.9 %copy-start.8 = (bf16[72,192]{1,0:T(8,128)(2,1)S(1)}, bf16[72,192]{1,0:T(8,128)(2,1)}, u32[]{:S(2)}) copy-start(bf16[72,192]{1,0:T(8,128)(2,1)} %constant.19.clone.inner) | copy-start | bytes 82948
  42.8 11.5 %copy-start.1 = (bf16[128,32,256]{2,1,0:T(8,128)(2,1)}, bf16[128,32,256]{2,1,0:T(8,128)(2,1)S(1)}, u32[]{:S(2)}) copy-start(bf16[128,32,256]{2,1,0:T(8,128)(2,1)S(1)} %get-tuple-element.38.ci) | copy-start | bytes 6291460
  42.8 5.6 %collective-permute-start.4 = (bf16[2560,128]{1,0:T(8,128)(2,1)S(1)}, bf16[2560,128]{1,0:T(8,128)(2,1)S(1)}, u32[]{:S(2)}, u32[]{:S(2)}) collective-permute-start(bf16[2560,128]{1,0:T(8,128)(2,1)S(1)} %get-tuple-element.32), channel_id=1, source_target_pairs={{0,1},{1,0},{2,3},{3,2},{4,5},{5,4},{6,7},{7,6},{8,9},{9,8},{10,11... | collective-permute-start | bytes 1966088 | tf_op jit(solution)/shard_map/ppermute | solution.py:424
  44.1 1.5 collective-permute-start.5
  50.6 22.0 %collective-permute-start.6 = (bf16[128,256]{1,0:T(8,128)(2,1)S(1)}, bf16[128,256]{1,0:T(8,128)(2,1)S(1)}, u32[]{:S(2)}, u32[]{:S(2)}) collective-permute-start(bf16[128,256]{1,0:T(8,128)(2,1)S(1)} %get-tuple-element.51), channel_id=1, source_target_pairs={{0,1},{1,2},{2,3},{3,4},{4,5},{5,6},{6,7},{7,8},{8,9},{9,10},{10,1... | collective-permute-start | bytes 196616 | tf_op jit(solution)/shard_map/ppermute | solution.py:397
  54.3 48.7 %copy-start.2 = (bf16[128,32,256]{2,1,0:T(8,128)(2,1)S(1)}, bf16[128,32,256]{2,1,0:T(8,128)(2,1)}, u32[]{:S(2)}) copy-start(bf16[128,32,256]{2,1,0:T(8,128)(2,1)} %copy-done.1) | copy-start | bytes 6291460
  54.3 48.7 %copy-start.4 = (bf16[9,256,256]{2,1,0:T(8,128)(2,1)S(1)}, bf16[9,256,256]{2,1,0:T(8,128)(2,1)}, u32[]{:S(2)}) copy-start(bf16[9,256,256]{2,1,0:T(8,128)(2,1)} %wconv.1) | copy-start | bytes 3538948
  54.4 55.4 %all-to-all-start.1 = ((bf16[64,128,128]{2,1,0:T(8,128)(2,1)}), bf16[64,128,128]{2,1,0:T(8,128)(2,1)}, u32[]{:S(2)}, u32[]{:S(2)}) async-start(bf16[64,128,128]{2,1,0:T(8,128)(2,1)} %bitcast.12), calls=%async_computation.1 | async-start | bytes 4194304 | tf_op jit(solution)/shard_map/all_to_all | solution.py:429
  70.6 26.0 %collective-permute-start.7 = (bf16[128,256]{1,0:T(8,128)(2,1)S(1)}, bf16[128,256]{1,0:T(8,128)(2,1)S(1)}, u32[]{:S(2)}, u32[]{:S(2)}) collective-permute-start(bf16[128,256]{1,0:T(8,128)(2,1)S(1)} %get-tuple-element.52), channel_id=1, source_target_pairs={{1,0},{2,1},{3,2},{4,3},{5,4},{6,5},{7,6},{8,7},{9,8},{10,9},{11,1... | collective-permute-start | bytes 196616 | tf_op jit(solution)/shard_map/ppermute | solution.py:398
  96.7 5.3 %collective-permute-start.9 = (bf16[34,256]{1,0:T(8,128)(2,1)S(1)}, bf16[34,256]{1,0:T(8,128)(2,1)S(1)}, u32[]{:S(2)}, u32[]{:S(2)}) collective-permute-start(bf16[34,256]{1,0:T(8,128)(2,1)S(1)} %pad_maximum_fusion.5), channel_id=1, source_target_pairs={{16,0},{32,16},{48,32},{64,48},{80,64},{96,80},{112,96},{17,1},{33... | collective-permute-start | bytes 52232 | tf_op jit(solution)/shard_map/ppermute | solution.py:403
  98.0 4.9 %collective-permute-start.8 = (bf16[34,256]{1,0:T(8,128)(2,1)S(1)}, bf16[34,256]{1,0:T(8,128)(2,1)S(1)}, u32[]{:S(2)}, u32[]{:S(2)}) collective-permute-start(bf16[34,256]{1,0:T(8,128)(2,1)S(1)} %pad_maximum_fusion.4), channel_id=1, source_target_pairs={{0,16},{16,32},{32,48},{48,64},{64,80},{80,96},{96,112},{1,17},{17... | collective-permute-start | bytes 52232 | tf_op jit(solution)/shard_map/ppermute | solution.py:402
  151.3 6.0 %collective-permute-start.10 = (bf16[8192,128]{1,0:T(8,128)(2,1)S(1)}, bf16[8192,128]{1,0:T(8,128)(2,1)S(1)}, u32[]{:S(2)}, u32[]{:S(2)}) collective-permute-start(bf16[8192,128]{1,0:T(8,128)(2,1)S(1)} %bitcast.37), channel_id=1, source_target_pairs={{0,1},{1,0},{2,3},{3,2},{4,5},{5,4},{6,7},{7,6},{8,9},{9,8},{10,11... | collective-permute-start | bytes 6291464 | tf_op jit(solution)/shard_map/ppermute | solution.py:436

commit v4 on v3

--- a/solution.py
+++ b/solution.py
@@ -111,14 +111,24 @@
         out_specs=vm,
         out_shape=jax.ShapeDtypeStruct((CELLS, CF), BF),
         scratch_shapes=[pltpu.VMEM((TAPS, 2, CELLS, 128), F32)],
-        compiler_params=params(20, 0),
+        compiler_params=params(16, 0),
         cost_estimate=cost(600_000_000, 4_000_000),
         name="coarse_cotangent",
     )(oc.reshape(TR * TC, CF), rows, left, right, jnp.asarray(inner, BF), jnp.asarray(side, BF), wconv)
 
 
-def coarse_kernel(core, x, haar, wband, wpoint, wproj, sub, pre, hidden, cout, split, outs):
+def coarse_kernel(core, x, haar, wband, wp_hbm, wj_hbm, sub, pre, hidden, cout, split, outs, wpoint, wproj, sems):
     k = pl.program_id(0)
+    loads = [
+        pltpu.make_async_copy(src, dst, sems.at[n])
+        for n, (src, dst) in enumerate(((wp_hbm, wpoint), (wj_hbm, wproj)))
+    ]
+
+    @pl.when(k == 0)
+    def _():
+        for load in loads:
+            load.start()
+
     h = haar[pl.ds(pl.multiple_of(k * 64, 64), 64), :]
     part = jnp.concatenate([dot(h, x[:256, :]), dot(h, x[256:, :])], axis=0).astype(BF)
     sub[pl.ds(pl.multiple_of(k * 128, 128), 128), :] = part
@@ -132,6 +142,8 @@
 
     @pl.when(k == BANDS - 1)
     def _():
+        for load in loads:
+            load.wait()
         h = haar[...]
         for g in range(2):
             cells = slice(g * 256, (g + 1) * 256)
@@ -155,8 +167,8 @@
             whole(PAIR, C),
             whole(256, 256),
             pl.BlockSpec((1, C, C), lambda i: (i, 0, 0)),
-            whole(C, C),
-            whole(C, CF),
+            pl.BlockSpec(memory_space=pl.ANY),
+            pl.BlockSpec(memory_space=pl.ANY),
         ],
         out_specs=[whole(PAIR, C), whole(PAIR, C), whole(PAIR, C), whole(CELLS, CF)],
         out_shape=[
@@ -165,14 +177,26 @@
             jax.ShapeDtypeStruct((PAIR, C), BF),
             jax.ShapeDtypeStruct((CELLS, CF), BF),
         ],
-        scratch_shapes=[pltpu.VMEM((2, 2, 256, C), BF), pltpu.VMEM((IR, 2 * IC, CF), F32)],
-        compiler_params=params(24),
+        scratch_shapes=[
+            pltpu.VMEM((2, 2, 256, C), BF),
+            pltpu.VMEM((IR, 2 * IC, CF), F32),
+            pltpu.VMEM((C, C), BF),
+            pltpu.VMEM((C, CF), BF),
+            pltpu.SemaphoreType.DMA((2,)),
+        ],
+        compiler_params=params(16),
         cost_estimate=cost(1_000_000_000, 6_000_000),
         name="coarse_forward",
     )(core, x, haar, wband, wpoint, wproj)
 
 
-def grads_kernel(core, x, haar, wproj, sub, pre, hidden, dco, dtwin, out, both):
+def grads_kernel(core, x_hbm, haar, wproj, sub_hbm, pre, hidden_hbm, dco, dtwin, out, both, x, sub, hidden, sems):
+    loads = [
+        pltpu.make_async_copy(src, dst, sems.at[n])
+        for n, (src, dst) in enumerate(((sub_hbm, sub), (x_hbm, x), (hidden_hbm, hidden)))
+    ]
+    for load in loads:
+        load.start()
     own = pl.multiple_of(core[0] * IC, IC)
     both[:, pl.ds(own, IC), :] = dco[...].astype(F32).reshape(IR, IC, CF)
     both[:, pl.ds(IC - own, IC), :] = dtwin[...].astype(F32).reshape(IR, IC, CF)
@@ -185,6 +209,8 @@
     h = haar[...]
     dmix = [dot(h, dpre[g * 256 : (g + 1) * 256]).astype(BF) for g in range(2)]
     half = pl.ds(pl.multiple_of(core[0] * 256, 256), 256)
+    for load in loads:
+        load.wait()
     for k in range(5):
         if k < BANDS:
             dk = jnp.concatenate([dmix[g][k * 64 : (k + 1) * 64] for g in range(2)], axis=0)
@@ -201,32 +227,45 @@
 
 
 def grads_pass(core, x, haar, wproj, sub, pre, hidden, dco, dtwin):
-    vm = pl.BlockSpec(memory_space=pltpu.VMEM)
+    vm, hbm = pl.BlockSpec(memory_space=pltpu.VMEM), pl.BlockSpec(memory_space=pl.ANY)
     return pl.pallas_call(
         grads_kernel,
-        in_specs=[pl.BlockSpec(memory_space=pltpu.SMEM)] + [vm] * 8,
+        in_specs=[pl.BlockSpec(memory_space=pltpu.SMEM), hbm, vm, vm, hbm, vm, hbm, vm, vm],
         out_specs=vm,
         out_shape=jax.ShapeDtypeStruct((PACK, 128), BF),
-        scratch_shapes=[pltpu.VMEM((IR, 2 * IC, CF), F32)],
-        compiler_params=params(24, 0),
+        scratch_shapes=[pltpu.VMEM((IR, 2 * IC, CF), F32)]
+        + [pltpu.VMEM((PAIR, C), BF)] * 3
+        + [pltpu.SemaphoreType.DMA((3,))],
+        compiler_params=params(16, 0),
         cost_estimate=cost(1_000_000_000, 6_000_000),
         name="coarse_gradients",
     )(core, x, haar, wproj, sub, pre, hidden, dco, dtwin)
 
 
-def fill_windows(i, tile, rows, left, right, win):
+def window_specs():
+    return [
+        pl.BlockSpec((1, TC, CF), lambda i: (jnp.maximum(i * HB - 1, 0), 0, 0)),
+        pl.BlockSpec((HB, TC, CF), lambda i: (i, 0, 0)),
+        pl.BlockSpec((1, TC, CF), lambda i: (jnp.minimum(i * HB + HB, TR - 1), 0, 0)),
+        whole(2, TC, CF),
+        whole(SIDE, CF),
+        whole(SIDE, CF),
+    ]
+
+
+def fill_windows(i, before, tile, after, rows, left, right, win):
     r0 = i * HB
-    win[1 : HB + 1, 8 : 8 + TC, :] = tile[pl.ds(r0, HB)].astype(F32)
-    before = tile[pl.ds(jnp.maximum(r0 - 1, 0), 1)].astype(F32)
-    after = tile[pl.ds(jnp.minimum(r0 + HB, TR - 1), 1)].astype(F32)
-    win[0:1, 8 : 8 + TC, :] = jnp.where(i == 0, rows[0:1].astype(F32), before)
-    win[HB + 1 : HB + 2, 8 : 8 + TC, :] = jnp.where(i == NB - 1, rows[1:2].astype(F32), after)
+    win[1 : HB + 1, 8 : 8 + TC, :] = tile[...].astype(F32)
+    win[0:1, 8 : 8 + TC, :] = jnp.where(i == 0, rows[0:1], before[...]).astype(F32)
+    win[HB + 1 : HB + 2, 8 : 8 + TC, :] = jnp.where(i == NB - 1, rows[1:2], after[...]).astype(F32)
     for r in range(HB + 2):
         win[r, 7:8, :] = left[pl.ds(r0 + r, 1), :]
         win[r, 8 + TC : 9 + TC, :] = right[pl.ds(r0 + r, 1), :]
 
 
-def wgrad_kernel(core, fine, cout, oc, rows, left, right, conv_in, keep, send, up, win, shifted, acc):
+def wgrad_kernel(
+    core, fine, cout, before, oc, after, rows, left, right, conv_in, keep, send, up, win, shifted, acc
+):
     i = pl.program_id(0)
     coarse = cout[...].astype(F32)
     for q in range(HB // 4):
@@ -237,7 +276,7 @@
         grown = jnp.concatenate([up[q, 0], up[q, 1]], axis=-1)
         for t in range(4):
             conv_in[4 * q + t] = (fine[4 * q + t].astype(F32) + grown).astype(BF)
-    fill_windows(i, oc, rows, left, right, win)
+    fill_windows(i, before, oc, after, rows, left, right, win)
     for b in range(3):
         shifted[:, :, b * CF : (b + 1) * CF] = win[:, 9 - b : 9 - b + TC, :].astype(BF)
 
@@ -268,11 +307,8 @@
             pl.BlockSpec(memory_space=pltpu.SMEM),
             pl.BlockSpec((HB, TC, CF), lambda i: (i, 0, 0)),
             pl.BlockSpec((HB // 4 * IC, CF), lambda i: (i, 0)),
-            whole(TR, TC, CF),
-            whole(2, TC, CF),
-            whole(SIDE, CF),
-            whole(SIDE, CF),
-        ],
+        ]
+        + window_specs(),
         out_specs=[
             pl.BlockSpec((HB, TC, CF), lambda i: (i, 0, 0)),
             whole(LATE, 128),
@@ -289,15 +325,15 @@
             pltpu.VMEM((HB + 2, TC, 3 * CF), BF),
             pltpu.VMEM((3, CF, 3 * CF), F32),
         ],
-        compiler_params=params(32),
+        compiler_params=params(16),
         cost_estimate=cost(8_000_000_000, 9_000_000),
         name="conv_weight_gradient",
-    )(core, fine, cout, oc, rows, left, right)
-
-
-def conv_kernel(ci, rows, left, right, wconv, out, win, wide):
+    )(core, fine, cout, oc, oc, oc, rows, left, right)
+
+
+def conv_kernel(before, ci, after, rows, left, right, wconv, out, win, wide):
     i = pl.program_id(0)
-    fill_windows(i, ci, rows, left, right, win)
+    fill_windows(i, before, ci, after, rows, left, right, win)
     for b in range(3):
         wide[:, :, b * CF : (b + 1) * CF] = win[:, 7 + b : 7 + b + TC, :].astype(BF)
     total = jnp.zeros((HB * TC, CF), F32)
@@ -310,20 +346,14 @@
     return pl.pallas_call(
         conv_kernel,
         grid=(NB,),
-        in_specs=[
-            whole(TR, TC, CF),
-            whole(2, TC, CF),
-            whole(SIDE, CF),
-            whole(SIDE, CF),
-            whole(3, 3 * CF, CF),
-        ],
+        in_specs=window_specs() + [whole(3, 3 * CF, CF)],
         out_specs=pl.BlockSpec((HB, TC, CF), lambda i: (i, 0, 0)),
         out_shape=jax.ShapeDtypeStruct((TR, TC, CF), BF),
         scratch_shapes=[pltpu.VMEM((HB + 2, 48, CF), F32), pltpu.VMEM((HB + 2, TC, 3 * CF), BF)],
-        compiler_params=params(32),
-        cost_estimate=cost(8_000_000_000, 6_000_000),
+        compiler_params=params(16),
+        cost_estimate=cost(1_000_000, 1_000_000),
         name="conv_forward",
-    )(ci, rows, left, right, wconv.reshape(3, 3 * CF, CF))
+    )(ci, ci, ci, rows, left, right, wconv.reshape(3, 3 * CF, CF))
 
 
 def add_late_kernel(keep, got, packed, out):
@@ -381,30 +411,60 @@
             jax.ShapeDtypeStruct((C, CF), F32),
         ],
         input_output_aliases={2 + n: n for n in range(len(before))},
-        compiler_params=params(24),
+        compiler_params=params(16),
         cost_estimate=cost(0, 6_000_000),
         name="place_gradients",
     )(core, half, *before)
 
 
-def neighbours(axes, count):
-    forward = [(i, i + 1) for i in range(count - 1)]
-    return forward, [(b, a) for a, b in forward]
-
-
-def halo(tile, east_edge, west_edge):
-    forward, backward = neighbours(COL, 16)
-    west = lax.ppermute(east_edge, COL, forward)
-    east = lax.ppermute(west_edge, COL, backward)
-    forward, backward = neighbours(ROW, 8)
+def shift(value, axes, count, step):
+    pairs = [(i, i + step) for i in range(count) if 0 <= i + step < count]
+    return lax.ppermute(value, axes, pairs)
+
+
+def side_edges(first, last):
+    lower = lax.axis_index("c") == 0
+    twin = lax.ppermute(jnp.where(lower, last, first), "c", [(0, 1), (1, 0)])
+    pairs = [(2 * k + 1, 2 * k + 2) for k in range(7)]
+    pairs = pairs + [(b, a) for a, b in pairs]
+    chip = lax.ppermute(jnp.where(lower, first, last), COL, pairs)
+    return jnp.where(lower, chip, twin), jnp.where(lower, twin, chip)
+
+
+def sides(corners, west, east):
+    pad = jnp.zeros((SIDE - TR - 2, CF), BF)
+    left = jnp.concatenate([corners[0], west, corners[2], pad], axis=0)
+    right = jnp.concatenate([corners[1], east, corners[3], pad], axis=0)
+    return left.astype(F32), right.astype(F32)
+
+
+def row_halo(tile, west, east):
     low = jnp.concatenate([tile[TR - 1], west[TR - 1 :], east[TR - 1 :]], axis=0)
     high = jnp.concatenate([tile[0], west[:1], east[:1]], axis=0)
-    above = lax.ppermute(low, ROW, forward)
-    below = lax.ppermute(high, ROW, backward)
-    pad = jnp.zeros((SIDE - TR - 2, CF), BF)
-    left = jnp.concatenate([above[TC : TC + 1], west, below[TC : TC + 1], pad], axis=0)
-    right = jnp.concatenate([above[TC + 1 :], east, below[TC + 1 :], pad], axis=0)
-    return jnp.stack([above[:TC], below[:TC]]), left.astype(F32), right.astype(F32)
+    above, below = shift(low, ROW, 8, 1), shift(high, ROW, 8, -1)
+    corners = [part for row in (above, below) for part in (row[TC : TC + 1], row[TC + 1 :])]
+    return (jnp.stack([above[:TC], below[:TC]]),) + sides(corners, west, east)
+
+
+def whole_halo(tile):
+    first, last = tile[:, 0], tile[:, TC - 1]
+    lower = lax.axis_index("c") == 0
+    inner, outer = jnp.where(lower, last, first), jnp.where(lower, first, last)
+    twin = lax.ppermute(inner, "c", [(0, 1), (1, 0)])
+    chips = [(2 * k + 1, 2 * k + 2) for k in range(7)]
+    chips = chips + [(b, a) for a, b in chips]
+    chip = lax.ppermute(outer, COL, chips)
+    rows, far = [], []
+    for down, at in ((1, TR - 1), (-1, 0)):
+        rows.append(shift(jnp.concatenate([tile[at], twin[at : at + 1]], axis=0), ROW, 8, down))
+        pairs = [(16 * r + a, 16 * (r + down) + b) for r in range(8) for a, b in chips if 0 <= r + down < 8]
+        far.append(lax.ppermute(outer[at : at + 1], ROW + COL, pairs))
+    west, east = jnp.where(lower, chip, twin), jnp.where(lower, twin, chip)
+    corners = []
+    for row, cell in zip(rows, far):
+        near = row[TC:]
+        corners += [jnp.where(lower, cell, near), jnp.where(lower, near, cell)]
+    return (jnp.stack([row[:TC] for row in rows]),) + sides(corners, west, east)
 
 
 def local(coarse_in, fine_in, band_weight, point_weight, proj_weight, conv_weight, out_cot):
@@ -414,12 +474,14 @@
 
     chunks = coarse_in.reshape(2, 8, 16, C).transpose(1, 0, 2, 3)
     chunks = jnp.broadcast_to(chunks[:, None], (8, 2, 2, 16, C)).reshape(16, 2, 16, C)
-    chunks, last, first = lax.optimization_barrier((chunks, out_cot[:, TC - 1], out_cot[:, 0]))
+    west, east = side_edges(out_cot[:, 0], out_cot[:, TC - 1])
+    chunks, west, east = lax.optimization_barrier((chunks, west, east))
+    cot_halo = row_halo(out_cot, west, east)
     x = lax.all_to_all(chunks, COL, 0, 0, tiled=True).reshape(PAIR, C)
-    cot_halo = halo(out_cot, last, first)
-    sub, pre, hidden, cout = coarse_pass(core, x, haar, band_weight, point_weight, proj_weight)
     dco = dcoarse_pass(out_cot, *cot_halo, conv_weight)
     dtwin = lax.ppermute(dco, "c", swap)
+    x, dtwin = lax.optimization_barrier((x, dtwin))
+    sub, pre, hidden, cout = coarse_pass(core, x, haar, band_weight, point_weight, proj_weight)
     conv_in, keep, send = wgrad_pass(core, fine_in, cout, out_cot, *cot_halo)
     got = lax.ppermute(send, "c", swap)
     packed = grads_pass(core, x, haar, proj_weight, sub, pre, hidden, dco, dtwin)
@@ -427,12 +489,14 @@
 
     packed, conv_in = lax.optimization_barrier((packed, conv_in))
     parts = lax.all_to_all(packed, CHIPS, 0, 0, tiled=True)
-    fine_out = conv_pass(conv_in, *halo(conv_in, conv_in[:, TC - 1], conv_in[:, 0]), conv_weight)
-    parts, fine_out = lax.optimization_barrier((parts, fine_out))
+    conv_halo = whole_halo(conv_in)
     parts = parts.reshape(PEERS, PACK // PEERS, 128)
     done = (jnp.sum(parts.astype(F32), axis=0) * SCALE).astype(BF)
     spread = jnp.broadcast_to(done[None], (PEERS, PACK // PEERS, 128)).reshape(PACK, 128)
+    spread, conv_halo = lax.optimization_barrier((spread, conv_halo))
     mine = lax.all_to_all(spread, CHIPS, 0, 0, tiled=True)
+    fine_out = conv_pass(conv_in, *conv_halo, conv_weight)
+    mine, fine_out = lax.optimization_barrier((mine, fine_out))
     other = lax.ppermute(mine, "c", swap)
     grads = place_half(core, mine)
     grad_conv, grad_band, grad_point, grad_proj = place_half(1 - core, other, grads)

time: 160 us -> 150 us (0.938)
  blocking collectives: 39.1 us -> 0 us
  local copies, waits for them, and re-layouts: 7.94 us -> 20.4 us
  starting transfers between devices: 49.3 us -> 61.6 us
  other arithmetic: 2.16 us -> 5.26 us
    all_to_all x1 -> x0, blocking collectives: 39.1 us -> none  [local(): mine = lax.all_to_all(spread, CHIPS, 0, 0, tiled=True)]
    ppermute x8 -> x10, waiting for transfers between devices: 29.9 us -> 9.62 us  [the longest x1 8.69 us: whole_halo(): chip = lax.ppermute(outer, COL, chips)]
    all_to_all x0 -> x1, waiting for transfers between devices: none -> 19.8 us  [local(): mine = lax.all_to_all(spread, CHIPS, 0, 0, tiled=True)]
    all_to_all x0 -> x1, starting transfers between devices: none -> 10 us  [local(): mine = lax.all_to_all(spread, CHIPS, 0, 0, tiled=True)]
    unnamed x24 -> x44, local copies, waits for them, and re-layouts: 2.69 us -> 11.3 us
    ppermute x8 -> x10, starting transfers between devices: 21.8 us -> 25.2 us  [the longest x4 12.2 us: shift(): return lax.ppermute(value, axes, pairs)]
    all_to_all x1, starting transfers between devices: 16.3 us -> 14.5 us  [local(): parts = lax.all_to_all(packed, CHIPS, 0, 0, tiled=True)]
    all_to_all x1, waiting for transfers between devices: 0.01 us -> 1.74 us  [local(): parts = lax.all_to_all(packed, CHIPS, 0, 0, tiled=True)]
  transfers between devices with their start and end apart: 13 -> 16, of which waited for: 7 -> 6; matrix products, arithmetic and copies ran while one was open for 0% -> 4% of each run, Pallas kernels for 8% -> 9%
where the time goes in v4:
time: 150 us; the launch traced here: 149 us
  starting transfers between devices  61.6 us (41%)
  waiting for transfers between devices  31.6 us (21%)
  Pallas kernels  28.8 us (19%)
  local copies, waits for them, and re-layouts  20.4 us (14%)
  other arithmetic  5.26 us (4%)
    all_to_all x1, waiting for transfers between devices, local(): mine = lax.all_to_all(spread, CHIPS, 0, 0, tiled=True)  19.8 us
    all_to_all x1, starting transfers between devices, local(): parts = lax.all_to_all(packed, CHIPS, 0, 0, tiled=True)  14.5 us
    ppermute x4, starting transfers between devices, shift(): return lax.ppermute(value, axes, pairs)  12.2 us
    unnamed x44, local copies, waits for them, and re-layouts  11.3 us
    all_to_all x1, starting transfers between devices, local(): mine = lax.all_to_all(spread, CHIPS, 0, 0, tiled=True)  10 us
    pallas_call x1, Pallas kernels, wgrad_pass(): pl.pallas_call(wgrad_kernel, grid=(NB,), in_specs=[pl.BlockSpec(memory_sp...  8.75 us
    ppermute x1, waiting for transfers between devices, whole_halo(): chip = lax.ppermute(outer, COL, chips)  8.69 us
    all_to_all x1, starting transfers between devices, local(): x = lax.all_to_all(chunks, COL, 0, 0, tiled=True).reshape(PAIR, C)  8.11 us
  transfers between devices with their start and end apart: 16, of which 6 were waited for; matrix products, arithmetic and copies ran while one was open for 4% of the time, Pallas kernels for 9%

profile of v4, /device:TPU:1, one launch (start us, length us, event | category | flops | bytes accessed | tf_op | source)
XLA Modules:
  0.0 148.7 jit_solution(447493774768137022)
XLA Ops:
  0.7 1.6 %fusion = (bf16[128,1,256]{2,1,0:T(2,128)(2,1)S(1)}, bf16[128,1,256]{2,1,0:T(2,128)(2,1)S(1)}) fusion(bf16[128,32,256]{2,1,0:T(8,128)(2,1)} %after.1), kind=kLoop, calls=%fused_computation.34 | loop fusion | bytes 262144 | tf_op jit(solution)/shard_map/slice | solution.py:477
  2.3 1.5 %collective-permute-start.1 = (bf16[128,256]{1,0:T(8,128)(2,1)S(1)}, bf16[128,256]{1,0:T(8,128)(2,1)S(1)}, u32[]{:S(2)}, u32[]{:S(2)}) collective-permute-start(bf16[128,256]{1,0:T(8,128)(2,1)S(1)} %get-tuple-element.69), channel_id=1, source_target_pairs={{0,1},{1,0},{2,3},{3,2},{4,5},{5,4},{6,7},{7,6},{8,9},{9,8},{10,11... | collective-permute-start | bytes 196616 | tf_op jit(solution)/shard_map/ppermute | solution.py:427
  3.8 3.2 %collective-permute-start = (bf16[128,256]{1,0:T(8,128)(2,1)S(1)}, bf16[128,256]{1,0:T(8,128)(2,1)S(1)}, u32[]{:S(2)}, u32[]{:S(2)}) collective-permute-start(bf16[128,256]{1,0:T(8,128)(2,1)S(1)} %get-tuple-element.70), channel_id=1, source_target_pairs={{1,2},{3,4},{5,6},{7,8},{9,10},{11,12},{13,14},{2,1},{4,3},{6,5},{... | collective-permute-start | bytes 196616 | tf_op jit(solution)/shard_map/ppermute | solution.py:430
  7.0 0.7 slice_bitcast_fusion.7
  7.7 1.0 copy.20
  8.7 0.6 pad.21.clone
  9.4 0.9 broadcast_in_dim.4
  10.2 8.1 %all-to-all-start = ((bf16[16,2,16,512]{3,2,1,0:T(8,128)(2,1)}), bf16[16,2,16,512]{3,2,1,0:T(8,128)(2,1)}, u32[]{:S(2)}, u32[]{:S(2)}) async-start(bf16[16,2,16,512]{3,2,1,0:T(8,128)(2,1)} %bitcast.42), calls=%async_computation | async-start | bytes 1048576 | tf_op jit(solution)/shard_map/all_to_all | solution.py:480
  18.4 1.3 collective-permute-start.3
  19.7 4.2 %collective-permute-start.2 = (bf16[34,256]{1,0:T(8,128)(2,1)S(1)}, bf16[34,256]{1,0:T(8,128)(2,1)S(1)}, u32[]{:S(2)}, u32[]{:S(2)}) collective-permute-start(bf16[34,256]{1,0:T(8,128)(2,1)S(1)} %pad_maximum_fusion.2), channel_id=1, source_target_pairs={{0,16},{16,32},{32,48},{48,64},{64,80},{80,96},{96,112},{1,17},{17... | collective-permute-start | bytes 52232 | tf_op jit(solution)/shard_map/ppermute | solution.py:422
  23.9 0.9 collective-permute-done.2
  24.8 1.0 maximum_convert_fusion.1
  25.8 0.8 copy-done.15
  26.6 0.8 copy-done.16
  27.4 1.1 coarse_cotangent.1.dco
  28.5 1.2 collective-permute-start.4
  29.7 0.7 copy-done.4
  30.7 0.7 copy-done.13
  31.3 0.9 copy-done.6
  32.3 0.9 copy-done.11
  33.2 1.6 %copy-done.17 = bf16[4,512,512]{2,1,0:T(8,128)(2,1)S(1)} copy-done((bf16[4,512,512]{2,1,0:T(8,128)(2,1)S(1)}, bf16[4,512,512]{2,1,0:T(8,128)(2,1)}, u32[]{:S(2)}) %copy-start.17) | copy-done | bytes 2097176
  34.8 1.0 copy-done.19
  35.8 3.7 %coarse_forward.1 = (bf16[512,512]{1,0:T(8,128)(2,1)S(1)}, f32[512,512]{1,0:T(8,128)S(1)}, bf16[512,512]{1,0:T(8,128)(2,1)S(1)}, bf16[256,256]{1,0:T(8,128)(2,1)S(1)}) custom-call(s32[1]{0:T(128)} %bitcast.core, bf16[512,512]{1,0:T(8,128)(2,1)} %bitcast.6.x.x_hbm, bf16[256,256]{1,0:T(8,128)(2,1)S(1)} %copy-done.11, bf16[4,512,512]{2,1,0:T(8,128)(2,1)S(1)} %copy-done.17, ...), custom_call_target="tpu_custom_call" | custom-call | flops 1000000000 | bytes 6000000 | tf_op jit(solution)/shard_map/coarse_forward/pallas_call | solution.py:162
  39.5 1.6 %copy-done.3 = bf16[128,32,256]{2,1,0:T(8,128)(2,1)S(1)} copy-done((bf16[128,32,256]{2,1,0:T(8,128)(2,1)S(1)}, bf16[128,32,256]{2,1,0:T(8,128)(2,1)}, u32[]{:S(2)}) %copy-start.3) | copy-done | bytes 2097176
  41.1 1.6 %copy-done.18 = bf16[128,32,256]{2,1,0:T(8,128)(2,1)S(1)} copy-done((bf16[128,32,256]{2,1,0:T(8,128)(2,1)S(1)}, bf16[128,32,256]{2,1,0:T(8,128)(2,1)}, u32[]{:S(2)}) %copy-start.18) | copy-done | bytes 2097176
  42.7 8.7 %conv_weight_gradient.1 = (bf16[128,32,256]{2,1,0:T(8,128)(2,1)S(1)}, bf16[2560,128]{1,0:T(8,128)(2,1)S(1)}, bf16[2560,128]{1,0:T(8,128)(2,1)S(1)}) custom-call(s32[1]{0:T(128)} %bitcast.core, bf16[128,32,256]{2,1,0:T(8,128)(2,1)S(1)} %copy-done.18, bf16[256,256]{1,0:T(8,128)(2,1)S(1)} %get-tuple-element.37.cout, bf16[128,32,256]{2,1,0:T(8,128)(2,1)S(1)} %copy-done.3, ...), custom_call_target="tpu_custom_call" | custom-call | flops 8000000000 | bytes 9000000 | tf_op jit(solution)/shard_map/conv_weight_gradient/pallas_call | solution.py:303
  51.9 1.9 %coarse_gradients.1.packed = bf16[8192,128]{1,0:T(8,128)(2,1)S(1)} custom-call(s32[1]{0:T(128)} %bitcast.core, bf16[512,512]{1,0:T(8,128)(2,1)} %bitcast.6.x.x_hbm, bf16[256,256]{1,0:T(8,128)(2,1)S(1)} %copy-done.12, bf16[512,256]{1,0:T(8,128)(2,1)S(1)} %copy-done.7, bf16[512,512]{1,0:T(8,128)(2,1)S(1)} %get-tuple-element.40.sub_hbm, ...), custom_call_target="tpu_custom_call" | custom-call | flops 1000000000 | bytes 6000000 | tf_op jit(solution)/shard_map/coarse_gradients/pallas_call | solution.py:231
  54.2 2.5 %copy.23 = bf16[128,32,256]{2,0,1:T(8,128)(2,1)} copy(bf16[128,32,256]{2,1,0:T(8,128)(2,1)S(1)} %get-tuple-element.46.before.ci.after) | data formatting | bytes 4194304 | tf_op jit(solution)/shard_map/optimization_barrier | solution.py:490
  56.7 14.5 %all-to-all-start.1 = ((bf16[64,128,128]{2,1,0:T(8,128)(2,1)}), bf16[64,128,128]{2,1,0:T(8,128)(2,1)}, u32[]{:S(2)}, u32[]{:S(2)}) async-start(bf16[64,128,128]{2,1,0:T(8,128)(2,1)} %bitcast.39), calls=%async_computation.1 | async-start | bytes 4194304 | tf_op jit(solution)/shard_map/all_to_all | solution.py:491
  71.2 0.9 broadcast_select_fusion
  72.6 3.9 %collective-permute-start.9 = (bf16[1,256]{1,0:T(2,128)(2,1)S(1)}, bf16[1,256]{1,0:T(2,128)(2,1)S(1)}, u32[]{:S(2)}, u32[]{:S(2)}) collective-permute-start(bf16[1,256]{1,0:T(2,128)(2,1)S(1)} %get-tuple-element.75), channel_id=1, source_target_pairs={{1,18},{3,20},{5,22},{7,24},{9,26},{11,28},{13,30},{2,17},{4,19},{... | collective-permute-start | bytes 1544 | tf_op jit(solution)/shard_map/ppermute | solution.py:461
  76.6 1.3 collective-permute-start.11
  77.9 2.6 %collective-permute-start.10 = (bf16[128,256]{1,0:T(8,128)(2,1)S(1)}, bf16[128,256]{1,0:T(8,128)(2,1)S(1)}, u32[]{:S(2)}, u32[]{:S(2)}) collective-permute-start(bf16[128,256]{1,0:T(8,128)(2,1)S(1)} %bitcast.44), channel_id=1, source_target_pairs={{1,2},{3,4},{5,6},{7,8},{9,10},{11,12},{13,14},{2,1},{4,3},{6,5},{... | collective-permute-start | bytes 196616 | tf_op jit(solution)/shard_map/ppermute | solution.py:456
  80.5 1.3 collective-permute-start.8
  81.8 5.4 %collective-permute-start.7 = (bf16[33,256]{1,0:T(8,128)(2,1)S(1)}, bf16[33,256]{1,0:T(8,128)(2,1)S(1)}, u32[]{:S(2)}, u32[]{:S(2)}) collective-permute-start(bf16[33,256]{1,0:T(8,128)(2,1)S(1)} %pad_maximum_fusion.4), channel_id=1, source_target_pairs={{0,16},{16,32},{32,48},{48,64},{64,80},{80,96},{96,112},{1,17},{17... | collective-permute-start | bytes 50696 | tf_op jit(solution)/shard_map/ppermute | solution.py:422
  87.2 8.7 %collective-permute-done.10 = bf16[128,256]{1,0:T(8,128)(2,1)S(1)} collective-permute-done((bf16[128,256]{1,0:T(8,128)(2,1)S(1)}, bf16[128,256]{1,0:T(8,128)(2,1)S(1)}, u32[]{:S(2)}, u32[]{:S(2)}) %collective-permute-start.10) | collective-permute-done | bytes 65568 | tf_op jit(solution)/shard_map/ppermute | solution.py:456
  96.0 0.6 pad_maximum_fusion.1.rows
  96.6 0.7 maximum_convert_fusion.3
  97.4 1.7 %all-to-all-done.1 = bf16[64,128,128]{2,1,0:T(8,128)(2,1)} async-done(((bf16[64,128,128]{2,1,0:T(8,128)(2,1)}), bf16[64,128,128]{2,1,0:T(8,128)(2,1)}, u32[]{:S(2)}, u32[]{:S(2)}) %all-to-all-start.1) | async-done | bytes 2097184 | tf_op jit(solution)/shard_map/all_to_all | solution.py:491
  99.1 1.9 %convert_reduce_fusion = f32[128,128]{1,0:T(8,128)S(1)} fusion(bf16[64,128,128]{2,1,0:T(8,128)(2,1)} %all-to-all-done.1), kind=kLoop, calls=%fused_computation | loop fusion | flops 2080768 | bytes 2162688 | tf_op jit(solution)/shard_map/reduce_sum | solution.py:494
  101.1 1.8 %broadcast_in_dim.5 = bf16[64,128,128]{2,1,0:T(8,128)(2,1)} broadcast(bf16[128,128]{1,0:T(8,128)(2,1)S(1)} %multiply_convert_fusion), dimensions={1,2} | broadcast | bytes 2129920 | tf_op jit(solution)/shard_map/broadcast_in_dim | solution.py:495
  102.9 10.0 %all-to-all-start.2 = ((bf16[64,128,128]{2,1,0:T(8,128)(2,1)}), bf16[64,128,128]{2,1,0:T(8,128)(2,1)}, u32[]{:S(2)}, u32[]{:S(2)}) async-start(bf16[64,128,128]{2,1,0:T(8,128)(2,1)} %broadcast_in_dim.5), calls=%async_computation.2 | async-start | bytes 4194304 | tf_op jit(solution)/shard_map/all_to_all | solution.py:497
  112.9 0.7 copy-done.8
  113.7 6.7 %conv_forward.1 = bf16[128,32,256]{2,1,0:T(8,128)(2,1)} custom-call(bf16[128,32,256]{2,1,0:T(8,128)(2,1)S(1)} %get-tuple-element.46.before.ci.after, bf16[128,32,256]{2,1,0:T(8,128)(2,1)S(1)} %get-tuple-element.46.before.ci.after, bf16[128,32,256]{2,1,0:T(8,128)(2,1)S(1)} %get-tuple-element.46.before.ci.after, bf16[2,32,256]{2,1,0:T(8,128)(2,1)S(1)} %copy-done.8, ...), custom_call_target="tpu_custom_call" | custom-call | flops 1000000 | bytes 1000000 | tf_op jit(solution)/shard_map/conv_forward/pallas_call | solution.py:346
  120.4 19.8 %all-to-all-done.2 = bf16[64,128,128]{2,1,0:T(8,128)(2,1)} async-done(((bf16[64,128,128]{2,1,0:T(8,128)(2,1)}), bf16[64,128,128]{2,1,0:T(8,128)(2,1)}, u32[]{:S(2)}, u32[]{:S(2)}) %all-to-all-start.2) | async-done | bytes 2097184 | tf_op jit(solution)/shard_map/all_to_all | solution.py:497
  140.2 2.1 %collective-permute-start.12 = (bf16[8192,128]{1,0:T(8,128)(2,1)}, bf16[8192,128]{1,0:T(8,128)(2,1)S(1)}, u32[]{:S(2)}, u32[]{:S(2)}) collective-permute-start(bf16[8192,128]{1,0:T(8,128)(2,1)} %bitcast.23.half), channel_id=1, source_target_pairs={{0,1},{1,0},{2,3},{3,2},{4,5},{5,4},{6,7},{7,6},{8,9},{9,8},{10,11... | collective-permute-start | bytes 6291464 | tf_op jit(solution)/shard_map/ppermute | solution.py:500
  142.3 3.9 %place_gradients.2 = (f32[9,256,256]{2,1,0:T(8,128)}, f32[4,512,512]{2,1,0:T(8,128)}, f32[512,512]{1,0:T(8,128)}, f32[512,256]{1,0:T(8,128)}) custom-call(s32[1]{0:T(128)} %bitcast.core, bf16[8192,128]{1,0:T(8,128)(2,1)} %bitcast.23.half), custom_call_target="tpu_custom_call" | custom-call | bytes 6000000 | tf_op jit(solution)/shard_map/place_gradients/pallas_call | solution.py:394
  146.3 2.4 %place_gradients.3 = (f32[9,256,256]{2,1,0:T(8,128)}, f32[4,512,512]{2,1,0:T(8,128)}, f32[512,512]{1,0:T(8,128)}, f32[512,256]{1,0:T(8,128)}) custom-call(s32[1]{0:T(128)S(6)} %sub.3.core, bf16[8192,128]{1,0:T(8,128)(2,1)S(1)} %collective-permute-done.12.half, ...), custom_call_target="tpu_custom_call", output_to_operand_aliasing={{0}: (2, {}), {1}: (3, {}), {2}: (4, {}), {3}: (5, {})} | custom-call | bytes 6000000 | tf_op jit(solution)/shard_map/place_gradients/pallas_call | solution.py:394
  (70 shorter events, 2.1 us)
Async XLA Ops:
  0.6 25.2 %copy-start.1 = (bf16[9,256,256]{2,1,0:T(8,128)(2,1)S(1)}, bf16[9,256,256]{2,1,0:T(8,128)(2,1)}, u32[]{:S(2)}) copy-start(bf16[9,256,256]{2,1,0:T(8,128)(2,1)} %wconv.1) | copy-start | bytes 3538948
  0.6 25.2 %copy-start.2 = (bf16[128,32,256]{2,1,0:T(8,128)(2,1)S(1)}, bf16[128,32,256]{2,1,0:T(8,128)(2,1)}, u32[]{:S(2)}) copy-start(bf16[128,32,256]{2,1,0:T(8,128)(2,1)} %after.1) | copy-start | bytes 6291460
  2.3 7.0 %collective-permute-start.1 = (bf16[128,256]{1,0:T(8,128)(2,1)S(1)}, bf16[128,256]{1,0:T(8,128)(2,1)S(1)}, u32[]{:S(2)}, u32[]{:S(2)}) collective-permute-start(bf16[128,256]{1,0:T(8,128)(2,1)S(1)} %get-tuple-element.69), channel_id=1, source_target_pairs={{0,1},{1,0},{2,3},{3,2},{4,5},{5,4},{6,7},{7,6},{8,9},{9,8},{10,11... | collective-permute-start | bytes 196616 | tf_op jit(solution)/shard_map/ppermute | solution.py:427
  3.8 5.6 %collective-permute-start = (bf16[128,256]{1,0:T(8,128)(2,1)S(1)}, bf16[128,256]{1,0:T(8,128)(2,1)S(1)}, u32[]{:S(2)}, u32[]{:S(2)}) collective-permute-start(bf16[128,256]{1,0:T(8,128)(2,1)S(1)} %get-tuple-element.70), channel_id=1, source_target_pairs={{1,2},{3,4},{5,6},{7,8},{9,10},{11,12},{13,14},{2,1},{4,3},{6,5},{... | collective-permute-start | bytes 196616 | tf_op jit(solution)/shard_map/ppermute | solution.py:430
  9.4 15.4 %copy-start.20 = (bf16[128,256]{1,0:T(8,128)(2,1)}, bf16[128,256]{1,0:T(8,128)(2,1)S(1)}, u32[]{:S(2)}) copy-start(bf16[128,256]{1,0:T(8,128)(2,1)S(1)} %get-tuple-element.35) | copy-start | bytes 196612
  9.4 15.4 %copy-start.21 = (bf16[128,256]{1,0:T(8,128)(2,1)}, bf16[128,256]{1,0:T(8,128)(2,1)S(1)}, u32[]{:S(2)}) copy-start(bf16[128,256]{1,0:T(8,128)(2,1)S(1)} %get-tuple-element.34) | copy-start | bytes 196612
  10.2 21.1 %all-to-all-start = ((bf16[16,2,16,512]{3,2,1,0:T(8,128)(2,1)}), bf16[16,2,16,512]{3,2,1,0:T(8,128)(2,1)}, u32[]{:S(2)}, u32[]{:S(2)}) async-start(bf16[16,2,16,512]{3,2,1,0:T(8,128)(2,1)} %bitcast.42), calls=%async_computation | async-start | bytes 1048576 | tf_op jit(solution)/shard_map/all_to_all | solution.py:480
  18.4 5.5 %collective-permute-start.3 = (bf16[34,256]{1,0:T(8,128)(2,1)S(1)}, bf16[34,256]{1,0:T(8,128)(2,1)S(1)}, u32[]{:S(2)}, u32[]{:S(2)}) collective-permute-start(bf16[34,256]{1,0:T(8,128)(2,1)S(1)} %pad_maximum_fusion.3), channel_id=1, source_target_pairs={{16,0},{32,16},{48,32},{64,48},{80,64},{96,80},{112,96},{17,1},{33... | collective-permute-start | bytes 52232 | tf_op jit(solution)/shard_map/ppermute | solution.py:422
  19.7 5.1 %collective-permute-start.2 = (bf16[34,256]{1,0:T(8,128)(2,1)S(1)}, bf16[34,256]{1,0:T(8,128)(2,1)S(1)}, u32[]{:S(2)}, u32[]{:S(2)}) collective-permute-start(bf16[34,256]{1,0:T(8,128)(2,1)S(1)} %pad_maximum_fusion.2), channel_id=1, source_target_pairs={{0,16},{16,32},{32,48},{48,64},{64,80},{80,96},{96,112},{1,17},{17... | collective-permute-start | bytes 52232 | tf_op jit(solution)/shard_map/ppermute | solution.py:422
  24.8 3.7 %copy-start.9 = (bf16[2,32,256]{2,1,0:T(8,128)(2,1)}, bf16[2,32,256]{2,1,0:T(8,128)(2,1)S(1)}, u32[]{:S(2)}) copy-start(bf16[2,32,256]{2,1,0:T(8,128)(2,1)S(1)} %pad_maximum_fusion.rows) | copy-start | bytes 98308
  25.8 0.8 copy-start.15
  26.6 0.8 copy-start.16
  28.5 2.2 %collective-permute-start.4 = (bf16[256,256]{1,0:T(8,128)(2,1)S(1)}, bf16[256,256]{1,0:T(8,128)(2,1)S(1)}, u32[]{:S(2)}, u32[]{:S(2)}) collective-permute-start(bf16[256,256]{1,0:T(8,128)(2,1)S(1)} %coarse_cotangent.1.dco), channel_id=1, source_target_pairs={{0,1},{1,0},{2,3},{3,2},{4,5},{5,4},{6,7},{7,6},{8,9},{9,8},{10,11... | collective-permute-start | bytes 393224 | tf_op jit(solution)/shard_map/ppermute | solution.py:482
  29.7 0.7 copy-start.4
  30.7 0.7 copy-start.13
  31.3 1.0 copy-start.6
  32.3 0.9 copy-start.11
  33.2 1.6 %copy-start.17 = (bf16[4,512,512]{2,1,0:T(8,128)(2,1)S(1)}, bf16[4,512,512]{2,1,0:T(8,128)(2,1)}, u32[]{:S(2)}) copy-start(bf16[4,512,512]{2,1,0:T(8,128)(2,1)} %wband.1) | copy-start | bytes 6291460
  34.8 1.0 copy-start.19
  35.8 3.7 %copy-start.10 = (bf16[2,32,256]{2,1,0:T(8,128)(2,1)S(1)}, bf16[2,32,256]{2,1,0:T(8,128)(2,1)}, u32[]{:S(2)}) copy-start(bf16[2,32,256]{2,1,0:T(8,128)(2,1)} %copy-done.9) | copy-start | bytes 98308
  39.5 1.6 %copy-start.3 = (bf16[128,32,256]{2,1,0:T(8,128)(2,1)S(1)}, bf16[128,32,256]{2,1,0:T(8,128)(2,1)}, u32[]{:S(2)}) copy-start(bf16[128,32,256]{2,1,0:T(8,128)(2,1)} %after.1) | copy-start | bytes 6291460
  41.1 1.6 %copy-start.18 = (bf16[128,32,256]{2,1,0:T(8,128)(2,1)S(1)}, bf16[128,32,256]{2,1,0:T(8,128)(2,1)}, u32[]{:S(2)}) copy-start(bf16[128,32,256]{2,1,0:T(8,128)(2,1)} %fine.1) | copy-start | bytes 6291460
  42.7 9.2 %copy-start.5 = (bf16[256,256]{1,0:T(8,128)(2,1)S(1)}, bf16[256,256]{1,0:T(8,128)(2,1)}, u32[]{:S(2)}) copy-start(bf16[256,256]{1,0:T(8,128)(2,1)} %copy-done.4) | copy-start | bytes 393220
  42.7 9.2 %copy-start.7 = (bf16[512,256]{1,0:T(8,128)(2,1)S(1)}, bf16[512,256]{1,0:T(8,128)(2,1)}, u32[]{:S(2)}) copy-start(bf16[512,256]{1,0:T(8,128)(2,1)} %wproj.1) | copy-start | bytes 786436
  42.7 9.2 %copy-start.12 = (bf16[256,256]{1,0:T(8,128)(2,1)S(1)}, bf16[256,256]{1,0:T(8,128)(2,1)}, u32[]{:S(2)}) copy-start(bf16[256,256]{1,0:T(8,128)(2,1)} %constant.20.clone.haar) | copy-start | bytes 393220
  42.7 9.2 %copy-start.14 = (bf16[256,256]{1,0:T(8,128)(2,1)S(1)}, bf16[256,256]{1,0:T(8,128)(2,1)}, u32[]{:S(2)}) copy-start(bf16[256,256]{1,0:T(8,128)(2,1)} %copy-done.13) | copy-start | bytes 393220
  51.5 2.3 %collective-permute-start.5 = (bf16[2560,128]{1,0:T(8,128)(2,1)S(1)}, bf16[2560,128]{1,0:T(8,128)(2,1)S(1)}, u32[]{:S(2)}, u32[]{:S(2)}) collective-permute-start(bf16[2560,128]{1,0:T(8,128)(2,1)S(1)} %get-tuple-element.39), channel_id=1, source_target_pairs={{0,1},{1,0},{2,3},{3,2},{4,5},{5,4},{6,7},{7,6},{8,9},{9,8},{10,11... | collective-permute-start | bytes 1966088 | tf_op jit(solution)/shard_map/ppermute | solution.py:486
  54.2 2.5 %copy-start = (bf16[8192,128]{1,0:T(8,128)(2,1)}, bf16[8192,128]{1,0:T(8,128)(2,1)S(1)}, u32[]{:S(2)}) copy-start(bf16[8192,128]{1,0:T(8,128)(2,1)S(1)} %late_core_sum.1) | copy-start | bytes 6291460
  56.7 42.4 %all-to-all-start.1 = ((bf16[64,128,128]{2,1,0:T(8,128)(2,1)}), bf16[64,128,128]{2,1,0:T(8,128)(2,1)}, u32[]{:S(2)}, u32[]{:S(2)}) async-start(bf16[64,128,128]{2,1,0:T(8,128)(2,1)} %bitcast.39), calls=%async_computation.1 | async-start | bytes 4194304 | tf_op jit(solution)/shard_map/all_to_all | solution.py:491
  72.1 8.4 %collective-permute-start.6 = (bf16[128,256]{1,0:T(8,128)(2,1)S(1)}, bf16[128,256]{1,0:T(8,128)(2,1)S(1)}, u32[]{:S(2)}, u32[]{:S(2)}) collective-permute-start(bf16[128,256]{1,0:T(8,128)(2,1)S(1)} %get-tuple-element.62), channel_id=1, source_target_pairs={{0,1},{1,0},{2,3},{3,2},{4,5},{5,4},{6,7},{7,6},{8,9},{9,8},{10,11... | collective-permute-start | bytes 196616 | tf_op jit(solution)/shard_map/ppermute | solution.py:453
  72.6 24.0 %collective-permute-start.9 = (bf16[1,256]{1,0:T(2,128)(2,1)S(1)}, bf16[1,256]{1,0:T(2,128)(2,1)S(1)}, u32[]{:S(2)}, u32[]{:S(2)}) collective-permute-start(bf16[1,256]{1,0:T(2,128)(2,1)S(1)} %get-tuple-element.75), channel_id=1, source_target_pairs={{1,18},{3,20},{5,22},{7,24},{9,26},{11,28},{13,30},{2,17},{4,19},{... | collective-permute-start | bytes 1544 | tf_op jit(solution)/shard_map/ppermute | solution.py:461
  76.6 19.4 %collective-permute-start.11 = (bf16[1,256]{1,0:T(2,128)(2,1)S(1)}, bf16[1,256]{1,0:T(2,128)(2,1)S(1)}, u32[]{:S(2)}, u32[]{:S(2)}) collective-permute-start(bf16[1,256]{1,0:T(2,128)(2,1)S(1)} %get-tuple-element.76), channel_id=1, source_target_pairs={{17,2},{19,4},{21,6},{23,8},{25,10},{27,12},{29,14},{18,1},{20,3},... | collective-permute-start | bytes 1544 | tf_op jit(solution)/shard_map/ppermute | solution.py:461
  77.9 18.0 %collective-permute-start.10 = (bf16[128,256]{1,0:T(8,128)(2,1)S(1)}, bf16[128,256]{1,0:T(8,128)(2,1)S(1)}, u32[]{:S(2)}, u32[]{:S(2)}) collective-permute-start(bf16[128,256]{1,0:T(8,128)(2,1)S(1)} %bitcast.44), channel_id=1, source_target_pairs={{1,2},{3,4},{5,6},{7,8},{9,10},{11,12},{13,14},{2,1},{4,3},{6,5},{... | collective-permute-start | bytes 196616 | tf_op jit(solution)/shard_map/ppermute | solution.py:456
  80.5 15.5 %collective-permute-start.8 = (bf16[33,256]{1,0:T(8,128)(2,1)S(1)}, bf16[33,256]{1,0:T(8,128)(2,1)S(1)}, u32[]{:S(2)}, u32[]{:S(2)}) collective-permute-start(bf16[33,256]{1,0:T(8,128)(2,1)S(1)} %pad_maximum_fusion.5), channel_id=1, source_target_pairs={{16,0},{32,16},{48,32},{64,48},{80,64},{96,80},{112,96},{17,1},{33... | collective-permute-start | bytes 50696 | tf_op jit(solution)/shard_map/ppermute | solution.py:422
  81.8 14.2 %collective-permute-start.7 = (bf16[33,256]{1,0:T(8,128)(2,1)S(1)}, bf16[33,256]{1,0:T(8,128)(2,1)S(1)}, u32[]{:S(2)}, u32[]{:S(2)}) collective-permute-start(bf16[33,256]{1,0:T(8,128)(2,1)S(1)} %pad_maximum_fusion.4), channel_id=1, source_target_pairs={{0,16},{16,32},{32,48},{48,64},{64,80},{80,96},{96,112},{1,17},{17... | collective-permute-start | bytes 50696 | tf_op jit(solution)/shard_map/ppermute | solution.py:422
  102.9 37.4 %all-to-all-start.2 = ((bf16[64,128,128]{2,1,0:T(8,128)(2,1)}), bf16[64,128,128]{2,1,0:T(8,128)(2,1)}, u32[]{:S(2)}, u32[]{:S(2)}) async-start(bf16[64,128,128]{2,1,0:T(8,128)(2,1)} %broadcast_in_dim.5), calls=%async_computation.2 | async-start | bytes 4194304 | tf_op jit(solution)/shard_map/all_to_all | solution.py:497
  112.9 0.8 copy-start.8
  140.2 6.1 %collective-permute-start.12 = (bf16[8192,128]{1,0:T(8,128)(2,1)}, bf16[8192,128]{1,0:T(8,128)(2,1)S(1)}, u32[]{:S(2)}, u32[]{:S(2)}) collective-permute-start(bf16[8192,128]{1,0:T(8,128)(2,1)} %bitcast.23.half), channel_id=1, source_target_pairs={{0,1},{1,0},{2,3},{3,2},{4,5},{5,4},{6,7},{7,6},{8,9},{9,8},{10,11... | collective-permute-start | bytes 6291464 | tf_op jit(solution)/shard_map/ppermute | solution.py:500

commit v5 on v4

v5 whole, which is shorter than its diff:
```python
import functools

import jax
import jax.numpy as jnp
import numpy as np
from jax import lax
from jax.experimental import pallas as pl
from jax.experimental.pallas import tpu as pltpu
from jax.sharding import Mesh
from jax.sharding import PartitionSpec as P

BF = jnp.bfloat16
F32 = jnp.float32
ROW = ("xl", "z")
COL = ("xh", "y", "c")
CHIPS = ("xl", "z", "xh", "y")
GRID = (("xl", 2), ("z", 4), ("xh", 2), ("y", 4), ("c", 2))

C, CF, BANDS, TAPS = 512, 256, 4, 9
TR, TC = 128, 32
IR, IC = 32, 8
CELLS = IR * IC
PAIR = 2 * CELLS
HB = 32
NB = TR // HB
SIDE = 136
LATE = TAPS * 2 * 128 + 256
EARLY = 5 * 4 * 256 + 2 * 256
PACK = LATE + EARLY
PEERS = 64
SCALE = float(1024 * 512) ** (-0.5)
MIB = 1024 * 1024
GELU_A = 0.7978845608028654
GELU_B = 0.044715


def params(mib, grid=1):
    return pltpu.CompilerParams(
        vmem_limit_bytes=mib * MIB, dimension_semantics=("arbitrary",) * grid if grid else None
    )


def cost(flops, moved):
    return pl.CostEstimate(flops=flops, bytes_accessed=moved, transcendentals=0)


def whole(*shape):
    return pl.BlockSpec(shape, lambda i: (0,) * len(shape))


def dot(a, b, dims=((1,), (0,))):
    return lax.dot_general(a, b, (dims, ((), ())), preferred_element_type=F32)


def iotas(*shape):
    return tuple(lax.broadcasted_iota(jnp.int32, shape, n) for n in range(len(shape)))


def haar_matrix():
    row, col = iotas(256, 256)
    inside = ((row >> 3) & 7 == col >> 5) & (row & 7 == (col & 15) >> 1)
    flip = ((row >> 6) & col & 1) ^ ((row >> 7) & (col >> 4) & 1)
    return jnp.where(inside, 0.5 - flip.astype(F32), 0.0).astype(BF)


def pool_matrix():
    row, col = iotas(TAPS * IC, 6 * TC)
    tap, j = row >> 3, row & 7
    a = (tap >= 3).astype(jnp.int32) + (tap >= 6).astype(jnp.int32)
    u = (col >> 5) + a - 2
    v = (col & 31) + (tap - 3 * a) - 1 - 4 * j
    return ((u >= 0) & (u < 4) & (v >= 0) & (v < 4)).astype(F32).astype(BF)


def side_matrix():
    row, col = iotas(3 * IR, SIDE)
    u = col + (row >> 5) - 2 - 4 * (row & 31)
    return ((u >= 0) & (u < 4)).astype(F32).astype(BF)


def dcoarse_kernel(oc, rows, left, right, wconv, out, pooled):
    pool, side = pool_matrix(), side_matrix()
    for i in range(IR):
        if i == 0:
            block = jnp.concatenate([rows[0], oc[: 5 * TC, :]], axis=0)
        elif i == IR - 1:
            block = jnp.concatenate([oc[(4 * i - 1) * TC :, :], rows[1]], axis=0)
        else:
            block = oc[(4 * i - 1) * TC : (4 * i + 5) * TC, :]
        part = dot(pool, block)
        for t in range(TAPS):
            for h in range(2):
                pooled[t, h, i * IC : (i + 1) * IC, :] = part[t * IC : (t + 1) * IC, h * 128 : (h + 1) * 128]
    for edge, b, start in ((left, 2, 0), (right, 0, IC - 1)):
        part = dot(side, edge[...].astype(BF))
        for a in range(3):
            for h in range(2):
                cells = pl.ds(start, IR, stride=IC)
                pooled[3 * a + b, h, cells, :] += part[a * IR : (a + 1) * IR, h * 128 : (h + 1) * 128]
    total = jnp.zeros((CELLS, CF), F32)
    for t in range(TAPS):
        s = jnp.concatenate([pooled[t, 0], pooled[t, 1]], axis=-1).astype(BF)
        total += dot(s, wconv[t], ((1,), (1,)))
    out[...] = total.astype(BF)


def dcoarse_pass(oc, rows, left, right, wconv):
    vm = pl.BlockSpec(memory_space=pltpu.VMEM)
    return pl.pallas_call(
        dcoarse_kernel,
        in_specs=[vm] * 5,
        out_specs=vm,
        out_shape=jax.ShapeDtypeStruct((CELLS, CF), BF),
        scratch_shapes=[pltpu.VMEM((TAPS, 2, CELLS, 128), F32)],
        compiler_params=params(16, 0),
        cost_estimate=cost(1_000, 1_000),
        name="coarse_cotangent",
    )(oc.reshape(TR * TC, CF), rows, left, right, wconv)


def coarse_gradients(core, haar, x, wproj, sub, slope, hidden, dco, dtwin, out, both):
    own = pl.multiple_of(core[0] * IC, IC)
    both[:, pl.ds(own, IC), :] = dco[...].astype(F32).reshape(IR, IC, CF)
    both[:, pl.ds(IC - own, IC), :] = dtwin[...].astype(F32).reshape(IR, IC, CF)
    d = both[...].reshape(PAIR, CF).astype(BF)
    dpre = (dot(d, wproj[...], ((1,), (1,))) * slope[...]).astype(BF)
    dmix = [dot(haar, dpre[g * 256 : (g + 1) * 256]).astype(BF) for g in range(2)]
    half = pl.ds(pl.multiple_of(core[0] * 256, 256), 256)
    for k in range(5):
        if k < BANDS:
            dk = jnp.concatenate([dmix[g][k * 64 : (k + 1) * 64] for g in range(2)], axis=0)
            grad = dot(sub[k * 128 : (k + 1) * 128, half], dk, ((0,), (0,)))
        else:
            grad = dot(x[:, half], dpre, ((0,), (0,)))
        for n in range(4):
            out[(4 * k + n) * 256 : (4 * k + n + 1) * 256, :] = grad[:, n * 128 : (n + 1) * 128].astype(BF)
    grad = dot(hidden[:, half], d, ((0,), (0,)))
    for n in range(2):
        out[(20 + n) * 256 : (21 + n) * 256, :] = grad[:, n * 128 : (n + 1) * 128].astype(BF)


def forward_kernel(
    core, x_hbm, wb_hbm, wp_hbm, wj_hbm, fine_hbm, oc_hbm, dco, dtwin, rows, left, right,
    packed, conv_in, edges, keep, send,
    x, wband, wpoint, wproj, fine, oc, split, outs, up, ends, win, shifted, acc,
    sub, slope, hidden, early, both, sems,
):
    pairs = [(x_hbm, x)] + [(wb_hbm.at[k], wband.at[k]) for k in range(BANDS)]
    pairs += [(wp_hbm, wpoint), (wj_hbm, wproj), (fine_hbm, fine), (oc_hbm, oc)]
    loads = [pltpu.make_async_copy(src, dst, sems.at[n]) for n, (src, dst) in enumerate(pairs)]
    store = pltpu.make_async_copy(early, packed.at[pl.ds(LATE, EARLY)], sems.at[len(pairs)])

    for load in loads:
        load.start()
    haar = haar_matrix()
    loads[0].wait()
    parts = [dot(haar, x[g * 256 : (g + 1) * 256, :]).astype(BF) for g in range(2)]
    for k in range(BANDS):
        part = jnp.concatenate([p[k * 64 : (k + 1) * 64] for p in parts], axis=0)
        sub[k * 128 : (k + 1) * 128, :] = part
        loads[1 + k].wait()
        m = dot(part, wband[k])
        hi = m.astype(BF)
        lo = (m - hi.astype(F32)).astype(BF)
        for g in range(2):
            split[g, 0, k * 64 : (k + 1) * 64, :] = hi[g * 64 : (g + 1) * 64]
            split[g, 1, k * 64 : (k + 1) * 64, :] = lo[g * 64 : (g + 1) * 64]
    loads[5].wait()
    loads[6].wait()
    for g in range(2):
        cells = slice(g * 256, (g + 1) * 256)
        value = dot(haar, split[g, 0], ((0,), (0,))) + dot(haar, split[g, 1], ((0,), (0,)))
        value = value + dot(x[cells, :], wpoint[...])
        square = value * value
        th = jnp.tanh(GELU_A * (value + GELU_B * (value * square)))
        slope[cells, :] = 0.5 * (1.0 + th) + 0.5 * value * (1.0 - th * th) * (GELU_A * (1.0 + 3.0 * GELU_B * square))
        act = (0.5 * value * (1.0 + th)).astype(BF)
        hidden[cells, :] = act
        outs[g * 16 : (g + 1) * 16] = dot(act, wproj[...]).astype(BF).astype(F32).reshape(16, 16, CF)
    coarse_gradients(core, haar, x, wproj, sub, slope, hidden, dco, dtwin, early, both)
    store.start()
    loads[7].wait()
    loads[8].wait()

    def prepare(i):
        r0, slot = i * HB, i % 2
        for q in range(HB // 4):
            cell = outs[r0 // 4 + q, own, :]
            for s in range(4):
                up[slot, q, 0, pl.ds(s, IC, stride=4), :] = cell[:, :128]
                up[slot, q, 1, pl.ds(s, IC, stride=4), :] = cell[:, 128:]
            grown = jnp.concatenate([up[slot, q, 0], up[slot, q, 1]], axis=-1)
            for t in range(4):
                r = r0 + 4 * q + t
                value = fine[r].astype(F32) + grown
                fine[r] = value.astype(BF)
                ends[0, r : r + 1, :] = value[:1]
                ends[1, r : r + 1, :] = value[TC - 1 :]
        before = rows[0:1] if i == 0 else oc[r0 - 1 : r0]
        after = rows[1:2] if i == NB - 1 else oc[r0 + HB : r0 + HB + 1]
        fill_windows(r0, before, oc[r0 : r0 + HB], after, left, right, win.at[slot])
        for b in range(3):
            shifted[slot, :, :, b * CF : (b + 1) * CF] = win[slot, :, 9 - b : 9 - b + TC, :].astype(BF)

    def multiply(i):
        cells = fine[i * HB : (i + 1) * HB].reshape(HB * TC, CF).T
        for a in range(3):
            part = dot(cells, shifted[i % 2, 2 - a : 2 - a + HB].reshape(HB * TC, 3 * CF))
            acc[a] = part if i == 0 else acc[a] + part

    own = pl.ds(pl.multiple_of(core[0] * IC, IC), IC)
    prepare(0)
    for i in range(NB):
        if i + 1 < NB:
            prepare(i + 1)
        multiply(i)
    back = pltpu.make_async_copy(fine, conv_in, sems.at[len(pairs) + 1])
    back.start()
    edges[...] = ends[...].astype(BF)
    for out, c in ((keep, core[0]), (send, 1 - core[0])):
        half = pl.ds(pl.multiple_of(c * 128, 128), 128)
        for t in range(TAPS):
            for n in range(2):
                at = (t % 3) * CF + n * 128
                out[(2 * t + n) * 128 : (2 * t + n + 1) * 128, :] = acc[t // 3, half, at : at + 128].astype(BF)
        out[TAPS * 256 :, :] = jnp.zeros((LATE - TAPS * 256, 128), BF)
    store.wait()
    back.wait()


def forward_pass(core, x, wband, wpoint, wproj, fine, oc, dco, dtwin, rows, left, right):
    hbm, vm = pl.BlockSpec(memory_space=pltpu.HBM), pl.BlockSpec(memory_space=pltpu.VMEM)
    return pl.pallas_call(
        forward_kernel,
        in_specs=[pl.BlockSpec(memory_space=pltpu.SMEM)]
        + [hbm] * 6
        + [vm] * 5,
        out_specs=[hbm, hbm, vm, vm, vm],
        out_shape=[
            jax.ShapeDtypeStruct((PACK, 128), BF),
            jax.ShapeDtypeStruct((TR, TC, CF), BF),
            jax.ShapeDtypeStruct((2, TR, CF), BF),
            jax.ShapeDtypeStruct((LATE, 128), BF),
            jax.ShapeDtypeStruct((LATE, 128), BF),
        ],
        scratch_shapes=[
            pltpu.VMEM((PAIR, C), BF),
            pltpu.VMEM((BANDS, C, C), BF),
            pltpu.VMEM((C, C), BF),
            pltpu.VMEM((C, CF), BF),
            pltpu.VMEM((TR, TC, CF), BF),
            pltpu.VMEM((TR, TC, CF), BF),
            pltpu.VMEM((2, 2, 256, C), BF),
            pltpu.VMEM((IR, 2 * IC, CF), F32),
            pltpu.VMEM((2, HB // 4, 2, TC, 128), F32),
            pltpu.VMEM((2, TR, CF), F32),
            pltpu.VMEM((2, HB + 2, 48, CF), F32),
            pltpu.VMEM((2, HB + 2, TC, 3 * CF), BF),
            pltpu.VMEM((3, CF, 3 * CF), F32),
            pltpu.VMEM((PAIR, C), BF),
            pltpu.VMEM((PAIR, C), F32),
            pltpu.VMEM((PAIR, C), BF),
            pltpu.VMEM((EARLY, 128), BF),
            pltpu.VMEM((IR, 2 * IC, CF), F32),
            pltpu.SemaphoreType.DMA((11,)),
        ],
        compiler_params=params(56, 0),
        cost_estimate=cost(8_000_000_000, 14_000_000),
        name="forward_and_gradients",
    )(core, x, wband, wpoint, wproj, fine, oc, dco, dtwin, rows, left, right)


def window_specs():
    return [
        pl.BlockSpec((1, TC, CF), lambda i: (jnp.maximum(i * HB - 1, 0), 0, 0)),
        pl.BlockSpec((HB, TC, CF), lambda i: (i, 0, 0)),
        pl.BlockSpec((1, TC, CF), lambda i: (jnp.minimum(i * HB + HB, TR - 1), 0, 0)),
        whole(2, TC, CF),
        whole(SIDE, CF),
        whole(SIDE, CF),
    ]


def fill_windows(r0, before, tile, after, left, right, win):
    win[1 : HB + 1, 8 : 8 + TC, :] = tile.astype(F32)
    win[0:1, 8 : 8 + TC, :] = before.astype(F32)
    win[HB + 1 : HB + 2, 8 : 8 + TC, :] = after.astype(F32)
    for r in range(HB + 2):
        win[r, 7:8, :] = left[pl.ds(r0 + r, 1), :]
        win[r, 8 + TC : 9 + TC, :] = right[pl.ds(r0 + r, 1), :]


def conv_kernel(before, ci, after, rows, left, right, wconv, out, win, wide):
    i = pl.program_id(0)
    above = jnp.where(i == 0, rows[0:1], before[...])
    below = jnp.where(i == NB - 1, rows[1:2], after[...])
    fill_windows(i * HB, above, ci[...], below, left, right, win)
    for b in range(3):
        wide[:, :, b * CF : (b + 1) * CF] = win[:, 7 + b : 7 + b + TC, :].astype(BF)
    total = jnp.zeros((HB * TC, CF), F32)
    for a in range(3):
        total += dot(wide[a : a + HB].reshape(HB * TC, 3 * CF), wconv[a])
    out[...] = total.astype(BF).reshape(HB, TC, CF)


def conv_pass(ci, rows, left, right, wconv):
    return pl.pallas_call(
        conv_kernel,
        grid=(NB,),
        in_specs=window_specs() + [whole(3, 3 * CF, CF)],
        out_specs=pl.BlockSpec((HB, TC, CF), lambda i: (i, 0, 0)),
        out_shape=jax.ShapeDtypeStruct((TR, TC, CF), BF),
        scratch_shapes=[pltpu.VMEM((HB + 2, 48, CF), F32), pltpu.VMEM((HB + 2, TC, 3 * CF), BF)],
        compiler_params=params(16),
        cost_estimate=cost(1_000_000, 1_000_000),
        name="conv_forward",
    )(ci, ci, ci, rows, left, right, wconv.reshape(3, 3 * CF, CF))


def reduce_kernel(parts, out, held, copies, sems):
    n = PEERS // 8
    loads = [pltpu.make_async_copy(parts.at[pl.ds(g * n, n)], held.at[g], sems.at[g]) for g in range(8)]
    for load in loads:
        load.start()
    total = None
    for g in range(8):
        loads[g].wait()
        part = jnp.sum(held[g].astype(F32), axis=0)
        total = part if total is None else total + part
    done = (total * SCALE).astype(BF)
    for p in range(n):
        copies[p] = done
    stores = [pltpu.make_async_copy(copies, out.at[pl.ds(g * n, n)], sems.at[8 + g]) for g in range(8)]
    for store in stores:
        store.start()
    for store in stores:
        store.wait()


def reduce_pass(parts):
    n = PACK // PEERS
    hbm = pl.BlockSpec(memory_space=pltpu.HBM)
    return pl.pallas_call(
        reduce_kernel,
        in_specs=[hbm],
        out_specs=hbm,
        out_shape=jax.ShapeDtypeStruct((PEERS, n, 128), BF),
        scratch_shapes=[
            pltpu.VMEM((8, PEERS // 8, n, 128), BF),
            pltpu.VMEM((PEERS // 8, n, 128), BF),
            pltpu.SemaphoreType.DMA((16,)),
        ],
        compiler_params=params(56, 0),
        name="chip_sum",
    )(parts.reshape(PEERS, n, 128)).reshape(PACK, 128)


def place_kernel(core, half, *refs):
    conv, band, point, proj = refs[-4:]

    def place(out, n, start, cols):
        out[:, cols : cols + 128] = half[start : start + n, :].astype(F32)

    for t in range(TAPS):
        for n in range(2):
            place(conv.at[t], 128, (2 * t + n) * 128, 128 * n)
    for k in range(5):
        for n in range(4):
            place(band.at[k] if k < BANDS else point, 256, LATE + (4 * k + n) * 256, 128 * n)
    for n in range(2):
        place(proj, 256, LATE + (20 + n) * 256, 128 * n)


def place_half(core, half, before=()):
    any_ref = pl.BlockSpec(memory_space=pl.ANY)
    return pl.pallas_call(
        place_kernel,
        grid_spec=pltpu.PrefetchScalarGridSpec(
            num_scalar_prefetch=1,
            grid=(1,),
            in_specs=[pl.BlockSpec((PACK, 128), lambda i, c: (0, 0))] + [any_ref] * len(before),
            out_specs=[
                pl.BlockSpec((TAPS, 128, CF), lambda i, c: (0, c[0], 0)),
                pl.BlockSpec((BANDS, 256, C), lambda i, c: (0, c[0], 0)),
                pl.BlockSpec((256, C), lambda i, c: (c[0], 0)),
                pl.BlockSpec((256, CF), lambda i, c: (c[0], 0)),
            ],
        ),
        out_shape=[
            jax.ShapeDtypeStruct((TAPS, CF, CF), F32),
            jax.ShapeDtypeStruct((BANDS, C, C), F32),
            jax.ShapeDtypeStruct((C, C), F32),
            jax.ShapeDtypeStruct((C, CF), F32),
        ],
        input_output_aliases={2 + n: n for n in range(len(before))},
        compiler_params=params(16),
        cost_estimate=cost(0, 6_000_000),
        name="place_gradients",
    )(core, half, *before)


def shift(value, axes, count, step):
    pairs = [(i, i + step) for i in range(count) if 0 <= i + step < count]
    return lax.ppermute(value, axes, pairs)


def side_edges(first, last):
    lower = lax.axis_index("c") == 0
    twin = lax.ppermute(jnp.where(lower, last, first), "c", [(0, 1), (1, 0)])
    pairs = [(2 * k + 1, 2 * k + 2) for k in range(7)]
    pairs = pairs + [(b, a) for a, b in pairs]
    chip = lax.ppermute(jnp.where(lower, first, last), COL, pairs)
    return jnp.where(lower, chip, twin), jnp.where(lower, twin, chip)


def sides(corners, west, east):
    pad = jnp.zeros((SIDE - TR - 2, CF), BF)
    left = jnp.concatenate([corners[0], west, corners[2], pad], axis=0)
    right = jnp.concatenate([corners[1], east, corners[3], pad], axis=0)
    return left.astype(F32), right.astype(F32)


def row_halo(tile, west, east):
    low = jnp.concatenate([tile[TR - 1], west[TR - 1 :], east[TR - 1 :]], axis=0)
    high = jnp.concatenate([tile[0], west[:1], east[:1]], axis=0)
    even = lax.axis_index(ROW) % 2 == 0
    pairs = [(1, 2), (3, 4), (5, 6)]
    outer = lax.ppermute(jnp.where(even, high, low), ROW, pairs + [(b, a) for a, b in pairs])
    pairs = [(0, 1), (2, 3), (4, 5), (6, 7)]
    inner = lax.ppermute(jnp.where(even, low, high), ROW, pairs + [(b, a) for a, b in pairs])
    above, below = jnp.where(even, outer, inner), jnp.where(even, inner, outer)
    corners = [part for row in (above, below) for part in (row[TC : TC + 1], row[TC + 1 :])]
    return (jnp.stack([above[:TC], below[:TC]]),) + sides(corners, west, east)


def whole_halo(tile, first, last):
    lower = lax.axis_index("c") == 0
    inner, outer = jnp.where(lower, last, first), jnp.where(lower, first, last)
    twin = lax.ppermute(inner, "c", [(0, 1), (1, 0)])
    chips = [(2 * k + 1, 2 * k + 2) for k in range(7)]
    chips = chips + [(b, a) for a, b in chips]
    chip = lax.ppermute(outer, COL, chips)
    rows, far = [], []
    for down, at in ((1, TR - 1), (-1, 0)):
        rows.append(shift(jnp.concatenate([tile[at], twin[at : at + 1]], axis=0), ROW, 8, down))
        pairs = [(16 * r + a, 16 * (r + down) + b) for r in range(8) for a, b in chips if 0 <= r + down < 8]
        far.append(lax.ppermute(outer[at : at + 1], ROW + COL, pairs))
    west, east = jnp.where(lower, chip, twin), jnp.where(lower, twin, chip)
    corners = []
    for row, cell in zip(rows, far):
        near = row[TC:]
        corners += [jnp.where(lower, cell, near), jnp.where(lower, near, cell)]
    return (jnp.stack([row[:TC] for row in rows]),) + sides(corners, west, east)


def local(coarse_in, fine_in, band_weight, point_weight, proj_weight, conv_weight, out_cot):
    core = lax.axis_index("c").astype(jnp.int32).reshape(1)
    swap = [(0, 1), (1, 0)]

    chunks = coarse_in.reshape(2, 8, 16, C).transpose(1, 0, 2, 3)
    chunks = jnp.broadcast_to(chunks[:, None], (8, 2, 2, 16, C)).reshape(16, 2, 16, C)
    west, east = side_edges(out_cot[:, 0], out_cot[:, TC - 1])
    chunks, west, east = lax.optimization_barrier((chunks, west, east))
    cot_halo = row_halo(out_cot, west, east)
    x = lax.all_to_all(chunks, COL, 0, 0, tiled=True).reshape(PAIR, C)
    dco = dcoarse_pass(out_cot, *cot_halo, conv_weight)
    dtwin = lax.ppermute(dco, "c", swap)
    packed, conv_in, edges, keep, send = forward_pass(
        core, x, band_weight, point_weight, proj_weight, fine_in, out_cot, dco, dtwin, *cot_halo
    )
    got = lax.ppermute(send, "c", swap)
    late = (keep.astype(F32) + got.astype(F32)).astype(BF)
    packed = lax.dynamic_update_slice(packed, late, (0, 0))

    packed, conv_in, edges = lax.optimization_barrier((packed, conv_in, edges))
    parts = lax.all_to_all(packed, CHIPS, 0, 0, tiled=True)
    conv_halo = whole_halo(conv_in, edges[0], edges[1])
    spread = reduce_pass(parts)
    spread, conv_halo = lax.optimization_barrier((spread, conv_halo))
    mine = lax.all_to_all(spread, CHIPS, 0, 0, tiled=True)
    fine_out = conv_pass(conv_in, *conv_halo, conv_weight)
    mine, fine_out = lax.optimization_barrier((mine, fine_out))
    other = lax.ppermute(mine, "c", swap)
    grads = place_half(core, mine)
    grad_conv, grad_band, grad_point, grad_proj = place_half(1 - core, other, grads)
    return fine_out, grad_conv, grad_band, grad_point, grad_proj


def solution(mesh):
    fine_mesh = Mesh(
        np.asarray(mesh.devices).reshape([n for _, n in GRID]), tuple(name for name, _ in GRID)
    )
    fine = P(ROW, COL, None)
    in_specs = (P(ROW + COL, None, None), fine, P(), P(), P(), P(), fine)
    out_specs = (fine, P(), P(), P(), P())
    return jax.shard_map(local, mesh=fine_mesh, in_specs=in_specs, out_specs=out_specs, check_vma=False)
```

time: 150 us -> 139 us (0.927)
  local copies, waits for them, and re-layouts: 20.4 us -> 6.01 us
  waiting for transfers between devices: 31.6 us -> 42.1 us
  starting transfers between devices: 61.6 us -> 53 us
  Pallas kernels: 28.8 us -> 30.6 us
    unnamed x44 -> x24, local copies, waits for them, and re-layouts: 11.3 us -> 1.21 us
    all_to_all x1, starting transfers between devices: 14.5 us -> 5.87 us  [local(): parts = lax.all_to_all(packed, CHIPS, 0, 0, tiled=True)]
    all_to_all x1, waiting for transfers between devices: 0.01 us -> 7.7 us  [local(): x = lax.all_to_all(chunks, COL, 0, 0, tiled=True).reshape(PAIR, C)]
    ppermute x4 -> x2, starting transfers between devices: 12.2 us -> 6.73 us  [shift(): return lax.ppermute(value, axes, pairs)]
    ppermute x0 -> x2, starting transfers between devices: none -> 5.35 us  [the longest x1 4.68 us: row_halo(): lax.ppermute(jnp.where(even, low, high), ROW, pairs + [(b, a) for a, b in...]
    optimization_barrier x1 -> x0, local copies, waits for them, and re-layouts: 2.5 us -> none  [local(): packed, conv_in = lax.optimization_barrier((packed, conv_in))]
    dynamic_update_slice x0 -> x1, other arithmetic: none -> 2.09 us  [local(): packed = lax.dynamic_update_slice(packed, late, (0, 0))]
    ppermute x1, waiting for transfers between devices: 0.01 us -> 1.93 us  [local(): got = lax.ppermute(send, 'c', swap)]
  transfers between devices with their start and end apart: 16 -> 16, of which waited for: 6 -> 7; matrix products, arithmetic and copies ran while one was open for 4% -> 3% of each run, Pallas kernels for 9% -> 9%
where the time goes in v5:
time: 139 us; the launch traced here: 138 us
  starting transfers between devices  53 us (38%)
  waiting for transfers between devices  42.1 us (30%)
  Pallas kernels  30.6 us (22%)
  local copies, waits for them, and re-layouts  6.01 us (4%)
  other arithmetic  5.19 us (4%)
    all_to_all x1, waiting for transfers between devices, local(): mine = lax.all_to_all(spread, CHIPS, 0, 0, tiled=True)  19.8 us
    pallas_call x1, Pallas kernels, forward_pass(): pl.pallas_call(forward_kernel, in_specs=[pl.BlockSpec(memory_space=pltpu....  13.5 us
    all_to_all x1, starting transfers between devices, local(): mine = lax.all_to_all(spread, CHIPS, 0, 0, tiled=True)  10 us
    ppermute x1, waiting for transfers between devices, whole_halo(): chip = lax.ppermute(outer, COL, chips)  9.58 us
    all_to_all x1, starting transfers between devices, local(): x = lax.all_to_all(chunks, COL, 0, 0, tiled=True).reshape(PAIR, C)  8.49 us
    all_to_all x1, waiting for transfers between devices, local(): x = lax.all_to_all(chunks, COL, 0, 0, tiled=True).reshape(PAIR, C)  7.7 us
    pallas_call x1, Pallas kernels, conv_pass(): pl.pallas_call(conv_kernel, grid=(NB,), in_specs=window_specs() + [whole(...  6.74 us
    ppermute x2, starting transfers between devices, shift(): return lax.ppermute(value, axes, pairs)  6.73 us
  transfers between devices with their start and end apart: 16, of which 7 were waited for; matrix products, arithmetic and copies ran while one was open for 3% of the time, Pallas kernels for 9%

profile of v5, /device:TPU:1, one launch (start us, length us, event | category | flops | bytes accessed | tf_op | source)
XLA Modules:
  0.0 138.0 jit_solution(16232205372878818995)
XLA Ops:
  0.6 0.0 copy-start.2
  0.7 1.6 %fusion.1 = (bf16[128,1,256]{2,1,0:T(2,128)(2,1)S(1)}, bf16[128,1,256]{2,1,0:T(2,128)(2,1)S(1)}) fusion(bf16[128,32,256]{2,1,0:T(8,128)(2,1)} %oc_hbm.1), kind=kLoop, calls=%fused_computation.38 | loop fusion | bytes 262144 | tf_op jit(solution)/shard_map/slice | solution.py:462
  2.2 0.7 select_bitcast_fusion.1
  2.9 1.4 %collective-permute-start.1 = (bf16[128,256]{1,0:T(8,128)(2,1)}, bf16[128,256]{1,0:T(8,128)(2,1)S(1)}, u32[]{:S(2)}, u32[]{:S(2)}) collective-permute-start(bf16[128,256]{1,0:T(8,128)(2,1)} %get-tuple-element.61), channel_id=1, source_target_pairs={{0,1},{1,0},{2,3},{3,2},{4,5},{5,4},{6,7},{7,6},{8,9},{9,8},{10,11... | collective-permute-start | bytes 196616 | tf_op jit(solution)/shard_map/ppermute | solution.py:409
  4.3 3.2 %collective-permute-start = (bf16[128,256]{1,0:T(8,128)(2,1)}, bf16[128,256]{1,0:T(8,128)(2,1)S(1)}, u32[]{:S(2)}, u32[]{:S(2)}) collective-permute-start(bf16[128,256]{1,0:T(8,128)(2,1)} %get-tuple-element.62), channel_id=1, source_target_pairs={{1,2},{3,4},{5,6},{7,8},{9,10},{11,12},{13,14},{2,1},{4,3},{6,5},{... | collective-permute-start | bytes 196616 | tf_op jit(solution)/shard_map/ppermute | solution.py:412
  7.5 0.7 slice_bitcast_fusion.7
  8.2 1.0 copy.16
  9.2 0.9 collective-permute-done
  10.1 0.0 copy-start.8
  10.1 0.0 copy-start.9
  10.2 0.9 broadcast_in_dim.2
  11.1 0.7 collective-permute-start.2
  11.7 4.7 %collective-permute-start.3 = (bf16[34,256]{1,0:T(8,128)(2,1)S(1)}, bf16[34,256]{1,0:T(8,128)(2,1)S(1)}, u32[]{:S(2)}, u32[]{:S(2)}) collective-permute-start(bf16[34,256]{1,0:T(8,128)(2,1)S(1)} %get-tuple-element.80), channel_id=1, source_target_pairs={{0,16},{32,48},{64,80},{96,112},{16,0},{48,32},{80,64},{112,96},{1... | collective-permute-start | bytes 52232 | tf_op jit(solution)/shard_map/ppermute | solution.py:430
  16.4 0.6 pad.21.clone
  17.0 8.5 %all-to-all-start = ((bf16[16,2,16,512]{3,2,1,0:T(8,128)(2,1)}), bf16[16,2,16,512]{3,2,1,0:T(8,128)(2,1)}, u32[]{:S(2)}, u32[]{:S(2)}) async-start(bf16[16,2,16,512]{3,2,1,0:T(8,128)(2,1)} %bitcast.42), calls=%async_computation | async-start | bytes 1048576 | tf_op jit(solution)/shard_map/all_to_all | solution.py:465
  25.5 0.0 collective-permute-done.2
  25.5 0.0 collective-permute-done.3
  25.6 1.0 maximum_convert_fusion.1
  26.6 1.1 coarse_cotangent.1.dco
  27.8 0.2 collective-permute-start.4
  28.0 0.4 copy-done.7
  28.4 0.8 collective-permute-done.4.dtwin
  29.2 7.7 %all-to-all-done = bf16[16,2,16,512]{3,2,1,0:T(8,128)(2,1)} async-done(((bf16[16,2,16,512]{3,2,1,0:T(8,128)(2,1)}), bf16[16,2,16,512]{3,2,1,0:T(8,128)(2,1)}, u32[]{:S(2)}, u32[]{:S(2)}) %all-to-all-start) | async-done | bytes 524320 | tf_op jit(solution)/shard_map/all_to_all | solution.py:465
  36.9 13.5 %forward_and_gradients.1 = (bf16[8192,128]{1,0:T(8,128)(2,1)}, bf16[128,32,256]{2,1,0:T(8,128)(2,1)}, bf16[2,128,256]{2,1,0:T(8,128)(2,1)}, bf16[2560,128]{1,0:T(8,128)(2,1)}, bf16[2560,128]{1,0:T(8,128)(2,1)}) custom-call(s32[1]{0:T(128)} %bitcast.core, bf16[512,512]{1,0:T(8,128)(2,1)} %bitcast.6.x_hbm, bf16[4,512,512]{2,1,0:T(8,128)(2,1)} %wb_hbm.1, ...), custom_call_target="tpu_custom_call" | custom-call | flops 8000000000 | bytes 14000000 | tf_op jit(solution)/shard_map/forward_and_gradients/pallas_call | solution.py:233
  50.4 1.2 collective-permute-start.5
  51.6 1.9 %collective-permute-done.5 = bf16[2560,128]{1,0:T(8,128)(2,1)S(1)} collective-permute-done((bf16[2560,128]{1,0:T(8,128)(2,1)}, bf16[2560,128]{1,0:T(8,128)(2,1)S(1)}, u32[]{:S(2)}, u32[]{:S(2)}) %collective-permute-start.5) | collective-permute-done | bytes 655392 | tf_op jit(solution)/shard_map/ppermute | solution.py:471
  53.6 2.1 %fusion = bf16[8192,128]{1,0:T(8,128)(2,1)} fusion(bf16[8192,128]{1,0:T(8,128)(2,1)} %get-tuple-element.33, bf16[2560,128]{1,0:T(8,128)(2,1)S(1)} %collective-permute-done.5, bf16[2560,128]{1,0:T(8,128)(2,1)} %get-tuple-element.34), kind=kLoop, calls=%fused_computation.1 | loop fusion | flops 1310720 | bytes 1966080 | tf_op jit(solution)/shard_map/dynamic_update_slice | solution.py:473
  55.7 5.9 %all-to-all-start.1 = ((bf16[64,128,128]{2,1,0:T(8,128)(2,1)}), bf16[64,128,128]{2,1,0:T(8,128)(2,1)}, u32[]{:S(2)}, u32[]{:S(2)}) async-start(bf16[64,128,128]{2,1,0:T(8,128)(2,1)} %bitcast.41), calls=%async_computation.1 | async-start | bytes 4194304 | tf_op jit(solution)/shard_map/all_to_all | solution.py:476
  61.6 0.7 collective-permute-start.6
  62.3 3.9 %collective-permute-start.9 = (bf16[1,256]{1,0:T(2,128)(2,1)S(1)}, bf16[1,256]{1,0:T(2,128)(2,1)S(1)}, u32[]{:S(2)}, u32[]{:S(2)}) collective-permute-start(bf16[1,256]{1,0:T(2,128)(2,1)S(1)} %get-tuple-element.69), channel_id=1, source_target_pairs={{1,18},{3,20},{5,22},{7,24},{9,26},{11,28},{13,30},{2,17},{4,19},{... | collective-permute-start | bytes 1544 | tf_op jit(solution)/shard_map/ppermute | solution.py:447
  66.2 1.3 collective-permute-start.11
  67.5 2.6 %collective-permute-start.10 = (bf16[128,256]{1,0:T(8,128)(2,1)S(1)}, bf16[128,256]{1,0:T(8,128)(2,1)S(1)}, u32[]{:S(2)}, u32[]{:S(2)}) collective-permute-start(bf16[128,256]{1,0:T(8,128)(2,1)S(1)} %bitcast.44), channel_id=1, source_target_pairs={{1,2},{3,4},{5,6},{7,8},{9,10},{11,12},{13,14},{2,1},{4,3},{6,5},{... | collective-permute-start | bytes 196616 | tf_op jit(solution)/shard_map/ppermute | solution.py:442
  70.1 1.3 collective-permute-start.8
  71.4 5.4 %collective-permute-start.7 = (bf16[33,256]{1,0:T(8,128)(2,1)S(1)}, bf16[33,256]{1,0:T(8,128)(2,1)S(1)}, u32[]{:S(2)}, u32[]{:S(2)}) collective-permute-start(bf16[33,256]{1,0:T(8,128)(2,1)S(1)} %pad_maximum_fusion.4), channel_id=1, source_target_pairs={{0,16},{16,32},{32,48},{48,64},{64,80},{80,96},{96,112},{1,17},{17... | collective-permute-start | bytes 50696 | tf_op jit(solution)/shard_map/ppermute | solution.py:404
  76.9 9.6 %collective-permute-done.10 = bf16[128,256]{1,0:T(8,128)(2,1)S(1)} collective-permute-done((bf16[128,256]{1,0:T(8,128)(2,1)S(1)}, bf16[128,256]{1,0:T(8,128)(2,1)S(1)}, u32[]{:S(2)}, u32[]{:S(2)}) %collective-permute-start.10) | collective-permute-done | bytes 65568 | tf_op jit(solution)/shard_map/ppermute | solution.py:442
  86.5 0.6 pad_maximum_fusion.1.rows
  87.2 0.7 maximum_convert_fusion.3
  87.9 1.3 all-to-all-done.1.parts
  89.2 3.0 %chip_sum.1 = bf16[64,128,128]{2,1,0:T(8,128)(2,1)} custom-call(bf16[64,128,128]{2,1,0:T(8,128)(2,1)} %all-to-all-done.1.parts), custom_call_target="tpu_custom_call" | custom-call | tf_op jit(solution)/shard_map/chip_sum/pallas_call | solution.py:343
  92.2 10.0 %all-to-all-start.2 = ((bf16[64,128,128]{2,1,0:T(8,128)(2,1)}), bf16[64,128,128]{2,1,0:T(8,128)(2,1)}, u32[]{:S(2)}, u32[]{:S(2)}) async-start(bf16[64,128,128]{2,1,0:T(8,128)(2,1)} %chip_sum.1), calls=%async_computation.2 | async-start | bytes 4194304 | tf_op jit(solution)/shard_map/all_to_all | solution.py:480
  102.2 0.0 copy-start.5
  102.3 0.7 copy-done.5
  103.0 6.7 %conv_forward.1 = bf16[128,32,256]{2,1,0:T(8,128)(2,1)} custom-call(bf16[128,32,256]{2,1,0:T(8,128)(2,1)S(1)} %copy-done, bf16[128,32,256]{2,1,0:T(8,128)(2,1)S(1)} %copy-done, bf16[128,32,256]{2,1,0:T(8,128)(2,1)S(1)} %copy-done, bf16[2,32,256]{2,1,0:T(8,128)(2,1)S(1)} %copy-done.5, f32[136,256]{1,0:T(8,128)S(1)} %get-tuple-element.43.left, ...), custom_call_target="tpu_custom_call" | custom-call | flops 1000000 | bytes 1000000 | tf_op jit(solution)/shard_map/conv_forward/pallas_call | solution.py:307
  109.7 19.8 %all-to-all-done.2 = bf16[64,128,128]{2,1,0:T(8,128)(2,1)} async-done(((bf16[64,128,128]{2,1,0:T(8,128)(2,1)}), bf16[64,128,128]{2,1,0:T(8,128)(2,1)}, u32[]{:S(2)}, u32[]{:S(2)}) %all-to-all-start.2) | async-done | bytes 2097184 | tf_op jit(solution)/shard_map/all_to_all | solution.py:480
  129.5 2.1 %collective-permute-start.12 = (bf16[8192,128]{1,0:T(8,128)(2,1)}, bf16[8192,128]{1,0:T(8,128)(2,1)S(1)}, u32[]{:S(2)}, u32[]{:S(2)}) collective-permute-start(bf16[8192,128]{1,0:T(8,128)(2,1)} %bitcast.23.half), channel_id=1, source_target_pairs={{0,1},{1,0},{2,3},{3,2},{4,5},{5,4},{6,7},{7,6},{8,9},{9,8},{10,11... | collective-permute-start | bytes 6291464 | tf_op jit(solution)/shard_map/ppermute | solution.py:483
  131.6 3.9 %place_gradients.2 = (f32[9,256,256]{2,1,0:T(8,128)}, f32[4,512,512]{2,1,0:T(8,128)}, f32[512,512]{1,0:T(8,128)}, f32[512,256]{1,0:T(8,128)}) custom-call(s32[1]{0:T(128)} %bitcast.core, bf16[8192,128]{1,0:T(8,128)(2,1)} %bitcast.23.half), custom_call_target="tpu_custom_call" | custom-call | bytes 6000000 | tf_op jit(solution)/shard_map/place_gradients/pallas_call | solution.py:376
  135.6 0.0 collective-permute-done.12.half
  135.6 2.4 %place_gradients.3 = (f32[9,256,256]{2,1,0:T(8,128)}, f32[4,512,512]{2,1,0:T(8,128)}, f32[512,512]{1,0:T(8,128)}, f32[512,256]{1,0:T(8,128)}) custom-call(s32[1]{0:T(128)S(6)} %sub.3.core, bf16[8192,128]{1,0:T(8,128)(2,1)S(1)} %collective-permute-done.12.half, ...), custom_call_target="tpu_custom_call", output_to_operand_aliasing={{0}: (2, {}), {1}: (3, {}), {2}: (4, {}), {3}: (5, {})} | custom-call | bytes 6000000 | tf_op jit(solution)/shard_map/place_gradients/pallas_call | solution.py:376
  (45 shorter events, 0.2 us)
Async XLA Ops:
  0.6 26.0 %copy-start.1 = (bf16[9,256,256]{2,1,0:T(8,128)(2,1)S(1)}, bf16[9,256,256]{2,1,0:T(8,128)(2,1)}, u32[]{:S(2)}) copy-start(bf16[9,256,256]{2,1,0:T(8,128)(2,1)} %wconv.1) | copy-start | bytes 3538948
  0.6 26.0 %copy-start.2 = (bf16[128,32,256]{2,1,0:T(8,128)(2,1)S(1)}, bf16[128,32,256]{2,1,0:T(8,128)(2,1)}, u32[]{:S(2)}) copy-start(bf16[128,32,256]{2,1,0:T(8,128)(2,1)} %oc_hbm.1) | copy-start | bytes 6291460
  2.9 6.3 %collective-permute-start.1 = (bf16[128,256]{1,0:T(8,128)(2,1)}, bf16[128,256]{1,0:T(8,128)(2,1)S(1)}, u32[]{:S(2)}, u32[]{:S(2)}) collective-permute-start(bf16[128,256]{1,0:T(8,128)(2,1)} %get-tuple-element.61), channel_id=1, source_target_pairs={{0,1},{1,0},{2,3},{3,2},{4,5},{5,4},{6,7},{7,6},{8,9},{9,8},{10,11... | collective-permute-start | bytes 196616 | tf_op jit(solution)/shard_map/ppermute | solution.py:409
  4.3 5.8 %collective-permute-start = (bf16[128,256]{1,0:T(8,128)(2,1)}, bf16[128,256]{1,0:T(8,128)(2,1)S(1)}, u32[]{:S(2)}, u32[]{:S(2)}) collective-permute-start(bf16[128,256]{1,0:T(8,128)(2,1)} %get-tuple-element.62), channel_id=1, source_target_pairs={{1,2},{3,4},{5,6},{7,8},{9,10},{11,12},{13,14},{2,1},{4,3},{6,5},{... | collective-permute-start | bytes 196616 | tf_op jit(solution)/shard_map/ppermute | solution.py:412
  10.1 0.9 copy-start.8
  10.1 0.9 copy-start.9
  11.1 14.5 %collective-permute-start.2 = (bf16[34,256]{1,0:T(8,128)(2,1)S(1)}, bf16[34,256]{1,0:T(8,128)(2,1)S(1)}, u32[]{:S(2)}, u32[]{:S(2)}) collective-permute-start(bf16[34,256]{1,0:T(8,128)(2,1)S(1)} %get-tuple-element.79), channel_id=1, source_target_pairs={{16,32},{48,64},{80,96},{32,16},{64,48},{96,80},{17,33},{49,65},{8... | collective-permute-start | bytes 52232 | tf_op jit(solution)/shard_map/ppermute | solution.py:428
  11.7 13.8 %collective-permute-start.3 = (bf16[34,256]{1,0:T(8,128)(2,1)S(1)}, bf16[34,256]{1,0:T(8,128)(2,1)S(1)}, u32[]{:S(2)}, u32[]{:S(2)}) collective-permute-start(bf16[34,256]{1,0:T(8,128)(2,1)S(1)} %get-tuple-element.80), channel_id=1, source_target_pairs={{0,16},{32,48},{64,80},{96,112},{16,0},{48,32},{80,64},{112,96},{1... | collective-permute-start | bytes 52232 | tf_op jit(solution)/shard_map/ppermute | solution.py:430
  17.0 19.9 %all-to-all-start = ((bf16[16,2,16,512]{3,2,1,0:T(8,128)(2,1)}), bf16[16,2,16,512]{3,2,1,0:T(8,128)(2,1)}, u32[]{:S(2)}, u32[]{:S(2)}) async-start(bf16[16,2,16,512]{3,2,1,0:T(8,128)(2,1)} %bitcast.42), calls=%async_computation | async-start | bytes 1048576 | tf_op jit(solution)/shard_map/all_to_all | solution.py:465
  25.6 2.2 %copy-start.6 = (bf16[2,32,256]{2,1,0:T(8,128)(2,1)}, bf16[2,32,256]{2,1,0:T(8,128)(2,1)S(1)}, u32[]{:S(2)}) copy-start(bf16[2,32,256]{2,1,0:T(8,128)(2,1)S(1)} %pad_maximum_fusion.rows) | copy-start | bytes 98308
  26.6 10.3 %copy-start.3 = (f32[136,256]{1,0:T(8,128)}, f32[136,256]{1,0:T(8,128)S(1)}, u32[]{:S(2)}) copy-start(f32[136,256]{1,0:T(8,128)S(1)} %get-tuple-element.91.right) | copy-start | bytes 417796
  26.6 10.3 %copy-start.4 = (f32[136,256]{1,0:T(8,128)}, f32[136,256]{1,0:T(8,128)S(1)}, u32[]{:S(2)}) copy-start(f32[136,256]{1,0:T(8,128)S(1)} %get-tuple-element.92.left) | copy-start | bytes 417796
  27.8 0.6 copy-start.7
  27.8 1.4 %collective-permute-start.4 = (bf16[256,256]{1,0:T(8,128)(2,1)S(1)}, bf16[256,256]{1,0:T(8,128)(2,1)S(1)}, u32[]{:S(2)}, u32[]{:S(2)}) collective-permute-start(bf16[256,256]{1,0:T(8,128)(2,1)S(1)} %coarse_cotangent.1.dco), channel_id=1, source_target_pairs={{0,1},{1,0},{2,3},{3,2},{4,5},{5,4},{6,7},{7,6},{8,9},{9,8},{10,11... | collective-permute-start | bytes 393224 | tf_op jit(solution)/shard_map/ppermute | solution.py:467
  29.2 7.7 %copy-start.11 = (bf16[256,256]{1,0:T(8,128)(2,1)}, bf16[256,256]{1,0:T(8,128)(2,1)S(1)}, u32[]{:S(2)}) copy-start(bf16[256,256]{1,0:T(8,128)(2,1)S(1)} %collective-permute-done.4.dtwin) | copy-start | bytes 393220
  50.4 3.2 %collective-permute-start.5 = (bf16[2560,128]{1,0:T(8,128)(2,1)}, bf16[2560,128]{1,0:T(8,128)(2,1)S(1)}, u32[]{:S(2)}, u32[]{:S(2)}) collective-permute-start(bf16[2560,128]{1,0:T(8,128)(2,1)} %get-tuple-element.35), channel_id=1, source_target_pairs={{0,1},{1,0},{2,3},{3,2},{4,5},{5,4},{6,7},{7,6},{8,9},{9,8},{10,11... | collective-permute-start | bytes 1966088 | tf_op jit(solution)/shard_map/ppermute | solution.py:471
  55.7 5.9 %copy-start = (bf16[128,32,256]{2,1,0:T(8,128)(2,1)S(1)}, bf16[128,32,256]{2,1,0:T(8,128)(2,1)}, u32[]{:S(2)}) copy-start(bf16[128,32,256]{2,1,0:T(8,128)(2,1)} %get-tuple-element.39.before.ci.after) | copy-start | bytes 6291460
  55.7 5.9 %copy-start.10 = (bf16[2,128,256]{2,1,0:T(8,128)(2,1)S(1)}, bf16[2,128,256]{2,1,0:T(8,128)(2,1)}, u32[]{:S(2)}) copy-start(bf16[2,128,256]{2,1,0:T(8,128)(2,1)} %get-tuple-element.40) | copy-start | bytes 393220
  55.7 33.5 %all-to-all-start.1 = ((bf16[64,128,128]{2,1,0:T(8,128)(2,1)}), bf16[64,128,128]{2,1,0:T(8,128)(2,1)}, u32[]{:S(2)}, u32[]{:S(2)}) async-start(bf16[64,128,128]{2,1,0:T(8,128)(2,1)} %bitcast.41), calls=%async_computation.1 | async-start | bytes 4194304 | tf_op jit(solution)/shard_map/all_to_all | solution.py:476
  61.6 8.5 %collective-permute-start.6 = (bf16[128,256]{1,0:T(8,128)(2,1)S(1)}, bf16[128,256]{1,0:T(8,128)(2,1)S(1)}, u32[]{:S(2)}, u32[]{:S(2)}) collective-permute-start(bf16[128,256]{1,0:T(8,128)(2,1)S(1)} %get-tuple-element.66), channel_id=1, source_target_pairs={{0,1},{1,0},{2,3},{3,2},{4,5},{5,4},{6,7},{7,6},{8,9},{9,8},{10,11... | collective-permute-start | bytes 196616 | tf_op jit(solution)/shard_map/ppermute | solution.py:439
  62.3 24.9 %collective-permute-start.9 = (bf16[1,256]{1,0:T(2,128)(2,1)S(1)}, bf16[1,256]{1,0:T(2,128)(2,1)S(1)}, u32[]{:S(2)}, u32[]{:S(2)}) collective-permute-start(bf16[1,256]{1,0:T(2,128)(2,1)S(1)} %get-tuple-element.69), channel_id=1, source_target_pairs={{1,18},{3,20},{5,22},{7,24},{9,26},{11,28},{13,30},{2,17},{4,19},{... | collective-permute-start | bytes 1544 | tf_op jit(solution)/shard_map/ppermute | solution.py:447
  66.2 20.3 %collective-permute-start.11 = (bf16[1,256]{1,0:T(2,128)(2,1)S(1)}, bf16[1,256]{1,0:T(2,128)(2,1)S(1)}, u32[]{:S(2)}, u32[]{:S(2)}) collective-permute-start(bf16[1,256]{1,0:T(2,128)(2,1)S(1)} %get-tuple-element.70), channel_id=1, source_target_pairs={{17,2},{19,4},{21,6},{23,8},{25,10},{27,12},{29,14},{18,1},{20,3},... | collective-permute-start | bytes 1544 | tf_op jit(solution)/shard_map/ppermute | solution.py:447
  67.5 18.9 %collective-permute-start.10 = (bf16[128,256]{1,0:T(8,128)(2,1)S(1)}, bf16[128,256]{1,0:T(8,128)(2,1)S(1)}, u32[]{:S(2)}, u32[]{:S(2)}) collective-permute-start(bf16[128,256]{1,0:T(8,128)(2,1)S(1)} %bitcast.44), channel_id=1, source_target_pairs={{1,2},{3,4},{5,6},{7,8},{9,10},{11,12},{13,14},{2,1},{4,3},{6,5},{... | collective-permute-start | bytes 196616 | tf_op jit(solution)/shard_map/ppermute | solution.py:442
  70.1 16.4 %collective-permute-start.8 = (bf16[33,256]{1,0:T(8,128)(2,1)S(1)}, bf16[33,256]{1,0:T(8,128)(2,1)S(1)}, u32[]{:S(2)}, u32[]{:S(2)}) collective-permute-start(bf16[33,256]{1,0:T(8,128)(2,1)S(1)} %pad_maximum_fusion.5), channel_id=1, source_target_pairs={{16,0},{32,16},{48,32},{64,48},{80,64},{96,80},{112,96},{17,1},{33... | collective-permute-start | bytes 50696 | tf_op jit(solution)/shard_map/ppermute | solution.py:404
  71.4 15.1 %collective-permute-start.7 = (bf16[33,256]{1,0:T(8,128)(2,1)S(1)}, bf16[33,256]{1,0:T(8,128)(2,1)S(1)}, u32[]{:S(2)}, u32[]{:S(2)}) collective-permute-start(bf16[33,256]{1,0:T(8,128)(2,1)S(1)} %pad_maximum_fusion.4), channel_id=1, source_target_pairs={{0,16},{16,32},{32,48},{48,64},{64,80},{80,96},{96,112},{1,17},{17... | collective-permute-start | bytes 50696 | tf_op jit(solution)/shard_map/ppermute | solution.py:404
  92.2 37.4 %all-to-all-start.2 = ((bf16[64,128,128]{2,1,0:T(8,128)(2,1)}), bf16[64,128,128]{2,1,0:T(8,128)(2,1)}, u32[]{:S(2)}, u32[]{:S(2)}) async-start(bf16[64,128,128]{2,1,0:T(8,128)(2,1)} %chip_sum.1), calls=%async_computation.2 | async-start | bytes 4194304 | tf_op jit(solution)/shard_map/all_to_all | solution.py:480
  102.2 0.8 copy-start.5
  129.5 6.1 %collective-permute-start.12 = (bf16[8192,128]{1,0:T(8,128)(2,1)}, bf16[8192,128]{1,0:T(8,128)(2,1)S(1)}, u32[]{:S(2)}, u32[]{:S(2)}) collective-permute-start(bf16[8192,128]{1,0:T(8,128)(2,1)} %bitcast.23.half), channel_id=1, source_target_pairs={{0,1},{1,0},{2,3},{3,2},{4,5},{5,4},{6,7},{7,6},{8,9},{9,8},{10,11... | collective-permute-start | bytes 6291464 | tf_op jit(solution)/shard_map/ppermute | solution.py:483

commit v6 on v5

--- a/solution.py
+++ b/solution.py
@@ -120,9 +120,9 @@
 
 def coarse_gradients(core, haar, x, wproj, sub, slope, hidden, dco, dtwin, out, both):
     own = pl.multiple_of(core[0] * IC, IC)
-    both[:, pl.ds(own, IC), :] = dco[...].astype(F32).reshape(IR, IC, CF)
-    both[:, pl.ds(IC - own, IC), :] = dtwin[...].astype(F32).reshape(IR, IC, CF)
-    d = both[...].reshape(PAIR, CF).astype(BF)
+    both[:, :, :, pl.ds(own, IC), :] = dco[...].astype(F32).reshape(8, 2, 2, IC, CF)
+    both[:, :, :, pl.ds(IC - own, IC), :] = dtwin[...].astype(F32).reshape(8, 2, 2, IC, CF)
+    d = jnp.concatenate([both[:, g].reshape(CELLS, CF) for g in range(2)], axis=0).astype(BF)
     dpre = (dot(d, wproj[...], ((1,), (1,))) * slope[...]).astype(BF)
     dmix = [dot(haar, dpre[g * 256 : (g + 1) * 256]).astype(BF) for g in range(2)]
     half = pl.ds(pl.multiple_of(core[0] * 256, 256), 256)
@@ -140,20 +140,23 @@
 
 
 def forward_kernel(
-    core, x_hbm, wb_hbm, wp_hbm, wj_hbm, fine_hbm, oc_hbm, dco, dtwin, rows, left, right,
+    core, x_hbm, xtwin_hbm, wb_hbm, wp_hbm, wj_hbm, fine_hbm, oc_hbm, dco, dtwin, rows, left, right,
     packed, conv_in, edges, keep, send,
     x, wband, wpoint, wproj, fine, oc, split, outs, up, ends, win, shifted, acc,
     sub, slope, hidden, early, both, sems,
 ):
-    pairs = [(x_hbm, x)] + [(wb_hbm.at[k], wband.at[k]) for k in range(BANDS)]
+    at = pl.multiple_of(core[0] * CELLS, CELLS)
+    pairs = [(x_hbm, x.at[pl.ds(at, CELLS)])] + [(wb_hbm.at[k], wband.at[k]) for k in range(BANDS)]
     pairs += [(wp_hbm, wpoint), (wj_hbm, wproj), (fine_hbm, fine), (oc_hbm, oc)]
+    pairs += [(xtwin_hbm, x.at[pl.ds(CELLS - at, CELLS)])]
     loads = [pltpu.make_async_copy(src, dst, sems.at[n]) for n, (src, dst) in enumerate(pairs)]
     store = pltpu.make_async_copy(early, packed.at[pl.ds(LATE, EARLY)], sems.at[len(pairs)])
 
-    for load in loads:
+    for load in loads[:1] + loads[-1:] + loads[1:-1]:
         load.start()
     haar = haar_matrix()
     loads[0].wait()
+    loads[-1].wait()
     parts = [dot(haar, x[g * 256 : (g + 1) * 256, :]).astype(BF) for g in range(2)]
     for k in range(BANDS):
         part = jnp.concatenate([p[k * 64 : (k + 1) * 64] for p in parts], axis=0)
@@ -176,7 +179,7 @@
         slope[cells, :] = 0.5 * (1.0 + th) + 0.5 * value * (1.0 - th * th) * (GELU_A * (1.0 + 3.0 * GELU_B * square))
         act = (0.5 * value * (1.0 + th)).astype(BF)
         hidden[cells, :] = act
-        outs[g * 16 : (g + 1) * 16] = dot(act, wproj[...]).astype(BF).astype(F32).reshape(16, 16, CF)
+        outs[:, g] = dot(act, wproj[...]).astype(BF).astype(F32).reshape(8, 2, 16, CF)
     coarse_gradients(core, haar, x, wproj, sub, slope, hidden, dco, dtwin, early, both)
     store.start()
     loads[7].wait()
@@ -185,7 +188,8 @@
     def prepare(i):
         r0, slot = i * HB, i % 2
         for q in range(HB // 4):
-            cell = outs[r0 // 4 + q, own, :]
+            at = r0 // 4 + q
+            cell = outs[at // 4, at // 2 % 2, at % 2, own, :]
             for s in range(4):
                 up[slot, q, 0, pl.ds(s, IC, stride=4), :] = cell[:, :128]
                 up[slot, q, 1, pl.ds(s, IC, stride=4), :] = cell[:, 128:]
@@ -228,12 +232,12 @@
     back.wait()
 
 
-def forward_pass(core, x, wband, wpoint, wproj, fine, oc, dco, dtwin, rows, left, right):
+def forward_pass(core, x, xtwin, wband, wpoint, wproj, fine, oc, dco, dtwin, rows, left, right):
     hbm, vm = pl.BlockSpec(memory_space=pltpu.HBM), pl.BlockSpec(memory_space=pltpu.VMEM)
     return pl.pallas_call(
         forward_kernel,
         in_specs=[pl.BlockSpec(memory_space=pltpu.SMEM)]
-        + [hbm] * 6
+        + [hbm] * 7
         + [vm] * 5,
         out_specs=[hbm, hbm, vm, vm, vm],
         out_shape=[
@@ -251,7 +255,7 @@
             pltpu.VMEM((TR, TC, CF), BF),
             pltpu.VMEM((TR, TC, CF), BF),
             pltpu.VMEM((2, 2, 256, C), BF),
-            pltpu.VMEM((IR, 2 * IC, CF), F32),
+            pltpu.VMEM((8, 2, 2, 2 * IC, CF), F32),
             pltpu.VMEM((2, HB // 4, 2, TC, 128), F32),
             pltpu.VMEM((2, TR, CF), F32),
             pltpu.VMEM((2, HB + 2, 48, CF), F32),
@@ -261,13 +265,13 @@
             pltpu.VMEM((PAIR, C), F32),
             pltpu.VMEM((PAIR, C), BF),
             pltpu.VMEM((EARLY, 128), BF),
-            pltpu.VMEM((IR, 2 * IC, CF), F32),
-            pltpu.SemaphoreType.DMA((11,)),
+            pltpu.VMEM((8, 2, 2, 2 * IC, CF), F32),
+            pltpu.SemaphoreType.DMA((12,)),
         ],
         compiler_params=params(56, 0),
         cost_estimate=cost(8_000_000_000, 14_000_000),
         name="forward_and_gradients",
-    )(core, x, wband, wpoint, wproj, fine, oc, dco, dtwin, rows, left, right)
+    )(core, x, xtwin, wband, wpoint, wproj, fine, oc, dco, dtwin, rows, left, right)
 
 
 def window_specs():
@@ -458,15 +462,15 @@
     swap = [(0, 1), (1, 0)]
 
     chunks = coarse_in.reshape(2, 8, 16, C).transpose(1, 0, 2, 3)
-    chunks = jnp.broadcast_to(chunks[:, None], (8, 2, 2, 16, C)).reshape(16, 2, 16, C)
     west, east = side_edges(out_cot[:, 0], out_cot[:, TC - 1])
     chunks, west, east = lax.optimization_barrier((chunks, west, east))
     cot_halo = row_halo(out_cot, west, east)
-    x = lax.all_to_all(chunks, COL, 0, 0, tiled=True).reshape(PAIR, C)
+    x = lax.all_to_all(chunks, ("xh", "y"), 0, 0, tiled=True).reshape(CELLS, C)
     dco = dcoarse_pass(out_cot, *cot_halo, conv_weight)
-    dtwin = lax.ppermute(dco, "c", swap)
+    x, dco = lax.optimization_barrier((x, dco))
+    xtwin, dtwin = lax.ppermute(x, "c", swap), lax.ppermute(dco, "c", swap)
     packed, conv_in, edges, keep, send = forward_pass(
-        core, x, band_weight, point_weight, proj_weight, fine_in, out_cot, dco, dtwin, *cot_halo
+        core, x, xtwin, band_weight, point_weight, proj_weight, fine_in, out_cot, dco, dtwin, *cot_halo
     )
     got = lax.ppermute(send, "c", swap)
     late = (keep.astype(F32) + got.astype(F32)).astype(BF)

time: 139 us -> 136 us (0.978)
  waiting for transfers between devices: 42.1 us -> 38.4 us
  other arithmetic: 5.19 us -> 3.71 us
    all_to_all x1, waiting for transfers between devices: 7.7 us -> 4.53 us  [local(): x = lax.all_to_all(chunks, ('xh', 'y'), 0, 0, tiled=True).reshape(CELLS, C)]
    unnamed x24 -> x26, local copies, waits for them, and re-layouts: 1.21 us -> 3.16 us
    ppermute x1 -> x2, starting transfers between devices: 0.23 us -> 2.1 us  [local(): xtwin, dtwin = (lax.ppermute(x, 'c', swap), lax.ppermute(dco, 'c', swap))]
    reshape x0 -> x1, local copies, waits for them, and re-layouts: none -> 1.67 us  [local(): chunks = coarse_in.reshape(2, 8, 16, C).transpose(1, 0, 2, 3)]
  transfers between devices with their start and end apart: 16 -> 17, of which waited for: 7 -> 6; matrix products, arithmetic and copies ran while one was open for 3% -> 3% of each run, Pallas kernels for 9% -> 9%
where the time goes in v6:
time: 136 us; the launch traced here: 135 us
  starting transfers between devices  54 us (40%)
  waiting for transfers between devices  38.4 us (28%)
  Pallas kernels  30.6 us (22%)
  local copies, waits for them, and re-layouts  7.21 us (5%)
  other arithmetic  3.71 us (3%)
    all_to_all x1, waiting for transfers between devices, local(): mine = lax.all_to_all(spread, CHIPS, 0, 0, tiled=True)  19.8 us
    pallas_call x1, Pallas kernels, forward_pass(): pl.pallas_call(forward_kernel, in_specs=[pl.BlockSpec(memory_space=pltpu....  13.5 us
    all_to_all x1, starting transfers between devices, local(): mine = lax.all_to_all(spread, CHIPS, 0, 0, tiled=True)  10.2 us
    ppermute x1, waiting for transfers between devices, whole_halo(): chip = lax.ppermute(outer, COL, chips)  9.5 us
    all_to_all x1, starting transfers between devices, local(): x = lax.all_to_all(chunks, ('xh', 'y'), 0, 0, tiled=True).reshape(CELLS, C)  7.62 us
    pallas_call x1, Pallas kernels, conv_pass(): pl.pallas_call(conv_kernel, grid=(NB,), in_specs=window_specs() + [whole(...  6.73 us
    ppermute x2, starting transfers between devices, shift(): return lax.ppermute(value, axes, pairs)  6.73 us
    all_to_all x1, starting transfers between devices, local(): parts = lax.all_to_all(packed, CHIPS, 0, 0, tiled=True)  6.37 us
  transfers between devices with their start and end apart: 17, of which 6 were waited for; matrix products, arithmetic and copies ran while one was open for 3% of the time, Pallas kernels for 9%

profile of v6, /device:TPU:1, one launch (start us, length us, event | category | flops | bytes accessed | tf_op | source)
XLA Modules:
  0.0 134.9 jit_solution(13105116313253313487)
XLA Ops:
  0.6 1.5 %fusion.1 = (bf16[128,1,256]{2,1,0:T(2,128)(2,1)S(1)}, bf16[128,1,256]{2,1,0:T(2,128)(2,1)S(1)}) fusion(bf16[128,32,256]{2,1,0:T(8,128)(2,1)} %oc_hbm.1), kind=kLoop, calls=%fused_computation.39 | loop fusion | bytes 262144 | tf_op jit(solution)/shard_map/slice | solution.py:465
  2.2 1.5 %collective-permute-start.1 = (bf16[128,256]{1,0:T(8,128)(2,1)S(1)}, bf16[128,256]{1,0:T(8,128)(2,1)S(1)}, u32[]{:S(2)}, u32[]{:S(2)}) collective-permute-start(bf16[128,256]{1,0:T(8,128)(2,1)S(1)} %get-tuple-element.65), channel_id=1, source_target_pairs={{0,1},{1,0},{2,3},{3,2},{4,5},{5,4},{6,7},{7,6},{8,9},{9,8},{10,11... | collective-permute-start | bytes 196616 | tf_op jit(solution)/shard_map/ppermute | solution.py:413
  3.7 3.2 %collective-permute-start = (bf16[128,256]{1,0:T(8,128)(2,1)S(1)}, bf16[128,256]{1,0:T(8,128)(2,1)S(1)}, u32[]{:S(2)}, u32[]{:S(2)}) collective-permute-start(bf16[128,256]{1,0:T(8,128)(2,1)S(1)} %get-tuple-element.66), channel_id=1, source_target_pairs={{1,2},{3,4},{5,6},{7,8},{9,10},{11,12},{13,14},{2,1},{4,3},{6,5},{... | collective-permute-start | bytes 196616 | tf_op jit(solution)/shard_map/ppermute | solution.py:416
  6.9 0.7 slice_bitcast_fusion.7
  7.6 1.7 %copy.26 = bf16[2,8,16,512]{3,2,0,1:T(8,128)(2,1)} copy(bf16[2,8,16,512]{3,2,1,0:T(8,128)(2,1)} %bitcast.42) | data formatting | bytes 524288 | tf_op jit(solution)/shard_map/reshape | solution.py:464
  9.3 0.0 collective-permute-done.1
  9.3 0.0 collective-permute-done
  9.4 0.7 collective-permute-start.2
  10.0 4.6 %collective-permute-start.3 = (bf16[34,256]{1,0:T(8,128)(2,1)S(1)}, bf16[34,256]{1,0:T(8,128)(2,1)S(1)}, u32[]{:S(2)}, u32[]{:S(2)}) collective-permute-start(bf16[34,256]{1,0:T(8,128)(2,1)S(1)} %get-tuple-element.84), channel_id=1, source_target_pairs={{0,16},{32,48},{64,80},{96,112},{16,0},{48,32},{80,64},{112,96},{1... | collective-permute-start | bytes 52232 | tf_op jit(solution)/shard_map/ppermute | solution.py:434
  14.7 0.1 pad.21.clone
  14.8 7.6 %all-to-all-start = ((bf16[8,2,16,512]{3,2,1,0:T(8,128)(2,1)}), bf16[8,2,16,512]{3,2,1,0:T(8,128)(2,1)S(1)}, u32[]{:S(2)}, u32[]{:S(2)}) async-start(bf16[8,2,16,512]{3,2,1,0:T(8,128)(2,1)} %bitcast.38), calls=%async_computation | async-start | bytes 524288 | tf_op jit(solution)/shard_map/all_to_all | solution.py:468
  22.4 0.0 collective-permute-done.2
  22.5 0.1 maximum_convert_fusion.1
  22.6 0.0 copy-start.2
  22.6 1.7 %copy-done.2 = bf16[128,32,256]{2,1,0:T(8,128)(2,1)S(1)} copy-done((bf16[128,32,256]{2,1,0:T(8,128)(2,1)S(1)}, bf16[128,32,256]{2,1,0:T(8,128)(2,1)}, u32[]{:S(2)}) %copy-start.2) | copy-done | bytes 2097176
  24.3 1.1 coarse_cotangent.1.dco
  25.4 4.5 %all-to-all-done = bf16[8,2,16,512]{3,2,1,0:T(8,128)(2,1)S(1)} async-done(((bf16[8,2,16,512]{3,2,1,0:T(8,128)(2,1)}), bf16[8,2,16,512]{3,2,1,0:T(8,128)(2,1)S(1)}, u32[]{:S(2)}, u32[]{:S(2)}) %all-to-all-start) | async-done | bytes 262176 | tf_op jit(solution)/shard_map/all_to_all | solution.py:468
  30.0 2.1 %collective-permute-start.4 = (bf16[256,512]{1,0:T(8,128)(2,1)S(1)}, bf16[256,512]{1,0:T(8,128)(2,1)S(1)}, u32[]{:S(2)}, u32[]{:S(2)}) collective-permute-start(bf16[256,512]{1,0:T(8,128)(2,1)S(1)} %bitcast.43), channel_id=1, source_target_pairs={{0,1},{1,0},{2,3},{3,2},{4,5},{5,4},{6,7},{7,6},{8,9},{9,8},{10,11... | collective-permute-start | bytes 786440 | tf_op jit(solution)/shard_map/ppermute | solution.py:471
  32.1 0.0 collective-permute-start.5
  32.1 1.3 collective-permute-done.5.dtwin
  33.4 0.0 collective-permute-done.4.xtwin_hbm
  33.5 0.6 copy-done.12
  34.1 0.1 copy-done.11
  34.2 13.5 %forward_and_gradients.1 = (bf16[8192,128]{1,0:T(8,128)(2,1)}, bf16[128,32,256]{2,1,0:T(8,128)(2,1)}, bf16[2,128,256]{2,1,0:T(8,128)(2,1)}, bf16[2560,128]{1,0:T(8,128)(2,1)}, bf16[2560,128]{1,0:T(8,128)(2,1)}) custom-call(s32[1]{0:T(128)} %bitcast.core, bf16[256,512]{1,0:T(8,128)(2,1)} %bitcast.44, bf16[256,512]{1,0:T(8,128)(2,1)} %copy-done.11, ...), custom_call_target="tpu_custom_call" | custom-call | flops 8000000000 | bytes 14000000 | tf_op jit(solution)/shard_map/forward_and_gradients/pallas_call | solution.py:237
  47.6 0.4 collective-permute-start.6
  48.1 2.0 %collective-permute-done.6 = bf16[2560,128]{1,0:T(8,128)(2,1)S(1)} collective-permute-done((bf16[2560,128]{1,0:T(8,128)(2,1)}, bf16[2560,128]{1,0:T(8,128)(2,1)S(1)}, u32[]{:S(2)}, u32[]{:S(2)}) %collective-permute-start.6) | collective-permute-done | bytes 655392 | tf_op jit(solution)/shard_map/ppermute | solution.py:475
  50.0 2.1 %fusion = bf16[8192,128]{1,0:T(8,128)(2,1)} fusion(bf16[8192,128]{1,0:T(8,128)(2,1)} %get-tuple-element.37, bf16[2560,128]{1,0:T(8,128)(2,1)S(1)} %collective-permute-done.6, bf16[2560,128]{1,0:T(8,128)(2,1)} %get-tuple-element.38), kind=kLoop, calls=%fused_computation.1 | loop fusion | flops 1310720 | bytes 1966080 | tf_op jit(solution)/shard_map/dynamic_update_slice | solution.py:477
  52.1 6.4 %all-to-all-start.1 = ((bf16[64,128,128]{2,1,0:T(8,128)(2,1)}), bf16[64,128,128]{2,1,0:T(8,128)(2,1)}, u32[]{:S(2)}, u32[]{:S(2)}) async-start(bf16[64,128,128]{2,1,0:T(8,128)(2,1)} %bitcast.41), calls=%async_computation.1 | async-start | bytes 4194304 | tf_op jit(solution)/shard_map/all_to_all | solution.py:480
  58.6 0.7 collective-permute-start.7
  59.3 3.9 %collective-permute-start.10 = (bf16[1,256]{1,0:T(2,128)(2,1)S(1)}, bf16[1,256]{1,0:T(2,128)(2,1)S(1)}, u32[]{:S(2)}, u32[]{:S(2)}) collective-permute-start(bf16[1,256]{1,0:T(2,128)(2,1)S(1)} %get-tuple-element.73), channel_id=1, source_target_pairs={{1,18},{3,20},{5,22},{7,24},{9,26},{11,28},{13,30},{2,17},{4,19},{... | collective-permute-start | bytes 1544 | tf_op jit(solution)/shard_map/ppermute | solution.py:451
  63.2 1.3 collective-permute-start.12
  64.5 2.6 %collective-permute-start.11 = (bf16[128,256]{1,0:T(8,128)(2,1)S(1)}, bf16[128,256]{1,0:T(8,128)(2,1)S(1)}, u32[]{:S(2)}, u32[]{:S(2)}) collective-permute-start(bf16[128,256]{1,0:T(8,128)(2,1)S(1)} %bitcast.45), channel_id=1, source_target_pairs={{1,2},{3,4},{5,6},{7,8},{9,10},{11,12},{13,14},{2,1},{4,3},{6,5},{... | collective-permute-start | bytes 196616 | tf_op jit(solution)/shard_map/ppermute | solution.py:446
  67.1 1.3 collective-permute-start.9
  68.4 5.4 %collective-permute-start.8 = (bf16[33,256]{1,0:T(8,128)(2,1)S(1)}, bf16[33,256]{1,0:T(8,128)(2,1)S(1)}, u32[]{:S(2)}, u32[]{:S(2)}) collective-permute-start(bf16[33,256]{1,0:T(8,128)(2,1)S(1)} %pad_maximum_fusion.4), channel_id=1, source_target_pairs={{0,16},{16,32},{32,48},{48,64},{64,80},{80,96},{96,112},{1,17},{17... | collective-permute-start | bytes 50696 | tf_op jit(solution)/shard_map/ppermute | solution.py:408
  73.9 9.5 %collective-permute-done.11 = bf16[128,256]{1,0:T(8,128)(2,1)S(1)} collective-permute-done((bf16[128,256]{1,0:T(8,128)(2,1)S(1)}, bf16[128,256]{1,0:T(8,128)(2,1)S(1)}, u32[]{:S(2)}, u32[]{:S(2)}) %collective-permute-start.11) | collective-permute-done | bytes 65568 | tf_op jit(solution)/shard_map/ppermute | solution.py:446
  83.4 0.6 pad_maximum_fusion.1.rows
  84.1 0.8 maximum_convert_fusion.3
  84.9 1.2 all-to-all-done.1.parts
  86.0 3.0 %chip_sum.1 = bf16[64,128,128]{2,1,0:T(8,128)(2,1)} custom-call(bf16[64,128,128]{2,1,0:T(8,128)(2,1)} %all-to-all-done.1.parts), custom_call_target="tpu_custom_call" | custom-call | tf_op jit(solution)/shard_map/chip_sum/pallas_call | solution.py:347
  89.0 10.2 %all-to-all-start.2 = ((bf16[64,128,128]{2,1,0:T(8,128)(2,1)}), bf16[64,128,128]{2,1,0:T(8,128)(2,1)}, u32[]{:S(2)}, u32[]{:S(2)}) async-start(bf16[64,128,128]{2,1,0:T(8,128)(2,1)} %chip_sum.1), calls=%async_computation.2 | async-start | bytes 4194304 | tf_op jit(solution)/shard_map/all_to_all | solution.py:484
  99.2 0.0 copy-start.6
  99.2 0.7 copy-done.6
  100.0 6.7 %conv_forward.1 = bf16[128,32,256]{2,1,0:T(8,128)(2,1)} custom-call(bf16[128,32,256]{2,1,0:T(8,128)(2,1)S(1)} %copy-done, bf16[128,32,256]{2,1,0:T(8,128)(2,1)S(1)} %copy-done, bf16[128,32,256]{2,1,0:T(8,128)(2,1)S(1)} %copy-done, bf16[2,32,256]{2,1,0:T(8,128)(2,1)S(1)} %copy-done.6, f32[136,256]{1,0:T(8,128)S(1)} %get-tuple-element.47.left, ...), custom_call_target="tpu_custom_call" | custom-call | flops 1000000 | bytes 1000000 | tf_op jit(solution)/shard_map/conv_forward/pallas_call | solution.py:311
  106.7 19.8 %all-to-all-done.2 = bf16[64,128,128]{2,1,0:T(8,128)(2,1)} async-done(((bf16[64,128,128]{2,1,0:T(8,128)(2,1)}), bf16[64,128,128]{2,1,0:T(8,128)(2,1)}, u32[]{:S(2)}, u32[]{:S(2)}) %all-to-all-start.2) | async-done | bytes 2097184 | tf_op jit(solution)/shard_map/all_to_all | solution.py:484
  126.5 2.0 %collective-permute-start.13 = (bf16[8192,128]{1,0:T(8,128)(2,1)}, bf16[8192,128]{1,0:T(8,128)(2,1)S(1)}, u32[]{:S(2)}, u32[]{:S(2)}) collective-permute-start(bf16[8192,128]{1,0:T(8,128)(2,1)} %bitcast.22.half), channel_id=1, source_target_pairs={{0,1},{1,0},{2,3},{3,2},{4,5},{5,4},{6,7},{7,6},{8,9},{9,8},{10,11... | collective-permute-start | bytes 6291464 | tf_op jit(solution)/shard_map/ppermute | solution.py:487
  128.6 3.9 %place_gradients.2 = (f32[9,256,256]{2,1,0:T(8,128)}, f32[4,512,512]{2,1,0:T(8,128)}, f32[512,512]{1,0:T(8,128)}, f32[512,256]{1,0:T(8,128)}) custom-call(s32[1]{0:T(128)} %bitcast.core, bf16[8192,128]{1,0:T(8,128)(2,1)} %bitcast.22.half), custom_call_target="tpu_custom_call" | custom-call | bytes 6000000 | tf_op jit(solution)/shard_map/place_gradients/pallas_call | solution.py:380
  132.5 0.0 collective-permute-done.13.half
  132.6 2.4 %place_gradients.3 = (f32[9,256,256]{2,1,0:T(8,128)}, f32[4,512,512]{2,1,0:T(8,128)}, f32[512,512]{1,0:T(8,128)}, f32[512,256]{1,0:T(8,128)}) custom-call(s32[1]{0:T(128)S(6)} %sub.3.core, bf16[8192,128]{1,0:T(8,128)(2,1)S(1)} %collective-permute-done.13.half, ...), custom_call_target="tpu_custom_call", output_to_operand_aliasing={{0}: (2, {}), {1}: (3, {}), {2}: (4, {}), {3}: (5, {})} | custom-call | bytes 6000000 | tf_op jit(solution)/shard_map/place_gradients/pallas_call | solution.py:380
  (48 shorter events, 0.2 us)
Async XLA Ops:
  0.6 22.0 %copy-start.1 = (bf16[9,256,256]{2,1,0:T(8,128)(2,1)S(1)}, bf16[9,256,256]{2,1,0:T(8,128)(2,1)}, u32[]{:S(2)}) copy-start(bf16[9,256,256]{2,1,0:T(8,128)(2,1)} %wconv.1) | copy-start | bytes 3538948
  2.2 7.1 %collective-permute-start.1 = (bf16[128,256]{1,0:T(8,128)(2,1)S(1)}, bf16[128,256]{1,0:T(8,128)(2,1)S(1)}, u32[]{:S(2)}, u32[]{:S(2)}) collective-permute-start(bf16[128,256]{1,0:T(8,128)(2,1)S(1)} %get-tuple-element.65), channel_id=1, source_target_pairs={{0,1},{1,0},{2,3},{3,2},{4,5},{5,4},{6,7},{7,6},{8,9},{9,8},{10,11... | collective-permute-start | bytes 196616 | tf_op jit(solution)/shard_map/ppermute | solution.py:413
  3.7 5.6 %collective-permute-start = (bf16[128,256]{1,0:T(8,128)(2,1)S(1)}, bf16[128,256]{1,0:T(8,128)(2,1)S(1)}, u32[]{:S(2)}, u32[]{:S(2)}) collective-permute-start(bf16[128,256]{1,0:T(8,128)(2,1)S(1)} %get-tuple-element.66), channel_id=1, source_target_pairs={{1,2},{3,4},{5,6},{7,8},{9,10},{11,12},{13,14},{2,1},{4,3},{6,5},{... | collective-permute-start | bytes 196616 | tf_op jit(solution)/shard_map/ppermute | solution.py:416
  9.4 13.0 %collective-permute-start.2 = (bf16[34,256]{1,0:T(8,128)(2,1)S(1)}, bf16[34,256]{1,0:T(8,128)(2,1)S(1)}, u32[]{:S(2)}, u32[]{:S(2)}) collective-permute-start(bf16[34,256]{1,0:T(8,128)(2,1)S(1)} %get-tuple-element.83), channel_id=1, source_target_pairs={{16,32},{48,64},{80,96},{32,16},{64,48},{96,80},{17,33},{49,65},{8... | collective-permute-start | bytes 52232 | tf_op jit(solution)/shard_map/ppermute | solution.py:432
  10.0 12.4 %collective-permute-start.3 = (bf16[34,256]{1,0:T(8,128)(2,1)S(1)}, bf16[34,256]{1,0:T(8,128)(2,1)S(1)}, u32[]{:S(2)}, u32[]{:S(2)}) collective-permute-start(bf16[34,256]{1,0:T(8,128)(2,1)S(1)} %get-tuple-element.84), channel_id=1, source_target_pairs={{0,16},{32,48},{64,80},{96,112},{16,0},{48,32},{80,64},{112,96},{1... | collective-permute-start | bytes 52232 | tf_op jit(solution)/shard_map/ppermute | solution.py:434
  14.8 10.7 %copy-start.10 = (bf16[136]{0:T(256)(128)(2,1)}, bf16[136]{0:T(256)(128)(2,1)S(1)}, u32[]{:S(2)}) copy-start(bf16[136]{0:T(256)(128)(2,1)S(1)} %pad.21.clone) | copy-start | bytes 820
  14.8 15.2 %all-to-all-start = ((bf16[8,2,16,512]{3,2,1,0:T(8,128)(2,1)}), bf16[8,2,16,512]{3,2,1,0:T(8,128)(2,1)S(1)}, u32[]{:S(2)}, u32[]{:S(2)}) async-start(bf16[8,2,16,512]{3,2,1,0:T(8,128)(2,1)} %bitcast.38), calls=%async_computation | async-start | bytes 524288 | tf_op jit(solution)/shard_map/all_to_all | solution.py:468
  22.5 10.9 %copy-start.5 = (bf16[2,32,256]{2,1,0:T(8,128)(2,1)}, bf16[2,32,256]{2,1,0:T(8,128)(2,1)S(1)}, u32[]{:S(2)}) copy-start(bf16[2,32,256]{2,1,0:T(8,128)(2,1)S(1)} %pad_maximum_fusion.rows) | copy-start | bytes 98308
  22.6 10.8 %copy-start.3 = (f32[136,256]{1,0:T(8,128)}, f32[136,256]{1,0:T(8,128)S(1)}, u32[]{:S(2)}) copy-start(f32[136,256]{1,0:T(8,128)S(1)} %get-tuple-element.95.right) | copy-start | bytes 417796
  22.6 10.8 %copy-start.4 = (f32[136,256]{1,0:T(8,128)}, f32[136,256]{1,0:T(8,128)S(1)}, u32[]{:S(2)}) copy-start(f32[136,256]{1,0:T(8,128)S(1)} %get-tuple-element.96.left) | copy-start | bytes 417796
  22.6 1.7 %copy-start.2 = (bf16[128,32,256]{2,1,0:T(8,128)(2,1)S(1)}, bf16[128,32,256]{2,1,0:T(8,128)(2,1)}, u32[]{:S(2)}) copy-start(bf16[128,32,256]{2,1,0:T(8,128)(2,1)} %oc_hbm.1) | copy-start | bytes 6291460
  25.4 8.0 %copy-start.7 = (bf16[256,256]{1,0:T(8,128)(2,1)}, bf16[256,256]{1,0:T(8,128)(2,1)S(1)}, u32[]{:S(2)}) copy-start(bf16[256,256]{1,0:T(8,128)(2,1)S(1)} %coarse_cotangent.1.dco) | copy-start | bytes 393220
  30.0 3.5 %copy-start.8 = (bf16[8,2,16,512]{3,2,1,0:T(8,128)(2,1)}, bf16[8,2,16,512]{3,2,1,0:T(8,128)(2,1)S(1)}, u32[]{:S(2)}) copy-start(bf16[8,2,16,512]{3,2,1,0:T(8,128)(2,1)S(1)} %all-to-all-done) | copy-start | bytes 786436
  30.0 3.4 %collective-permute-start.4 = (bf16[256,512]{1,0:T(8,128)(2,1)S(1)}, bf16[256,512]{1,0:T(8,128)(2,1)S(1)}, u32[]{:S(2)}, u32[]{:S(2)}) collective-permute-start(bf16[256,512]{1,0:T(8,128)(2,1)S(1)} %bitcast.43), channel_id=1, source_target_pairs={{0,1},{1,0},{2,3},{3,2},{4,5},{5,4},{6,7},{7,6},{8,9},{9,8},{10,11... | collective-permute-start | bytes 786440 | tf_op jit(solution)/shard_map/ppermute | solution.py:471
  32.1 1.3 %collective-permute-start.5 = (bf16[256,256]{1,0:T(8,128)(2,1)S(1)}, bf16[256,256]{1,0:T(8,128)(2,1)S(1)}, u32[]{:S(2)}, u32[]{:S(2)}) collective-permute-start(bf16[256,256]{1,0:T(8,128)(2,1)S(1)} %coarse_cotangent.1.dco), channel_id=1, source_target_pairs={{0,1},{1,0},{2,3},{3,2},{4,5},{5,4},{6,7},{7,6},{8,9},{9,8},{10,11... | collective-permute-start | bytes 393224 | tf_op jit(solution)/shard_map/ppermute | solution.py:471
  33.4 0.6 copy-start.12
  33.4 0.7 copy-start.11
  47.6 2.4 %collective-permute-start.6 = (bf16[2560,128]{1,0:T(8,128)(2,1)}, bf16[2560,128]{1,0:T(8,128)(2,1)S(1)}, u32[]{:S(2)}, u32[]{:S(2)}) collective-permute-start(bf16[2560,128]{1,0:T(8,128)(2,1)} %get-tuple-element.39), channel_id=1, source_target_pairs={{0,1},{1,0},{2,3},{3,2},{4,5},{5,4},{6,7},{7,6},{8,9},{9,8},{10,11... | collective-permute-start | bytes 1966088 | tf_op jit(solution)/shard_map/ppermute | solution.py:475
  52.1 6.4 %copy-start = (bf16[128,32,256]{2,1,0:T(8,128)(2,1)S(1)}, bf16[128,32,256]{2,1,0:T(8,128)(2,1)}, u32[]{:S(2)}) copy-start(bf16[128,32,256]{2,1,0:T(8,128)(2,1)} %get-tuple-element.43.before.ci.after) | copy-start | bytes 6291460
  52.1 6.4 %copy-start.9 = (bf16[2,128,256]{2,1,0:T(8,128)(2,1)S(1)}, bf16[2,128,256]{2,1,0:T(8,128)(2,1)}, u32[]{:S(2)}) copy-start(bf16[2,128,256]{2,1,0:T(8,128)(2,1)} %get-tuple-element.44) | copy-start | bytes 393220
  52.1 33.9 %all-to-all-start.1 = ((bf16[64,128,128]{2,1,0:T(8,128)(2,1)}), bf16[64,128,128]{2,1,0:T(8,128)(2,1)}, u32[]{:S(2)}, u32[]{:S(2)}) async-start(bf16[64,128,128]{2,1,0:T(8,128)(2,1)} %bitcast.41), calls=%async_computation.1 | async-start | bytes 4194304 | tf_op jit(solution)/shard_map/all_to_all | solution.py:480
  58.6 8.5 %collective-permute-start.7 = (bf16[128,256]{1,0:T(8,128)(2,1)S(1)}, bf16[128,256]{1,0:T(8,128)(2,1)S(1)}, u32[]{:S(2)}, u32[]{:S(2)}) collective-permute-start(bf16[128,256]{1,0:T(8,128)(2,1)S(1)} %get-tuple-element.70), channel_id=1, source_target_pairs={{0,1},{1,0},{2,3},{3,2},{4,5},{5,4},{6,7},{7,6},{8,9},{9,8},{10,11... | collective-permute-start | bytes 196616 | tf_op jit(solution)/shard_map/ppermute | solution.py:443
  59.3 24.8 %collective-permute-start.10 = (bf16[1,256]{1,0:T(2,128)(2,1)S(1)}, bf16[1,256]{1,0:T(2,128)(2,1)S(1)}, u32[]{:S(2)}, u32[]{:S(2)}) collective-permute-start(bf16[1,256]{1,0:T(2,128)(2,1)S(1)} %get-tuple-element.73), channel_id=1, source_target_pairs={{1,18},{3,20},{5,22},{7,24},{9,26},{11,28},{13,30},{2,17},{4,19},{... | collective-permute-start | bytes 1544 | tf_op jit(solution)/shard_map/ppermute | solution.py:451
  63.2 20.2 %collective-permute-start.12 = (bf16[1,256]{1,0:T(2,128)(2,1)S(1)}, bf16[1,256]{1,0:T(2,128)(2,1)S(1)}, u32[]{:S(2)}, u32[]{:S(2)}) collective-permute-start(bf16[1,256]{1,0:T(2,128)(2,1)S(1)} %get-tuple-element.74), channel_id=1, source_target_pairs={{17,2},{19,4},{21,6},{23,8},{25,10},{27,12},{29,14},{18,1},{20,3},... | collective-permute-start | bytes 1544 | tf_op jit(solution)/shard_map/ppermute | solution.py:451
  64.5 18.9 %collective-permute-start.11 = (bf16[128,256]{1,0:T(8,128)(2,1)S(1)}, bf16[128,256]{1,0:T(8,128)(2,1)S(1)}, u32[]{:S(2)}, u32[]{:S(2)}) collective-permute-start(bf16[128,256]{1,0:T(8,128)(2,1)S(1)} %bitcast.45), channel_id=1, source_target_pairs={{1,2},{3,4},{5,6},{7,8},{9,10},{11,12},{13,14},{2,1},{4,3},{6,5},{... | collective-permute-start | bytes 196616 | tf_op jit(solution)/shard_map/ppermute | solution.py:446
  67.1 16.3 %collective-permute-start.9 = (bf16[33,256]{1,0:T(8,128)(2,1)S(1)}, bf16[33,256]{1,0:T(8,128)(2,1)S(1)}, u32[]{:S(2)}, u32[]{:S(2)}) collective-permute-start(bf16[33,256]{1,0:T(8,128)(2,1)S(1)} %pad_maximum_fusion.5), channel_id=1, source_target_pairs={{16,0},{32,16},{48,32},{64,48},{80,64},{96,80},{112,96},{17,1},{33... | collective-permute-start | bytes 50696 | tf_op jit(solution)/shard_map/ppermute | solution.py:408
  68.4 15.0 %collective-permute-start.8 = (bf16[33,256]{1,0:T(8,128)(2,1)S(1)}, bf16[33,256]{1,0:T(8,128)(2,1)S(1)}, u32[]{:S(2)}, u32[]{:S(2)}) collective-permute-start(bf16[33,256]{1,0:T(8,128)(2,1)S(1)} %pad_maximum_fusion.4), channel_id=1, source_target_pairs={{0,16},{16,32},{32,48},{48,64},{64,80},{80,96},{96,112},{1,17},{17... | collective-permute-start | bytes 50696 | tf_op jit(solution)/shard_map/ppermute | solution.py:408
  89.0 37.5 %all-to-all-start.2 = ((bf16[64,128,128]{2,1,0:T(8,128)(2,1)}), bf16[64,128,128]{2,1,0:T(8,128)(2,1)}, u32[]{:S(2)}, u32[]{:S(2)}) async-start(bf16[64,128,128]{2,1,0:T(8,128)(2,1)} %chip_sum.1), calls=%async_computation.2 | async-start | bytes 4194304 | tf_op jit(solution)/shard_map/all_to_all | solution.py:484
  99.2 0.8 copy-start.6
  126.5 6.0 %collective-permute-start.13 = (bf16[8192,128]{1,0:T(8,128)(2,1)}, bf16[8192,128]{1,0:T(8,128)(2,1)S(1)}, u32[]{:S(2)}, u32[]{:S(2)}) collective-permute-start(bf16[8192,128]{1,0:T(8,128)(2,1)} %bitcast.22.half), channel_id=1, source_target_pairs={{0,1},{1,0},{2,3},{3,2},{4,5},{5,4},{6,7},{7,6},{8,9},{9,8},{10,11... | collective-permute-start | bytes 6291464 | tf_op jit(solution)/shard_map/ppermute | solution.py:487

commit v7 on v6

--- a/solution.py
+++ b/solution.py
@@ -268,7 +268,7 @@
             pltpu.VMEM((8, 2, 2, 2 * IC, CF), F32),
             pltpu.SemaphoreType.DMA((12,)),
         ],
-        compiler_params=params(56, 0),
+        compiler_params=params(50, 0),
         cost_estimate=cost(8_000_000_000, 14_000_000),
         name="forward_and_gradients",
     )(core, x, xtwin, wband, wpoint, wproj, fine, oc, dco, dtwin, rows, left, right)

time: 136 us -> 132 us (0.971)
  Pallas kernels: 30.6 us -> 28 us
    pallas_call x1, Pallas kernels: 13.5 us -> 10.9 us  [forward_pass(): pl.pallas_call(forward_kernel, in_specs=[pl.BlockSpec(memory_space=pltpu....]
    unnamed x26 -> x14, local copies, waits for them, and re-layouts: 3.16 us -> 3.34 us
where the time goes in v7:
time: 132 us; the launch traced here: 131 us
  starting transfers between devices  54 us (41%)
  waiting for transfers between devices  38.2 us (29%)
  Pallas kernels  28 us (21%)
  local copies, waits for them, and re-layouts  7.39 us (6%)
  other arithmetic  2.6 us (2%)
    all_to_all x1, waiting for transfers between devices, local(): mine = lax.all_to_all(spread, CHIPS, 0, 0, tiled=True)  19.8 us
    pallas_call x1, Pallas kernels, forward_pass(): pl.pallas_call(forward_kernel, in_specs=[pl.BlockSpec(memory_space=pltpu....  10.9 us
    all_to_all x1, starting transfers between devices, local(): mine = lax.all_to_all(spread, CHIPS, 0, 0, tiled=True)  10.2 us
    ppermute x1, waiting for transfers between devices, whole_halo(): chip = lax.ppermute(outer, COL, chips)  9.49 us
    all_to_all x1, starting transfers between devices, local(): x = lax.all_to_all(chunks, ('xh', 'y'), 0, 0, tiled=True).reshape(CELLS, C)  7.62 us
    pallas_call x1, Pallas kernels, conv_pass(): pl.pallas_call(conv_kernel, grid=(NB,), in_specs=window_specs() + [whole(...  6.73 us
    ppermute x2, starting transfers between devices, shift(): return lax.ppermute(value, axes, pairs)  6.73 us
    all_to_all x1, starting transfers between devices, local(): parts = lax.all_to_all(packed, CHIPS, 0, 0, tiled=True)  6.36 us
  transfers between devices with their start and end apart: 17, of which 6 were waited for; matrix products, arithmetic and copies ran while one was open for 3% of the time, Pallas kernels for 9%

profile of v7, /device:TPU:1, one launch (start us, length us, event | category | flops | bytes accessed | tf_op | source)
XLA Modules:
  0.0 131.2 jit_solution(13722678035906314710)
XLA Ops:
  0.6 1.5 %fusion.1 = (bf16[128,1,256]{2,1,0:T(2,128)(2,1)S(1)}, bf16[128,1,256]{2,1,0:T(2,128)(2,1)S(1)}) fusion(bf16[128,32,256]{2,1,0:T(8,128)(2,1)} %oc_hbm.1), kind=kLoop, calls=%fused_computation.39 | loop fusion | bytes 262144 | tf_op jit(solution)/shard_map/slice | solution.py:465
  2.2 1.5 %collective-permute-start.1 = (bf16[128,256]{1,0:T(8,128)(2,1)S(1)}, bf16[128,256]{1,0:T(8,128)(2,1)S(1)}, u32[]{:S(2)}, u32[]{:S(2)}) collective-permute-start(bf16[128,256]{1,0:T(8,128)(2,1)S(1)} %get-tuple-element.65), channel_id=1, source_target_pairs={{0,1},{1,0},{2,3},{3,2},{4,5},{5,4},{6,7},{7,6},{8,9},{9,8},{10,11... | collective-permute-start | bytes 196616 | tf_op jit(solution)/shard_map/ppermute | solution.py:413
  3.7 3.2 %collective-permute-start = (bf16[128,256]{1,0:T(8,128)(2,1)S(1)}, bf16[128,256]{1,0:T(8,128)(2,1)S(1)}, u32[]{:S(2)}, u32[]{:S(2)}) collective-permute-start(bf16[128,256]{1,0:T(8,128)(2,1)S(1)} %get-tuple-element.66), channel_id=1, source_target_pairs={{1,2},{3,4},{5,6},{7,8},{9,10},{11,12},{13,14},{2,1},{4,3},{6,5},{... | collective-permute-start | bytes 196616 | tf_op jit(solution)/shard_map/ppermute | solution.py:416
  6.9 0.7 slice_bitcast_fusion.7
  7.6 1.7 %copy.26 = bf16[2,8,16,512]{3,2,0,1:T(8,128)(2,1)} copy(bf16[2,8,16,512]{3,2,1,0:T(8,128)(2,1)} %bitcast.44) | data formatting | bytes 524288 | tf_op jit(solution)/shard_map/reshape | solution.py:464
  9.3 0.0 collective-permute-done.1
  9.3 0.0 collective-permute-done
  9.4 0.7 collective-permute-start.2
  10.0 4.6 %collective-permute-start.3 = (bf16[34,256]{1,0:T(8,128)(2,1)S(1)}, bf16[34,256]{1,0:T(8,128)(2,1)S(1)}, u32[]{:S(2)}, u32[]{:S(2)}) collective-permute-start(bf16[34,256]{1,0:T(8,128)(2,1)S(1)} %get-tuple-element.84), channel_id=1, source_target_pairs={{0,16},{32,48},{64,80},{96,112},{16,0},{48,32},{80,64},{112,96},{1... | collective-permute-start | bytes 52232 | tf_op jit(solution)/shard_map/ppermute | solution.py:434
  14.7 0.1 pad.21.clone
  14.8 7.6 %all-to-all-start = ((bf16[8,2,16,512]{3,2,1,0:T(8,128)(2,1)}), bf16[8,2,16,512]{3,2,1,0:T(8,128)(2,1)S(1)}, u32[]{:S(2)}, u32[]{:S(2)}) async-start(bf16[8,2,16,512]{3,2,1,0:T(8,128)(2,1)} %bitcast.38), calls=%async_computation | async-start | bytes 524288 | tf_op jit(solution)/shard_map/all_to_all | solution.py:468
  22.4 0.0 collective-permute-done.2
  22.5 0.0 copy-start.4
  22.5 0.1 maximum_convert_fusion.1
  22.6 0.0 copy-start.2
  22.6 1.6 %copy-done.2 = bf16[128,32,256]{2,1,0:T(8,128)(2,1)S(1)} copy-done((bf16[128,32,256]{2,1,0:T(8,128)(2,1)S(1)}, bf16[128,32,256]{2,1,0:T(8,128)(2,1)}, u32[]{:S(2)}) %copy-start.2) | copy-done | bytes 2097176
  24.2 1.1 coarse_cotangent.1.dco
  25.4 4.6 %all-to-all-done = bf16[8,2,16,512]{3,2,1,0:T(8,128)(2,1)S(1)} async-done(((bf16[8,2,16,512]{3,2,1,0:T(8,128)(2,1)}), bf16[8,2,16,512]{3,2,1,0:T(8,128)(2,1)S(1)}, u32[]{:S(2)}, u32[]{:S(2)}) %all-to-all-start) | async-done | bytes 262176 | tf_op jit(solution)/shard_map/all_to_all | solution.py:468
  30.0 2.1 %collective-permute-start.4 = (bf16[256,512]{1,0:T(8,128)(2,1)S(1)}, bf16[256,512]{1,0:T(8,128)(2,1)S(1)}, u32[]{:S(2)}, u32[]{:S(2)}) collective-permute-start(bf16[256,512]{1,0:T(8,128)(2,1)S(1)} %bitcast.41), channel_id=1, source_target_pairs={{0,1},{1,0},{2,3},{3,2},{4,5},{5,4},{6,7},{7,6},{8,9},{9,8},{10,11... | collective-permute-start | bytes 786440 | tf_op jit(solution)/shard_map/ppermute | solution.py:471
  32.1 0.0 collective-permute-start.5
  32.1 1.3 %collective-permute-done.5.dtwin = bf16[256,256]{1,0:T(8,128)(2,1)S(1)} collective-permute-done((bf16[256,256]{1,0:T(8,128)(2,1)S(1)}, bf16[256,256]{1,0:T(8,128)(2,1)S(1)}, u32[]{:S(2)}, u32[]{:S(2)}) %collective-permute-start.5) | collective-permute-done | bytes 131104 | tf_op jit(solution)/shard_map/ppermute | solution.py:471
  33.4 0.0 collective-permute-done.4.xtwin_hbm
  33.4 0.9 copy-done.5
  34.4 10.9 %forward_and_gradients.1 = (bf16[8192,128]{1,0:T(8,128)(2,1)}, bf16[128,32,256]{2,1,0:T(8,128)(2,1)}, bf16[2,128,256]{2,1,0:T(8,128)(2,1)S(1)}, bf16[2560,128]{1,0:T(8,128)(2,1)S(1)}, bf16[2560,128]{1,0:T(8,128)(2,1)S(1)}) custom-call(s32[1]{0:T(128)} %bitcast.core, bf16[256,512]{1,0:T(8,128)(2,1)S(1)} %bitcast.42, ...), custom_call_target="tpu_custom_call" | custom-call | flops 8000000000 | bytes 14000000 | tf_op jit(solution)/shard_map/forward_and_gradients/pallas_call | solution.py:237
  45.3 0.4 collective-permute-start.6
  45.7 1.7 %collective-permute-done.6 = bf16[2560,128]{1,0:T(8,128)(2,1)S(1)} collective-permute-done((bf16[2560,128]{1,0:T(8,128)(2,1)S(1)}, bf16[2560,128]{1,0:T(8,128)(2,1)S(1)}, u32[]{:S(2)}, u32[]{:S(2)}) %collective-permute-start.6) | collective-permute-done | bytes 655392 | tf_op jit(solution)/shard_map/ppermute | solution.py:475
  47.4 1.0 fusion
  48.5 6.4 %all-to-all-start.1 = ((bf16[64,128,128]{2,1,0:T(8,128)(2,1)}), bf16[64,128,128]{2,1,0:T(8,128)(2,1)}, u32[]{:S(2)}, u32[]{:S(2)}) async-start(bf16[64,128,128]{2,1,0:T(8,128)(2,1)} %bitcast.43), calls=%async_computation.1 | async-start | bytes 4194304 | tf_op jit(solution)/shard_map/all_to_all | solution.py:480
  54.9 0.7 collective-permute-start.7
  55.6 3.9 %collective-permute-start.10 = (bf16[1,256]{1,0:T(2,128)(2,1)S(1)}, bf16[1,256]{1,0:T(2,128)(2,1)S(1)}, u32[]{:S(2)}, u32[]{:S(2)}) collective-permute-start(bf16[1,256]{1,0:T(2,128)(2,1)S(1)} %get-tuple-element.73), channel_id=1, source_target_pairs={{1,18},{3,20},{5,22},{7,24},{9,26},{11,28},{13,30},{2,17},{4,19},{... | collective-permute-start | bytes 1544 | tf_op jit(solution)/shard_map/ppermute | solution.py:451
  59.5 1.3 collective-permute-start.12
  60.8 2.6 %collective-permute-start.11 = (bf16[128,256]{1,0:T(8,128)(2,1)S(1)}, bf16[128,256]{1,0:T(8,128)(2,1)S(1)}, u32[]{:S(2)}, u32[]{:S(2)}) collective-permute-start(bf16[128,256]{1,0:T(8,128)(2,1)S(1)} %bitcast.45), channel_id=1, source_target_pairs={{1,2},{3,4},{5,6},{7,8},{9,10},{11,12},{13,14},{2,1},{4,3},{6,5},{... | collective-permute-start | bytes 196616 | tf_op jit(solution)/shard_map/ppermute | solution.py:446
  63.4 1.3 collective-permute-start.9
  64.8 5.4 %collective-permute-start.8 = (bf16[33,256]{1,0:T(8,128)(2,1)S(1)}, bf16[33,256]{1,0:T(8,128)(2,1)S(1)}, u32[]{:S(2)}, u32[]{:S(2)}) collective-permute-start(bf16[33,256]{1,0:T(8,128)(2,1)S(1)} %pad_maximum_fusion.4), channel_id=1, source_target_pairs={{0,16},{16,32},{32,48},{48,64},{64,80},{80,96},{96,112},{1,17},{17... | collective-permute-start | bytes 50696 | tf_op jit(solution)/shard_map/ppermute | solution.py:408
  70.2 9.5 %collective-permute-done.11 = bf16[128,256]{1,0:T(8,128)(2,1)S(1)} collective-permute-done((bf16[128,256]{1,0:T(8,128)(2,1)S(1)}, bf16[128,256]{1,0:T(8,128)(2,1)S(1)}, u32[]{:S(2)}, u32[]{:S(2)}) %collective-permute-start.11) | collective-permute-done | bytes 65568 | tf_op jit(solution)/shard_map/ppermute | solution.py:446
  79.8 0.6 pad_maximum_fusion.1.rows
  80.4 0.7 maximum_convert_fusion.3
  81.2 1.1 all-to-all-done.1.parts
  82.3 3.0 %chip_sum.1 = bf16[64,128,128]{2,1,0:T(8,128)(2,1)} custom-call(bf16[64,128,128]{2,1,0:T(8,128)(2,1)} %all-to-all-done.1.parts), custom_call_target="tpu_custom_call" | custom-call | tf_op jit(solution)/shard_map/chip_sum/pallas_call | solution.py:347
  85.3 10.2 %all-to-all-start.2 = ((bf16[64,128,128]{2,1,0:T(8,128)(2,1)}), bf16[64,128,128]{2,1,0:T(8,128)(2,1)}, u32[]{:S(2)}, u32[]{:S(2)}) async-start(bf16[64,128,128]{2,1,0:T(8,128)(2,1)} %chip_sum.1), calls=%async_computation.2 | async-start | bytes 4194304 | tf_op jit(solution)/shard_map/all_to_all | solution.py:484
  95.5 0.0 copy-start.3
  95.5 0.7 copy-done.3
  96.3 6.7 %conv_forward.1 = bf16[128,32,256]{2,1,0:T(8,128)(2,1)} custom-call(bf16[128,32,256]{2,1,0:T(8,128)(2,1)S(1)} %copy-done, bf16[128,32,256]{2,1,0:T(8,128)(2,1)S(1)} %copy-done, bf16[128,32,256]{2,1,0:T(8,128)(2,1)S(1)} %copy-done, bf16[2,32,256]{2,1,0:T(8,128)(2,1)S(1)} %copy-done.3, f32[136,256]{1,0:T(8,128)S(1)} %get-tuple-element.47.left, ...), custom_call_target="tpu_custom_call" | custom-call | flops 1000000 | bytes 1000000 | tf_op jit(solution)/shard_map/conv_forward/pallas_call | solution.py:311
  103.0 19.8 %all-to-all-done.2 = bf16[64,128,128]{2,1,0:T(8,128)(2,1)} async-done(((bf16[64,128,128]{2,1,0:T(8,128)(2,1)}), bf16[64,128,128]{2,1,0:T(8,128)(2,1)}, u32[]{:S(2)}, u32[]{:S(2)}) %all-to-all-start.2) | async-done | bytes 2097184 | tf_op jit(solution)/shard_map/all_to_all | solution.py:484
  122.8 2.1 %collective-permute-start.13 = (bf16[8192,128]{1,0:T(8,128)(2,1)}, bf16[8192,128]{1,0:T(8,128)(2,1)S(1)}, u32[]{:S(2)}, u32[]{:S(2)}) collective-permute-start(bf16[8192,128]{1,0:T(8,128)(2,1)} %bitcast.22.half), channel_id=1, source_target_pairs={{0,1},{1,0},{2,3},{3,2},{4,5},{5,4},{6,7},{7,6},{8,9},{9,8},{10,11... | collective-permute-start | bytes 6291464 | tf_op jit(solution)/shard_map/ppermute | solution.py:487
  124.9 3.9 %place_gradients.2 = (f32[9,256,256]{2,1,0:T(8,128)}, f32[4,512,512]{2,1,0:T(8,128)}, f32[512,512]{1,0:T(8,128)}, f32[512,256]{1,0:T(8,128)}) custom-call(s32[1]{0:T(128)} %bitcast.core, bf16[8192,128]{1,0:T(8,128)(2,1)} %bitcast.22.half), custom_call_target="tpu_custom_call" | custom-call | bytes 6000000 | tf_op jit(solution)/shard_map/place_gradients/pallas_call | solution.py:380
  128.8 0.0 collective-permute-done.13.half
  128.9 2.4 %place_gradients.3 = (f32[9,256,256]{2,1,0:T(8,128)}, f32[4,512,512]{2,1,0:T(8,128)}, f32[512,512]{1,0:T(8,128)}, f32[512,256]{1,0:T(8,128)}) custom-call(s32[1]{0:T(128)S(6)} %sub.3.core, bf16[8192,128]{1,0:T(8,128)(2,1)S(1)} %collective-permute-done.13.half, ...), custom_call_target="tpu_custom_call", output_to_operand_aliasing={{0}: (2, {}), {1}: (3, {}), {2}: (4, {}), {3}: (5, {})} | custom-call | bytes 6000000 | tf_op jit(solution)/shard_map/place_gradients/pallas_call | solution.py:380
  (36 shorter events, 0.2 us)
Async XLA Ops:
  0.6 22.0 %copy-start.1 = (bf16[9,256,256]{2,1,0:T(8,128)(2,1)S(1)}, bf16[9,256,256]{2,1,0:T(8,128)(2,1)}, u32[]{:S(2)}) copy-start(bf16[9,256,256]{2,1,0:T(8,128)(2,1)} %wconv.1) | copy-start | bytes 3538948
  2.2 7.1 %collective-permute-start.1 = (bf16[128,256]{1,0:T(8,128)(2,1)S(1)}, bf16[128,256]{1,0:T(8,128)(2,1)S(1)}, u32[]{:S(2)}, u32[]{:S(2)}) collective-permute-start(bf16[128,256]{1,0:T(8,128)(2,1)S(1)} %get-tuple-element.65), channel_id=1, source_target_pairs={{0,1},{1,0},{2,3},{3,2},{4,5},{5,4},{6,7},{7,6},{8,9},{9,8},{10,11... | collective-permute-start | bytes 196616 | tf_op jit(solution)/shard_map/ppermute | solution.py:413
  3.7 5.6 %collective-permute-start = (bf16[128,256]{1,0:T(8,128)(2,1)S(1)}, bf16[128,256]{1,0:T(8,128)(2,1)S(1)}, u32[]{:S(2)}, u32[]{:S(2)}) collective-permute-start(bf16[128,256]{1,0:T(8,128)(2,1)S(1)} %get-tuple-element.66), channel_id=1, source_target_pairs={{1,2},{3,4},{5,6},{7,8},{9,10},{11,12},{13,14},{2,1},{4,3},{6,5},{... | collective-permute-start | bytes 196616 | tf_op jit(solution)/shard_map/ppermute | solution.py:416
  9.4 13.0 %collective-permute-start.2 = (bf16[34,256]{1,0:T(8,128)(2,1)S(1)}, bf16[34,256]{1,0:T(8,128)(2,1)S(1)}, u32[]{:S(2)}, u32[]{:S(2)}) collective-permute-start(bf16[34,256]{1,0:T(8,128)(2,1)S(1)} %get-tuple-element.83), channel_id=1, source_target_pairs={{16,32},{48,64},{80,96},{32,16},{64,48},{96,80},{17,33},{49,65},{8... | collective-permute-start | bytes 52232 | tf_op jit(solution)/shard_map/ppermute | solution.py:432
  10.0 12.4 %collective-permute-start.3 = (bf16[34,256]{1,0:T(8,128)(2,1)S(1)}, bf16[34,256]{1,0:T(8,128)(2,1)S(1)}, u32[]{:S(2)}, u32[]{:S(2)}) collective-permute-start(bf16[34,256]{1,0:T(8,128)(2,1)S(1)} %get-tuple-element.84), channel_id=1, source_target_pairs={{0,16},{32,48},{64,80},{96,112},{16,0},{48,32},{80,64},{112,96},{1... | collective-permute-start | bytes 52232 | tf_op jit(solution)/shard_map/ppermute | solution.py:434
  14.8 10.6 %copy-start.6 = (bf16[136]{0:T(256)(128)(2,1)}, bf16[136]{0:T(256)(128)(2,1)S(1)}, u32[]{:S(2)}) copy-start(bf16[136]{0:T(256)(128)(2,1)S(1)} %pad.21.clone) | copy-start | bytes 820
  14.8 15.2 %all-to-all-start = ((bf16[8,2,16,512]{3,2,1,0:T(8,128)(2,1)}), bf16[8,2,16,512]{3,2,1,0:T(8,128)(2,1)S(1)}, u32[]{:S(2)}, u32[]{:S(2)}) async-start(bf16[8,2,16,512]{3,2,1,0:T(8,128)(2,1)} %bitcast.38), calls=%async_computation | async-start | bytes 524288 | tf_op jit(solution)/shard_map/all_to_all | solution.py:468
  22.5 11.0 %copy-start.4 = (bf16[512,512]{1,0:T(8,128)(2,1)S(1)}, bf16[512,512]{1,0:T(8,128)(2,1)}, u32[]{:S(2)}) copy-start(bf16[512,512]{1,0:T(8,128)(2,1)} %wp_hbm.1) | copy-start | bytes 1572868
  22.6 1.6 %copy-start.2 = (bf16[128,32,256]{2,1,0:T(8,128)(2,1)S(1)}, bf16[128,32,256]{2,1,0:T(8,128)(2,1)}, u32[]{:S(2)}) copy-start(bf16[128,32,256]{2,1,0:T(8,128)(2,1)} %oc_hbm.1) | copy-start | bytes 6291460
  30.0 3.4 %collective-permute-start.4 = (bf16[256,512]{1,0:T(8,128)(2,1)S(1)}, bf16[256,512]{1,0:T(8,128)(2,1)S(1)}, u32[]{:S(2)}, u32[]{:S(2)}) collective-permute-start(bf16[256,512]{1,0:T(8,128)(2,1)S(1)} %bitcast.41), channel_id=1, source_target_pairs={{0,1},{1,0},{2,3},{3,2},{4,5},{5,4},{6,7},{7,6},{8,9},{9,8},{10,11... | collective-permute-start | bytes 786440 | tf_op jit(solution)/shard_map/ppermute | solution.py:471
  32.1 1.3 %collective-permute-start.5 = (bf16[256,256]{1,0:T(8,128)(2,1)S(1)}, bf16[256,256]{1,0:T(8,128)(2,1)S(1)}, u32[]{:S(2)}, u32[]{:S(2)}) collective-permute-start(bf16[256,256]{1,0:T(8,128)(2,1)S(1)} %coarse_cotangent.1.dco), channel_id=1, source_target_pairs={{0,1},{1,0},{2,3},{3,2},{4,5},{5,4},{6,7},{7,6},{8,9},{9,8},{10,11... | collective-permute-start | bytes 393224 | tf_op jit(solution)/shard_map/ppermute | solution.py:471
  33.4 1.0 copy-start.5
  45.3 2.2 %collective-permute-start.6 = (bf16[2560,128]{1,0:T(8,128)(2,1)S(1)}, bf16[2560,128]{1,0:T(8,128)(2,1)S(1)}, u32[]{:S(2)}, u32[]{:S(2)}) collective-permute-start(bf16[2560,128]{1,0:T(8,128)(2,1)S(1)} %get-tuple-element.39), channel_id=1, source_target_pairs={{0,1},{1,0},{2,3},{3,2},{4,5},{5,4},{6,7},{7,6},{8,9},{9,8},{10,11... | collective-permute-start | bytes 1966088 | tf_op jit(solution)/shard_map/ppermute | solution.py:475
  48.5 6.4 %copy-start = (bf16[128,32,256]{2,1,0:T(8,128)(2,1)S(1)}, bf16[128,32,256]{2,1,0:T(8,128)(2,1)}, u32[]{:S(2)}) copy-start(bf16[128,32,256]{2,1,0:T(8,128)(2,1)} %get-tuple-element.43.before.ci.after) | copy-start | bytes 6291460
  48.5 33.8 %all-to-all-start.1 = ((bf16[64,128,128]{2,1,0:T(8,128)(2,1)}), bf16[64,128,128]{2,1,0:T(8,128)(2,1)}, u32[]{:S(2)}, u32[]{:S(2)}) async-start(bf16[64,128,128]{2,1,0:T(8,128)(2,1)} %bitcast.43), calls=%async_computation.1 | async-start | bytes 4194304 | tf_op jit(solution)/shard_map/all_to_all | solution.py:480
  54.9 8.5 %collective-permute-start.7 = (bf16[128,256]{1,0:T(8,128)(2,1)S(1)}, bf16[128,256]{1,0:T(8,128)(2,1)S(1)}, u32[]{:S(2)}, u32[]{:S(2)}) collective-permute-start(bf16[128,256]{1,0:T(8,128)(2,1)S(1)} %get-tuple-element.70), channel_id=1, source_target_pairs={{0,1},{1,0},{2,3},{3,2},{4,5},{5,4},{6,7},{7,6},{8,9},{9,8},{10,11... | collective-permute-start | bytes 196616 | tf_op jit(solution)/shard_map/ppermute | solution.py:443
  55.6 24.8 %collective-permute-start.10 = (bf16[1,256]{1,0:T(2,128)(2,1)S(1)}, bf16[1,256]{1,0:T(2,128)(2,1)S(1)}, u32[]{:S(2)}, u32[]{:S(2)}) collective-permute-start(bf16[1,256]{1,0:T(2,128)(2,1)S(1)} %get-tuple-element.73), channel_id=1, source_target_pairs={{1,18},{3,20},{5,22},{7,24},{9,26},{11,28},{13,30},{2,17},{4,19},{... | collective-permute-start | bytes 1544 | tf_op jit(solution)/shard_map/ppermute | solution.py:451
  59.5 20.2 %collective-permute-start.12 = (bf16[1,256]{1,0:T(2,128)(2,1)S(1)}, bf16[1,256]{1,0:T(2,128)(2,1)S(1)}, u32[]{:S(2)}, u32[]{:S(2)}) collective-permute-start(bf16[1,256]{1,0:T(2,128)(2,1)S(1)} %get-tuple-element.74), channel_id=1, source_target_pairs={{17,2},{19,4},{21,6},{23,8},{25,10},{27,12},{29,14},{18,1},{20,3},... | collective-permute-start | bytes 1544 | tf_op jit(solution)/shard_map/ppermute | solution.py:451
  60.8 18.8 %collective-permute-start.11 = (bf16[128,256]{1,0:T(8,128)(2,1)S(1)}, bf16[128,256]{1,0:T(8,128)(2,1)S(1)}, u32[]{:S(2)}, u32[]{:S(2)}) collective-permute-start(bf16[128,256]{1,0:T(8,128)(2,1)S(1)} %bitcast.45), channel_id=1, source_target_pairs={{1,2},{3,4},{5,6},{7,8},{9,10},{11,12},{13,14},{2,1},{4,3},{6,5},{... | collective-permute-start | bytes 196616 | tf_op jit(solution)/shard_map/ppermute | solution.py:446
  63.4 16.3 %collective-permute-start.9 = (bf16[33,256]{1,0:T(8,128)(2,1)S(1)}, bf16[33,256]{1,0:T(8,128)(2,1)S(1)}, u32[]{:S(2)}, u32[]{:S(2)}) collective-permute-start(bf16[33,256]{1,0:T(8,128)(2,1)S(1)} %pad_maximum_fusion.5), channel_id=1, source_target_pairs={{16,0},{32,16},{48,32},{64,48},{80,64},{96,80},{112,96},{17,1},{33... | collective-permute-start | bytes 50696 | tf_op jit(solution)/shard_map/ppermute | solution.py:408
  64.8 15.0 %collective-permute-start.8 = (bf16[33,256]{1,0:T(8,128)(2,1)S(1)}, bf16[33,256]{1,0:T(8,128)(2,1)S(1)}, u32[]{:S(2)}, u32[]{:S(2)}) collective-permute-start(bf16[33,256]{1,0:T(8,128)(2,1)S(1)} %pad_maximum_fusion.4), channel_id=1, source_target_pairs={{0,16},{16,32},{32,48},{48,64},{64,80},{80,96},{96,112},{1,17},{17... | collective-permute-start | bytes 50696 | tf_op jit(solution)/shard_map/ppermute | solution.py:408
  85.3 37.5 %all-to-all-start.2 = ((bf16[64,128,128]{2,1,0:T(8,128)(2,1)}), bf16[64,128,128]{2,1,0:T(8,128)(2,1)}, u32[]{:S(2)}, u32[]{:S(2)}) async-start(bf16[64,128,128]{2,1,0:T(8,128)(2,1)} %chip_sum.1), calls=%async_computation.2 | async-start | bytes 4194304 | tf_op jit(solution)/shard_map/all_to_all | solution.py:484
  95.5 0.8 copy-start.3
  122.8 6.1 %collective-permute-start.13 = (bf16[8192,128]{1,0:T(8,128)(2,1)}, bf16[8192,128]{1,0:T(8,128)(2,1)S(1)}, u32[]{:S(2)}, u32[]{:S(2)}) collective-permute-start(bf16[8192,128]{1,0:T(8,128)(2,1)} %bitcast.22.half), channel_id=1, source_target_pairs={{0,1},{1,0},{2,3},{3,2},{4,5},{5,4},{6,7},{7,6},{8,9},{9,8},{10,11... | collective-permute-start | bytes 6291464 | tf_op jit(solution)/shard_map/ppermute | solution.py:487

commit v8 on v7

--- a/solution.py
+++ b/solution.py
@@ -322,21 +322,23 @@
 
 
 def reduce_kernel(parts, out, held, copies, sems):
-    n = PEERS // 8
-    loads = [pltpu.make_async_copy(parts.at[pl.ds(g * n, n)], held.at[g], sems.at[g]) for g in range(8)]
+    n, m = held.shape[2], copies.shape[1]
+    loads, stores = [], []
+    for q in range(4):
+        rows = pl.ds(q * n, n)
+        loads.append(pltpu.make_async_copy(parts.at[:, rows], held.at[q], sems.at[q]))
+        for g in range(PEERS // m):
+            place = out.at[pl.ds(g * m, m), rows]
+            stores.append(pltpu.make_async_copy(copies.at[q], place, sems.at[4 + len(stores)]))
     for load in loads:
         load.start()
-    total = None
-    for g in range(8):
-        loads[g].wait()
-        part = jnp.sum(held[g].astype(F32), axis=0)
-        total = part if total is None else total + part
-    done = (total * SCALE).astype(BF)
-    for p in range(n):
-        copies[p] = done
-    stores = [pltpu.make_async_copy(copies, out.at[pl.ds(g * n, n)], sems.at[8 + g]) for g in range(8)]
-    for store in stores:
-        store.start()
+    for q in range(4):
+        loads[q].wait()
+        done = (jnp.sum(held[q].astype(F32), axis=0) * SCALE).astype(BF)
+        for p in range(m):
+            copies[q, p] = done
+        for store in stores[q * (PEERS // m) : (q + 1) * (PEERS // m)]:
+            store.start()
     for store in stores:
         store.wait()
 
@@ -350,9 +352,9 @@
         out_specs=hbm,
         out_shape=jax.ShapeDtypeStruct((PEERS, n, 128), BF),
         scratch_shapes=[
-            pltpu.VMEM((8, PEERS // 8, n, 128), BF),
-            pltpu.VMEM((PEERS // 8, n, 128), BF),
-            pltpu.SemaphoreType.DMA((16,)),
+            pltpu.VMEM((4, PEERS, n // 4, 128), BF),
+            pltpu.VMEM((4, 16, n // 4, 128), BF),
+            pltpu.SemaphoreType.DMA((20,)),
         ],
         compiler_params=params(56, 0),
         name="chip_sum",
@@ -360,36 +362,31 @@
 
 
 def place_kernel(core, half, *refs):
-    conv, band, point, proj = refs[-4:]
-
-    def place(out, n, start, cols):
-        out[:, cols : cols + 128] = half[start : start + n, :].astype(F32)
-
-    for t in range(TAPS):
-        for n in range(2):
-            place(conv.at[t], 128, (2 * t + n) * 128, 128 * n)
-    for k in range(5):
-        for n in range(4):
-            place(band.at[k] if k < BANDS else point, 256, LATE + (4 * k + n) * 256, 128 * n)
-    for n in range(2):
-        place(proj, 256, LATE + (20 + n) * 256, 128 * n)
+    conv, band, point, proj, conv_s, band_s, point_s, proj_s, sems = refs[-9:]
+    large = pl.ds(pl.multiple_of(core[0] * 256, 256), 256)
+    small = pl.ds(pl.multiple_of(core[0] * 128, 128), 128)
+    groups = [(LATE + 1024 * k, 256, [band_s.at[k]], band_s.at[k], band.at[k, large]) for k in range(BANDS)]
+    groups.append((LATE + 4096, 256, [point_s], point_s, point.at[large]))
+    groups.append((LATE + 5120, 256, [proj_s], proj_s, proj.at[large]))
+    groups.append((0, 128, [conv_s.at[t] for t in range(TAPS)], conv_s, conv.at[:, small]))
+    stores = []
+    for g, (start, n, tiles, held, out) in enumerate(groups):
+        for tile in tiles:
+            for col in range(0, tile.shape[1], 128):
+                tile[:, col : col + 128] = half[start : start + n, :].astype(F32)
+                start += n
+        stores.append(pltpu.make_async_copy(held, out, sems.at[g]))
+        stores[g].start()
+    for store in stores:
+        store.wait()
 
 
 def place_half(core, half, before=()):
-    any_ref = pl.BlockSpec(memory_space=pl.ANY)
+    hbm, vm = pl.BlockSpec(memory_space=pltpu.HBM), pl.BlockSpec(memory_space=pltpu.VMEM)
     return pl.pallas_call(
         place_kernel,
-        grid_spec=pltpu.PrefetchScalarGridSpec(
-            num_scalar_prefetch=1,
-            grid=(1,),
-            in_specs=[pl.BlockSpec((PACK, 128), lambda i, c: (0, 0))] + [any_ref] * len(before),
-            out_specs=[
-                pl.BlockSpec((TAPS, 128, CF), lambda i, c: (0, c[0], 0)),
-                pl.BlockSpec((BANDS, 256, C), lambda i, c: (0, c[0], 0)),
-                pl.BlockSpec((256, C), lambda i, c: (c[0], 0)),
-                pl.BlockSpec((256, CF), lambda i, c: (c[0], 0)),
-            ],
-        ),
+        in_specs=[pl.BlockSpec(memory_space=pltpu.SMEM), vm] + [hbm] * len(before),
+        out_specs=[hbm] * 4,
         out_shape=[
             jax.ShapeDtypeStruct((TAPS, CF, CF), F32),
             jax.ShapeDtypeStruct((BANDS, C, C), F32),
@@ -397,7 +394,14 @@
             jax.ShapeDtypeStruct((C, CF), F32),
         ],
         input_output_aliases={2 + n: n for n in range(len(before))},
-        compiler_params=params(16),
+        scratch_shapes=[
+            pltpu.VMEM((TAPS, 128, CF), F32),
+            pltpu.VMEM((BANDS, 256, C), F32),
+            pltpu.VMEM((256, C), F32),
+            pltpu.VMEM((256, CF), F32),
+            pltpu.SemaphoreType.DMA((7,)),
+        ],
+        compiler_params=params(16, 0),
         cost_estimate=cost(0, 6_000_000),
         name="place_gradients",
     )(core, half, *before)

time: 132 us -> 132 us (level)
  transfers between devices with their start and end apart: 17 -> 17, of which waited for: 6 -> 7; matrix products, arithmetic and copies ran while one was open for 3% -> 3% of each run, Pallas kernels for 9% -> 9%
where the time goes in v8:
time: 132 us; the launch traced here: 131 us
  starting transfers between devices  54 us (41%)
  waiting for transfers between devices  38.5 us (29%)
  Pallas kernels  27.1 us (21%)
  local copies, waits for them, and re-layouts  7.39 us (6%)
  other arithmetic  2.6 us (2%)
    all_to_all x1, waiting for transfers between devices, local(): mine = lax.all_to_all(spread, CHIPS, 0, 0, tiled=True)  19.8 us
    pallas_call x1, Pallas kernels, forward_pass(): pl.pallas_call(forward_kernel, in_specs=[pl.BlockSpec(memory_space=pltpu....  10.9 us
    all_to_all x1, starting transfers between devices, local(): mine = lax.all_to_all(spread, CHIPS, 0, 0, tiled=True)  10.2 us
    ppermute x1, waiting for transfers between devices, whole_halo(): chip = lax.ppermute(outer, COL, chips)  9.49 us
    all_to_all x1, starting transfers between devices, local(): x = lax.all_to_all(chunks, ('xh', 'y'), 0, 0, tiled=True).reshape(CELLS, C)  7.62 us
    pallas_call x1, Pallas kernels, conv_pass(): pl.pallas_call(conv_kernel, grid=(NB,), in_specs=window_specs() + [whole(...  6.74 us
    ppermute x2, starting transfers between devices, shift(): return lax.ppermute(value, axes, pairs)  6.73 us
    all_to_all x1, starting transfers between devices, local(): parts = lax.all_to_all(packed, CHIPS, 0, 0, tiled=True)  6.36 us
  transfers between devices with their start and end apart: 17, of which 7 were waited for; matrix products, arithmetic and copies ran while one was open for 3% of the time, Pallas kernels for 9%

profile of v8, /device:TPU:1, one launch (start us, length us, event | category | flops | bytes accessed | tf_op | source)
XLA Modules:
  0.0 130.7 jit_solution(10605331017945096224)
XLA Ops:
  0.6 1.5 %fusion.1 = (bf16[128,1,256]{2,1,0:T(2,128)(2,1)S(1)}, bf16[128,1,256]{2,1,0:T(2,128)(2,1)S(1)}) fusion(bf16[128,32,256]{2,1,0:T(8,128)(2,1)} %oc_hbm.1), kind=kLoop, calls=%fused_computation.39 | loop fusion | bytes 262144 | tf_op jit(solution)/shard_map/slice | solution.py:469
  2.2 1.5 %collective-permute-start.1 = (bf16[128,256]{1,0:T(8,128)(2,1)S(1)}, bf16[128,256]{1,0:T(8,128)(2,1)S(1)}, u32[]{:S(2)}, u32[]{:S(2)}) collective-permute-start(bf16[128,256]{1,0:T(8,128)(2,1)S(1)} %get-tuple-element.65), channel_id=1, source_target_pairs={{0,1},{1,0},{2,3},{3,2},{4,5},{5,4},{6,7},{7,6},{8,9},{9,8},{10,11... | collective-permute-start | bytes 196616 | tf_op jit(solution)/shard_map/ppermute | solution.py:417
  3.7 3.2 %collective-permute-start = (bf16[128,256]{1,0:T(8,128)(2,1)S(1)}, bf16[128,256]{1,0:T(8,128)(2,1)S(1)}, u32[]{:S(2)}, u32[]{:S(2)}) collective-permute-start(bf16[128,256]{1,0:T(8,128)(2,1)S(1)} %get-tuple-element.66), channel_id=1, source_target_pairs={{1,2},{3,4},{5,6},{7,8},{9,10},{11,12},{13,14},{2,1},{4,3},{6,5},{... | collective-permute-start | bytes 196616 | tf_op jit(solution)/shard_map/ppermute | solution.py:420
  6.9 0.7 slice_bitcast_fusion.7
  7.6 1.7 %copy.26 = bf16[2,8,16,512]{3,2,0,1:T(8,128)(2,1)} copy(bf16[2,8,16,512]{3,2,1,0:T(8,128)(2,1)} %bitcast.44) | data formatting | bytes 524288 | tf_op jit(solution)/shard_map/reshape | solution.py:468
  9.4 0.7 collective-permute-start.2
  10.0 4.6 %collective-permute-start.3 = (bf16[34,256]{1,0:T(8,128)(2,1)S(1)}, bf16[34,256]{1,0:T(8,128)(2,1)S(1)}, u32[]{:S(2)}, u32[]{:S(2)}) collective-permute-start(bf16[34,256]{1,0:T(8,128)(2,1)S(1)} %get-tuple-element.84), channel_id=1, source_target_pairs={{0,16},{32,48},{64,80},{96,112},{16,0},{48,32},{80,64},{112,96},{1... | collective-permute-start | bytes 52232 | tf_op jit(solution)/shard_map/ppermute | solution.py:438
  14.7 0.1 pad.21.clone
  14.8 7.6 %all-to-all-start = ((bf16[8,2,16,512]{3,2,1,0:T(8,128)(2,1)}), bf16[8,2,16,512]{3,2,1,0:T(8,128)(2,1)S(1)}, u32[]{:S(2)}, u32[]{:S(2)}) async-start(bf16[8,2,16,512]{3,2,1,0:T(8,128)(2,1)} %bitcast.38), calls=%async_computation | async-start | bytes 524288 | tf_op jit(solution)/shard_map/all_to_all | solution.py:472
  22.4 0.0 collective-permute-done.3
  22.5 0.0 copy-start.4
  22.5 0.1 maximum_convert_fusion.1
  22.6 0.0 copy-start.2
  22.6 1.6 %copy-done.2 = bf16[128,32,256]{2,1,0:T(8,128)(2,1)S(1)} copy-done((bf16[128,32,256]{2,1,0:T(8,128)(2,1)S(1)}, bf16[128,32,256]{2,1,0:T(8,128)(2,1)}, u32[]{:S(2)}) %copy-start.2) | copy-done | bytes 2097176
  24.2 1.1 coarse_cotangent.1.dco
  25.4 4.6 %all-to-all-done = bf16[8,2,16,512]{3,2,1,0:T(8,128)(2,1)S(1)} async-done(((bf16[8,2,16,512]{3,2,1,0:T(8,128)(2,1)}), bf16[8,2,16,512]{3,2,1,0:T(8,128)(2,1)S(1)}, u32[]{:S(2)}, u32[]{:S(2)}) %all-to-all-start) | async-done | bytes 262176 | tf_op jit(solution)/shard_map/all_to_all | solution.py:472
  30.0 2.1 %collective-permute-start.4 = (bf16[256,512]{1,0:T(8,128)(2,1)S(1)}, bf16[256,512]{1,0:T(8,128)(2,1)S(1)}, u32[]{:S(2)}, u32[]{:S(2)}) collective-permute-start(bf16[256,512]{1,0:T(8,128)(2,1)S(1)} %bitcast.41), channel_id=1, source_target_pairs={{0,1},{1,0},{2,3},{3,2},{4,5},{5,4},{6,7},{7,6},{8,9},{9,8},{10,11... | collective-permute-start | bytes 786440 | tf_op jit(solution)/shard_map/ppermute | solution.py:475
  32.1 0.0 collective-permute-start.5
  32.1 1.3 %collective-permute-done.5.dtwin = bf16[256,256]{1,0:T(8,128)(2,1)S(1)} collective-permute-done((bf16[256,256]{1,0:T(8,128)(2,1)S(1)}, bf16[256,256]{1,0:T(8,128)(2,1)S(1)}, u32[]{:S(2)}, u32[]{:S(2)}) %collective-permute-start.5) | collective-permute-done | bytes 131104 | tf_op jit(solution)/shard_map/ppermute | solution.py:475
  33.4 0.9 copy-done.5
  34.4 10.9 %forward_and_gradients.1 = (bf16[8192,128]{1,0:T(8,128)(2,1)}, bf16[128,32,256]{2,1,0:T(8,128)(2,1)}, bf16[2,128,256]{2,1,0:T(8,128)(2,1)S(1)}, bf16[2560,128]{1,0:T(8,128)(2,1)S(1)}, bf16[2560,128]{1,0:T(8,128)(2,1)S(1)}) custom-call(s32[1]{0:T(128)} %bitcast.core, bf16[256,512]{1,0:T(8,128)(2,1)S(1)} %bitcast.42, ...), custom_call_target="tpu_custom_call" | custom-call | flops 8000000000 | bytes 14000000 | tf_op jit(solution)/shard_map/forward_and_gradients/pallas_call | solution.py:237
  45.3 0.4 collective-permute-start.6
  45.7 1.7 %collective-permute-done.6 = bf16[2560,128]{1,0:T(8,128)(2,1)S(1)} collective-permute-done((bf16[2560,128]{1,0:T(8,128)(2,1)S(1)}, bf16[2560,128]{1,0:T(8,128)(2,1)S(1)}, u32[]{:S(2)}, u32[]{:S(2)}) %collective-permute-start.6) | collective-permute-done | bytes 655392 | tf_op jit(solution)/shard_map/ppermute | solution.py:479
  47.4 1.0 fusion
  48.5 6.4 %all-to-all-start.1 = ((bf16[64,128,128]{2,1,0:T(8,128)(2,1)}), bf16[64,128,128]{2,1,0:T(8,128)(2,1)}, u32[]{:S(2)}, u32[]{:S(2)}) async-start(bf16[64,128,128]{2,1,0:T(8,128)(2,1)} %bitcast.43), calls=%async_computation.1 | async-start | bytes 4194304 | tf_op jit(solution)/shard_map/all_to_all | solution.py:484
  54.9 0.7 collective-permute-start.7
  55.6 3.9 %collective-permute-start.10 = (bf16[1,256]{1,0:T(2,128)(2,1)S(1)}, bf16[1,256]{1,0:T(2,128)(2,1)S(1)}, u32[]{:S(2)}, u32[]{:S(2)}) collective-permute-start(bf16[1,256]{1,0:T(2,128)(2,1)S(1)} %get-tuple-element.73), channel_id=1, source_target_pairs={{1,18},{3,20},{5,22},{7,24},{9,26},{11,28},{13,30},{2,17},{4,19},{... | collective-permute-start | bytes 1544 | tf_op jit(solution)/shard_map/ppermute | solution.py:455
  59.5 1.3 collective-permute-start.12
  60.8 2.6 %collective-permute-start.11 = (bf16[128,256]{1,0:T(8,128)(2,1)S(1)}, bf16[128,256]{1,0:T(8,128)(2,1)S(1)}, u32[]{:S(2)}, u32[]{:S(2)}) collective-permute-start(bf16[128,256]{1,0:T(8,128)(2,1)S(1)} %bitcast.45), channel_id=1, source_target_pairs={{1,2},{3,4},{5,6},{7,8},{9,10},{11,12},{13,14},{2,1},{4,3},{6,5},{... | collective-permute-start | bytes 196616 | tf_op jit(solution)/shard_map/ppermute | solution.py:450
  63.4 1.3 collective-permute-start.9
  64.8 5.4 %collective-permute-start.8 = (bf16[33,256]{1,0:T(8,128)(2,1)S(1)}, bf16[33,256]{1,0:T(8,128)(2,1)S(1)}, u32[]{:S(2)}, u32[]{:S(2)}) collective-permute-start(bf16[33,256]{1,0:T(8,128)(2,1)S(1)} %pad_maximum_fusion.4), channel_id=1, source_target_pairs={{0,16},{16,32},{32,48},{48,64},{64,80},{80,96},{96,112},{1,17},{17... | collective-permute-start | bytes 50696 | tf_op jit(solution)/shard_map/ppermute | solution.py:412
  70.2 9.5 %collective-permute-done.11 = bf16[128,256]{1,0:T(8,128)(2,1)S(1)} collective-permute-done((bf16[128,256]{1,0:T(8,128)(2,1)S(1)}, bf16[128,256]{1,0:T(8,128)(2,1)S(1)}, u32[]{:S(2)}, u32[]{:S(2)}) %collective-permute-start.11) | collective-permute-done | bytes 65568 | tf_op jit(solution)/shard_map/ppermute | solution.py:450
  79.7 0.0 collective-permute-done.9
  79.7 0.0 collective-permute-done.12
  79.8 0.6 pad_maximum_fusion.1.rows
  80.4 0.0 collective-permute-done.10
  80.4 0.7 maximum_convert_fusion.3
  81.2 1.1 all-to-all-done.1.parts
  82.3 2.6 %chip_sum.1 = bf16[64,128,128]{2,1,0:T(8,128)(2,1)} custom-call(bf16[64,128,128]{2,1,0:T(8,128)(2,1)} %all-to-all-done.1.parts), custom_call_target="tpu_custom_call" | custom-call | tf_op jit(solution)/shard_map/chip_sum/pallas_call | solution.py:349
  84.9 10.2 %all-to-all-start.2 = ((bf16[64,128,128]{2,1,0:T(8,128)(2,1)}), bf16[64,128,128]{2,1,0:T(8,128)(2,1)}, u32[]{:S(2)}, u32[]{:S(2)}) async-start(bf16[64,128,128]{2,1,0:T(8,128)(2,1)} %chip_sum.1), calls=%async_computation.2 | async-start | bytes 4194304 | tf_op jit(solution)/shard_map/all_to_all | solution.py:488
  95.1 0.0 copy-start.3
  95.1 0.7 copy-done.3
  95.9 6.7 %conv_forward.1 = bf16[128,32,256]{2,1,0:T(8,128)(2,1)} custom-call(bf16[128,32,256]{2,1,0:T(8,128)(2,1)S(1)} %copy-done, bf16[128,32,256]{2,1,0:T(8,128)(2,1)S(1)} %copy-done, bf16[128,32,256]{2,1,0:T(8,128)(2,1)S(1)} %copy-done, bf16[2,32,256]{2,1,0:T(8,128)(2,1)S(1)} %copy-done.3, f32[136,256]{1,0:T(8,128)S(1)} %get-tuple-element.47.left, ...), custom_call_target="tpu_custom_call" | custom-call | flops 1000000 | bytes 1000000 | tf_op jit(solution)/shard_map/conv_forward/pallas_call | solution.py:311
  102.6 19.8 %all-to-all-done.2 = bf16[64,128,128]{2,1,0:T(8,128)(2,1)} async-done(((bf16[64,128,128]{2,1,0:T(8,128)(2,1)}), bf16[64,128,128]{2,1,0:T(8,128)(2,1)}, u32[]{:S(2)}, u32[]{:S(2)}) %all-to-all-start.2) | async-done | bytes 2097184 | tf_op jit(solution)/shard_map/all_to_all | solution.py:488
  122.4 2.1 %collective-permute-start.13 = (bf16[8192,128]{1,0:T(8,128)(2,1)}, bf16[8192,128]{1,0:T(8,128)(2,1)S(1)}, u32[]{:S(2)}, u32[]{:S(2)}) collective-permute-start(bf16[8192,128]{1,0:T(8,128)(2,1)} %bitcast.22.half), channel_id=1, source_target_pairs={{0,1},{1,0},{2,3},{3,2},{4,5},{5,4},{6,7},{7,6},{8,9},{9,8},{10,11... | collective-permute-start | bytes 6291464 | tf_op jit(solution)/shard_map/ppermute | solution.py:491
  124.5 3.7 %place_gradients.2 = (f32[9,256,256]{2,1,0:T(8,128)}, f32[4,512,512]{2,1,0:T(8,128)}, f32[512,512]{1,0:T(8,128)}, f32[512,256]{1,0:T(8,128)}) custom-call(s32[1]{0:T(128)} %bitcast.core, bf16[8192,128]{1,0:T(8,128)(2,1)} %bitcast.22.half), custom_call_target="tpu_custom_call" | custom-call | bytes 6000000 | tf_op jit(solution)/shard_map/place_gradients/pallas_call | solution.py:386
  128.2 0.3 collective-permute-done.13.half
  128.5 2.1 %place_gradients.3 = (f32[9,256,256]{2,1,0:T(8,128)}, f32[4,512,512]{2,1,0:T(8,128)}, f32[512,512]{1,0:T(8,128)}, f32[512,256]{1,0:T(8,128)}) custom-call(s32[1]{0:T(128)S(6)} %sub.3.core, bf16[8192,128]{1,0:T(8,128)(2,1)S(1)} %collective-permute-done.13.half, ...), custom_call_target="tpu_custom_call", output_to_operand_aliasing={{0}: (2, {}), {1}: (3, {}), {2}: (4, {}), {3}: (5, {})} | custom-call | bytes 6000000 | tf_op jit(solution)/shard_map/place_gradients/pallas_call | solution.py:386
  (36 shorter events, 0.2 us)
Async XLA Ops:
  0.6 22.0 %copy-start.1 = (bf16[9,256,256]{2,1,0:T(8,128)(2,1)S(1)}, bf16[9,256,256]{2,1,0:T(8,128)(2,1)}, u32[]{:S(2)}) copy-start(bf16[9,256,256]{2,1,0:T(8,128)(2,1)} %wconv.1) | copy-start | bytes 3538948
  2.2 7.1 %collective-permute-start.1 = (bf16[128,256]{1,0:T(8,128)(2,1)S(1)}, bf16[128,256]{1,0:T(8,128)(2,1)S(1)}, u32[]{:S(2)}, u32[]{:S(2)}) collective-permute-start(bf16[128,256]{1,0:T(8,128)(2,1)S(1)} %get-tuple-element.65), channel_id=1, source_target_pairs={{0,1},{1,0},{2,3},{3,2},{4,5},{5,4},{6,7},{7,6},{8,9},{9,8},{10,11... | collective-permute-start | bytes 196616 | tf_op jit(solution)/shard_map/ppermute | solution.py:417
  3.7 5.6 %collective-permute-start = (bf16[128,256]{1,0:T(8,128)(2,1)S(1)}, bf16[128,256]{1,0:T(8,128)(2,1)S(1)}, u32[]{:S(2)}, u32[]{:S(2)}) collective-permute-start(bf16[128,256]{1,0:T(8,128)(2,1)S(1)} %get-tuple-element.66), channel_id=1, source_target_pairs={{1,2},{3,4},{5,6},{7,8},{9,10},{11,12},{13,14},{2,1},{4,3},{6,5},{... | collective-permute-start | bytes 196616 | tf_op jit(solution)/shard_map/ppermute | solution.py:420
  9.4 13.0 %collective-permute-start.2 = (bf16[34,256]{1,0:T(8,128)(2,1)S(1)}, bf16[34,256]{1,0:T(8,128)(2,1)S(1)}, u32[]{:S(2)}, u32[]{:S(2)}) collective-permute-start(bf16[34,256]{1,0:T(8,128)(2,1)S(1)} %get-tuple-element.83), channel_id=1, source_target_pairs={{16,32},{48,64},{80,96},{32,16},{64,48},{96,80},{17,33},{49,65},{8... | collective-permute-start | bytes 52232 | tf_op jit(solution)/shard_map/ppermute | solution.py:436
  10.0 12.4 %collective-permute-start.3 = (bf16[34,256]{1,0:T(8,128)(2,1)S(1)}, bf16[34,256]{1,0:T(8,128)(2,1)S(1)}, u32[]{:S(2)}, u32[]{:S(2)}) collective-permute-start(bf16[34,256]{1,0:T(8,128)(2,1)S(1)} %get-tuple-element.84), channel_id=1, source_target_pairs={{0,16},{32,48},{64,80},{96,112},{16,0},{48,32},{80,64},{112,96},{1... | collective-permute-start | bytes 52232 | tf_op jit(solution)/shard_map/ppermute | solution.py:438
  14.8 10.6 %copy-start.6 = (bf16[136]{0:T(256)(128)(2,1)}, bf16[136]{0:T(256)(128)(2,1)S(1)}, u32[]{:S(2)}) copy-start(bf16[136]{0:T(256)(128)(2,1)S(1)} %pad.21.clone) | copy-start | bytes 820
  14.8 15.2 %all-to-all-start = ((bf16[8,2,16,512]{3,2,1,0:T(8,128)(2,1)}), bf16[8,2,16,512]{3,2,1,0:T(8,128)(2,1)S(1)}, u32[]{:S(2)}, u32[]{:S(2)}) async-start(bf16[8,2,16,512]{3,2,1,0:T(8,128)(2,1)} %bitcast.38), calls=%async_computation | async-start | bytes 524288 | tf_op jit(solution)/shard_map/all_to_all | solution.py:472
  22.5 11.0 %copy-start.4 = (bf16[512,512]{1,0:T(8,128)(2,1)S(1)}, bf16[512,512]{1,0:T(8,128)(2,1)}, u32[]{:S(2)}) copy-start(bf16[512,512]{1,0:T(8,128)(2,1)} %wp_hbm.1) | copy-start | bytes 1572868
  22.6 1.6 %copy-start.2 = (bf16[128,32,256]{2,1,0:T(8,128)(2,1)S(1)}, bf16[128,32,256]{2,1,0:T(8,128)(2,1)}, u32[]{:S(2)}) copy-start(bf16[128,32,256]{2,1,0:T(8,128)(2,1)} %oc_hbm.1) | copy-start | bytes 6291460
  30.0 3.4 %collective-permute-start.4 = (bf16[256,512]{1,0:T(8,128)(2,1)S(1)}, bf16[256,512]{1,0:T(8,128)(2,1)S(1)}, u32[]{:S(2)}, u32[]{:S(2)}) collective-permute-start(bf16[256,512]{1,0:T(8,128)(2,1)S(1)} %bitcast.41), channel_id=1, source_target_pairs={{0,1},{1,0},{2,3},{3,2},{4,5},{5,4},{6,7},{7,6},{8,9},{9,8},{10,11... | collective-permute-start | bytes 786440 | tf_op jit(solution)/shard_map/ppermute | solution.py:475
  32.1 1.3 %collective-permute-start.5 = (bf16[256,256]{1,0:T(8,128)(2,1)S(1)}, bf16[256,256]{1,0:T(8,128)(2,1)S(1)}, u32[]{:S(2)}, u32[]{:S(2)}) collective-permute-start(bf16[256,256]{1,0:T(8,128)(2,1)S(1)} %coarse_cotangent.1.dco), channel_id=1, source_target_pairs={{0,1},{1,0},{2,3},{3,2},{4,5},{5,4},{6,7},{7,6},{8,9},{9,8},{10,11... | collective-permute-start | bytes 393224 | tf_op jit(solution)/shard_map/ppermute | solution.py:475
  33.4 1.0 copy-start.5
  45.3 2.2 %collective-permute-start.6 = (bf16[2560,128]{1,0:T(8,128)(2,1)S(1)}, bf16[2560,128]{1,0:T(8,128)(2,1)S(1)}, u32[]{:S(2)}, u32[]{:S(2)}) collective-permute-start(bf16[2560,128]{1,0:T(8,128)(2,1)S(1)} %get-tuple-element.39), channel_id=1, source_target_pairs={{0,1},{1,0},{2,3},{3,2},{4,5},{5,4},{6,7},{7,6},{8,9},{9,8},{10,11... | collective-permute-start | bytes 1966088 | tf_op jit(solution)/shard_map/ppermute | solution.py:479
  48.5 6.4 %copy-start = (bf16[128,32,256]{2,1,0:T(8,128)(2,1)S(1)}, bf16[128,32,256]{2,1,0:T(8,128)(2,1)}, u32[]{:S(2)}) copy-start(bf16[128,32,256]{2,1,0:T(8,128)(2,1)} %get-tuple-element.43.before.ci.after) | copy-start | bytes 6291460
  48.5 33.8 %all-to-all-start.1 = ((bf16[64,128,128]{2,1,0:T(8,128)(2,1)}), bf16[64,128,128]{2,1,0:T(8,128)(2,1)}, u32[]{:S(2)}, u32[]{:S(2)}) async-start(bf16[64,128,128]{2,1,0:T(8,128)(2,1)} %bitcast.43), calls=%async_computation.1 | async-start | bytes 4194304 | tf_op jit(solution)/shard_map/all_to_all | solution.py:484
  54.9 8.5 %collective-permute-start.7 = (bf16[128,256]{1,0:T(8,128)(2,1)S(1)}, bf16[128,256]{1,0:T(8,128)(2,1)S(1)}, u32[]{:S(2)}, u32[]{:S(2)}) collective-permute-start(bf16[128,256]{1,0:T(8,128)(2,1)S(1)} %get-tuple-element.70), channel_id=1, source_target_pairs={{0,1},{1,0},{2,3},{3,2},{4,5},{5,4},{6,7},{7,6},{8,9},{9,8},{10,11... | collective-permute-start | bytes 196616 | tf_op jit(solution)/shard_map/ppermute | solution.py:447
  55.6 24.8 %collective-permute-start.10 = (bf16[1,256]{1,0:T(2,128)(2,1)S(1)}, bf16[1,256]{1,0:T(2,128)(2,1)S(1)}, u32[]{:S(2)}, u32[]{:S(2)}) collective-permute-start(bf16[1,256]{1,0:T(2,128)(2,1)S(1)} %get-tuple-element.73), channel_id=1, source_target_pairs={{1,18},{3,20},{5,22},{7,24},{9,26},{11,28},{13,30},{2,17},{4,19},{... | collective-permute-start | bytes 1544 | tf_op jit(solution)/shard_map/ppermute | solution.py:455
  59.5 20.2 %collective-permute-start.12 = (bf16[1,256]{1,0:T(2,128)(2,1)S(1)}, bf16[1,256]{1,0:T(2,128)(2,1)S(1)}, u32[]{:S(2)}, u32[]{:S(2)}) collective-permute-start(bf16[1,256]{1,0:T(2,128)(2,1)S(1)} %get-tuple-element.74), channel_id=1, source_target_pairs={{17,2},{19,4},{21,6},{23,8},{25,10},{27,12},{29,14},{18,1},{20,3},... | collective-permute-start | bytes 1544 | tf_op jit(solution)/shard_map/ppermute | solution.py:455
  60.8 18.8 %collective-permute-start.11 = (bf16[128,256]{1,0:T(8,128)(2,1)S(1)}, bf16[128,256]{1,0:T(8,128)(2,1)S(1)}, u32[]{:S(2)}, u32[]{:S(2)}) collective-permute-start(bf16[128,256]{1,0:T(8,128)(2,1)S(1)} %bitcast.45), channel_id=1, source_target_pairs={{1,2},{3,4},{5,6},{7,8},{9,10},{11,12},{13,14},{2,1},{4,3},{6,5},{... | collective-permute-start | bytes 196616 | tf_op jit(solution)/shard_map/ppermute | solution.py:450
  63.4 16.3 %collective-permute-start.9 = (bf16[33,256]{1,0:T(8,128)(2,1)S(1)}, bf16[33,256]{1,0:T(8,128)(2,1)S(1)}, u32[]{:S(2)}, u32[]{:S(2)}) collective-permute-start(bf16[33,256]{1,0:T(8,128)(2,1)S(1)} %pad_maximum_fusion.5), channel_id=1, source_target_pairs={{16,0},{32,16},{48,32},{64,48},{80,64},{96,80},{112,96},{17,1},{33... | collective-permute-start | bytes 50696 | tf_op jit(solution)/shard_map/ppermute | solution.py:412
  64.8 15.0 %collective-permute-start.8 = (bf16[33,256]{1,0:T(8,128)(2,1)S(1)}, bf16[33,256]{1,0:T(8,128)(2,1)S(1)}, u32[]{:S(2)}, u32[]{:S(2)}) collective-permute-start(bf16[33,256]{1,0:T(8,128)(2,1)S(1)} %pad_maximum_fusion.4), channel_id=1, source_target_pairs={{0,16},{16,32},{32,48},{48,64},{64,80},{80,96},{96,112},{1,17},{17... | collective-permute-start | bytes 50696 | tf_op jit(solution)/shard_map/ppermute | solution.py:412
  84.9 37.5 %all-to-all-start.2 = ((bf16[64,128,128]{2,1,0:T(8,128)(2,1)}), bf16[64,128,128]{2,1,0:T(8,128)(2,1)}, u32[]{:S(2)}, u32[]{:S(2)}) async-start(bf16[64,128,128]{2,1,0:T(8,128)(2,1)} %chip_sum.1), calls=%async_computation.2 | async-start | bytes 4194304 | tf_op jit(solution)/shard_map/all_to_all | solution.py:488
  95.1 0.8 copy-start.3
  122.4 6.1 %collective-permute-start.13 = (bf16[8192,128]{1,0:T(8,128)(2,1)}, bf16[8192,128]{1,0:T(8,128)(2,1)S(1)}, u32[]{:S(2)}, u32[]{:S(2)}) collective-permute-start(bf16[8192,128]{1,0:T(8,128)(2,1)} %bitcast.22.half), channel_id=1, source_target_pairs={{0,1},{1,0},{2,3},{3,2},{4,5},{5,4},{6,7},{7,6},{8,9},{9,8},{10,11... | collective-permute-start | bytes 6291464 | tf_op jit(solution)/shard_map/ppermute | solution.py:491
